TPU v7x, 32 devices: a whole 2x2x4 slice. The times are simulated.
32 devices in a mesh: exp: 8 (over z, x), tp: 4 (over y, core).
Axes of the slice: x: 2, y: 2, z: 4, core: 2. Of those that a mesh axis runs over, the one named last changes fastest.
Arguments:
- tokens: bfloat16 [4096, 2048], P('exp'), may hold values from -6 to 6
- cotangent: bfloat16 [4096, 2048], P('exp'), may hold values from -6 to 6
- lengths: int32 [1], replicated, may hold values from 1024 to 4096, as said below
- routes: int32 [4096, 4], P('exp'), may hold values from 0 to 15, all different within a row; in each aligned block of 512 rows (0 to 511, 512 to 1023, ...) at most 256 rows name the same one
- w_query: bfloat16 [2048, 2048], P('exp', 'tp'), may hold values from -0.125 to 0.125
- w_key: bfloat16 [2048, 2048], P('exp', 'tp'), may hold values from -0.125 to 0.125
- w_value: bfloat16 [2048, 2048], P('exp', 'tp'), may hold values from -0.125 to 0.125
- w_out: bfloat16 [2048, 2048], P('tp', 'exp'), may hold values from -0.75 to 0.75
- b_query: bfloat16 [2048], P(('tp', 'exp')), may hold values from -3 to 3
- b_key: bfloat16 [2048], P(('tp', 'exp')), may hold values from -3 to 3
- b_value: bfloat16 [2048], P(('tp', 'exp')), may hold values from -3 to 3
- gain_attention: bfloat16 [2048], P('exp'), may hold values from 0.5 to 1.5
- gain_experts: bfloat16 [2048], P('exp'), may hold values from 0.5 to 1.5
- w_router: bfloat16 [2048, 16], P('exp'), may hold values from -0.0625 to 0.0625
- w_shared_gate: bfloat16 [2048], P('exp'), may hold values from -0.125 to 0.125
- shared_gate: bfloat16 [2048, 5632], P('exp', 'tp'), may hold values from -0.125 to 0.125
- shared_up: bfloat16 [2048, 5632], P('exp', 'tp'), may hold values from -0.125 to 0.125
- shared_down: bfloat16 [5632, 2048], P('tp', 'exp'), may hold values from -0.15625 to 0.15625
- expert_gate: bfloat16 [16, 2048, 1408], P('exp', None, 'tp'), may hold values from -0.125 to 0.125
- expert_up: bfloat16 [16, 2048, 1408], P('exp', None, 'tp'), may hold values from -0.125 to 0.125
- expert_down: bfloat16 [16, 1408, 2048], P('exp', 'tp'), may hold values from -0.625 to 0.625
Outputs:
- mixed: bfloat16 [4096, 2048], P('exp')
- grad_tokens: bfloat16 [4096, 2048], P('exp')
- grad_w_query: float32 [2048, 2048], P('exp', 'tp')
- grad_w_key: float32 [2048, 2048], P('exp', 'tp')
- grad_w_value: float32 [2048, 2048], P('exp', 'tp')
- grad_w_out: float32 [2048, 2048], P('tp', 'exp')
- grad_b_query: float32 [2048], P(('tp', 'exp'))
- grad_b_key: float32 [2048], P(('tp', 'exp'))
- grad_b_value: float32 [2048], P(('tp', 'exp'))
- grad_gain_attention: float32 [2048], P('exp')
- grad_gain_experts: float32 [2048], P('exp')
- grad_w_router: float32 [2048, 16], P('exp')
- grad_w_shared_gate: float32 [2048], P('exp')
- grad_shared_gate: float32 [2048, 5632], P('exp', 'tp')
- grad_shared_up: float32 [2048, 5632], P('exp', 'tp')
- grad_shared_down: float32 [5632, 2048], P('tp', 'exp')
- grad_expert_gate: float32 [16, 2048, 1408], P('exp', None, 'tp')
- grad_expert_up: float32 [16, 2048, 1408], P('exp', None, 'tp')
- grad_expert_down: float32 [16, 1408, 2048], P('exp', 'tp')
- rms_output: float32 [], replicated
- rms_grad: float32 [], replicated
Inputs may be any that keep to these rules, and one draw needn't show every extreme that they name: `lengths`: every sequence's length; one sequence, drawn from the seed, fills all 4096 slots. `routes`: within the 512 rows of one index of exp no expert is named by more than 256 rows, a bound that some block reaches.
All inputs are finite; a program needn't handle non-finite values.
Results may differ from a plain program's by a relative error of at most 0.034.
Values may be sent and summed in bfloat16 or wider, within the bound.
A program may use at most 384 MiB of HBM per device.

v0:
```python
import jax
import jax.numpy as jnp
from jax import lax
from jax.sharding import PartitionSpec as P

HEAD_DIM = 128
SLOT = 4096


EPSILON = 1e-06
ROPE_BASE = 1000000.0
MASKED = -1e30


def shifted(shard, axis, by):
    length = lax.axis_size(axis)
    pairs = [(i, i + by) for i in range(length) if 0 <= i + by < length]
    return lax.ppermute(shard, axis, pairs)


def rope_tables(positions, head_dim):
    half_dim = head_dim // 2
    frequency = ROPE_BASE ** (-(jnp.arange(half_dim, dtype=jnp.float32) * 2.0) / head_dim)
    angles = positions.astype(jnp.float32)[:, None] * frequency[None, :]
    cosine = jnp.concatenate([jnp.cos(angles), jnp.cos(angles)], axis=1)
    sine_table = jnp.concatenate([jnp.sin(angles), jnp.sin(angles)], axis=1)
    return (cosine, sine_table)


def rotate(values, cosine, sine_table):
    half_dim = values.shape[-1] // 2
    turned = jnp.concatenate([-values[..., half_dim:], values[..., :half_dim]], axis=-1)
    return values * cosine[:, None, :] + turned * sine_table[:, None, :]


def rotate_back(grads, cosine, sine_table):
    half_dim = grads.shape[-1] // 2
    moved = grads * sine_table[:, None, :]
    return grads * cosine[:, None, :] + jnp.concatenate(
        [moved[..., half_dim:], -moved[..., :half_dim]], axis=-1
    )


def product(left, right):
    return jnp.dot(left, right, preferred_element_type=jnp.float32)


def product_bt(left, right):
    return lax.dot_general(
        left, right, (((1,), (1,)), ((), ())), preferred_element_type=jnp.float32
    )


def product_at(left, right):
    return lax.dot_general(
        left, right, (((0,), (0,)), ((), ())), preferred_element_type=jnp.float32
    )


def norm_scale(values):
    return lax.rsqrt(jnp.mean(values * values, axis=1, keepdims=True) + EPSILON)


def norm_back(grad_normed, values, inverse, gain):
    scaled = values * inverse
    pushed = grad_normed * gain
    back_rows = inverse * (pushed - scaled * jnp.mean(pushed * scaled, axis=1, keepdims=True))
    return (back_rows, jnp.sum(grad_normed * scaled, axis=0))


def silu_grad(values):
    sigma = jax.nn.sigmoid(values)
    return sigma * (1.0 + values * (1.0 - sigma))


def local(
    tokens,
    cotangent,
    lengths,
    routes,
    w_query,
    w_key,
    w_value,
    w_out,
    b_query,
    b_key,
    b_value,
    gain_attention,
    gain_experts,
    w_router,
    w_shared_gate,
    shared_gate,
    shared_up,
    shared_down,
    expert_gate,
    expert_up,
    expert_down,
):
    exp_count = lax.axis_size("exp")
    exp_index = lax.axis_index("exp")
    tp_count = lax.axis_size("tp")
    tp_index = lax.axis_index("tp")
    row_count, model_width = tokens.shape
    local_experts = expert_gate.shape[0]
    expert_count = local_experts * exp_count
    top_count = routes.shape[1]
    capacity = 2 * row_count * top_count // expert_count
    quarter = capacity // tp_count
    head_dim = HEAD_DIM
    heads_here = w_query.shape[1] // head_dim
    group_size = SLOT // row_count
    scale = 1.0 / head_dim**0.5

    def own_slots(whole_rows):
        return lax.dynamic_slice_in_dim(whole_rows, tp_index * quarter, quarter, 2)

    def place_slots(part_rows):
        empty_rows = jnp.zeros((exp_count, local_experts, capacity, model_width), part_rows.dtype)
        return lax.dynamic_update_slice_in_dim(empty_rows, part_rows, tp_index * quarter, 2)

    gathered = (
        lax.all_gather(w_query, "exp", axis=0, tiled=True),
        lax.all_gather(w_key, "exp", axis=0, tiled=True),
        lax.all_gather(w_value, "exp", axis=0, tiled=True),
        lax.all_gather(w_out, "exp", axis=1, tiled=True),
        lax.all_gather(b_query, "exp", axis=0, tiled=True),
        lax.all_gather(b_key, "exp", axis=0, tiled=True),
        lax.all_gather(b_value, "exp", axis=0, tiled=True),
        lax.all_gather(gain_attention, "exp", axis=0, tiled=True),
        lax.all_gather(gain_experts, "exp", axis=0, tiled=True),
        lax.all_gather(w_router, "exp", axis=0, tiled=True),
        lax.all_gather(w_shared_gate, "exp", axis=0, tiled=True),
        lax.all_gather(shared_gate, "exp", axis=0, tiled=True),
        lax.all_gather(shared_up, "exp", axis=0, tiled=True),
        lax.all_gather(shared_down, "exp", axis=1, tiled=True),
    )
    (
        query_full,
        key_full,
        value_full,
        out_full,
        query_bias,
        key_bias,
        value_bias,
        attn_gain,
        ffn_gain,
        router_full,
        share_vector,
        share_gate_full,
        share_up_full,
        share_down_full,
    ) = gathered
    attn_gain = attn_gain.astype(jnp.float32)
    ffn_gain = ffn_gain.astype(jnp.float32)
    first_row = exp_index * row_count
    slot_index = first_row // SLOT
    offset = first_row % SLOT
    positions = offset + jnp.arange(row_count, dtype=jnp.int32)
    length = jnp.sum(
        jnp.where(jnp.arange(lengths.shape[0], dtype=jnp.int32) == slot_index, lengths, 0)
    )
    valid_rows = (positions < length).astype(jnp.float32)
    cosine, sine_table = rope_tables(positions, head_dim)
    input_rows = tokens.astype(jnp.float32)
    inverse_first = norm_scale(input_rows)
    normed_first = (input_rows * inverse_first * attn_gain).astype(jnp.bfloat16)
    query_lin = product(normed_first, query_full) + query_bias.astype(jnp.float32)
    key_lin = product(normed_first, key_full) + key_bias.astype(jnp.float32)
    value_lin = product(normed_first, value_full) + value_bias.astype(jnp.float32)
    query_rot = rotate(
        query_lin.reshape(row_count, heads_here, head_dim), cosine, sine_table
    ).astype(jnp.bfloat16)
    key_rot = rotate(key_lin.reshape(row_count, heads_here, head_dim), cosine, sine_table).astype(
        jnp.bfloat16
    )
    value_low = value_lin.reshape(row_count, heads_here, head_dim).astype(jnp.bfloat16)
    key_list = [key_rot]
    value_list = [value_low]
    for distance in range(1, group_size):
        earlier_keys, earlier_values = shifted((key_rot, value_low), "exp", distance)
        key_list.append(earlier_keys)
        value_list.append(earlier_values)
    all_keys = jnp.concatenate(key_list, axis=0)
    all_values = jnp.concatenate(value_list, axis=0)
    key_index = jnp.arange(group_size * row_count, dtype=jnp.int32)
    key_pos = offset - key_index // row_count * row_count + key_index % row_count
    allowed = (
        (key_pos[None, :] >= 0)
        & (key_pos[None, :] <= positions[:, None])
        & (key_pos[None, :] < length)
    )
    scores = (
        jnp.einsum("qhd,khd->hqk", query_rot, all_keys, preferred_element_type=jnp.float32) * scale
    )
    scores = jnp.where(allowed[None, :, :], scores, MASKED)
    peak_score = jnp.max(scores, axis=2, keepdims=True)
    weights = jnp.exp(scores - peak_score)
    total_weight = jnp.sum(weights, axis=2, keepdims=True)
    log_total = peak_score + jnp.log(total_weight)
    attn_probs = (weights / total_weight).astype(jnp.bfloat16)
    attended = jnp.einsum(
        "hqk,khd->qhd", attn_probs, all_values, preferred_element_type=jnp.float32
    )
    attended = attended.reshape(row_count, heads_here * head_dim).astype(jnp.bfloat16)
    attn_sum = lax.psum(product(attended, out_full).astype(jnp.bfloat16), "tp").astype(jnp.float32)
    hidden_state = input_rows + attn_sum
    inverse_second = norm_scale(hidden_state)
    normed = (hidden_state * inverse_second * ffn_gain).astype(jnp.bfloat16)
    logits = product(normed, router_full)
    router_probs = jax.nn.softmax(logits, axis=1)
    chosen = (
        routes[:, :, None] == jnp.arange(expert_count, dtype=jnp.int32)[None, None, :]
    ).astype(jnp.float32)
    gates = jnp.sum(chosen * router_probs[:, None, :], axis=2)
    share_weight = jax.nn.sigmoid(product(normed, share_vector))
    share_pre = product(normed, share_gate_full)
    share_lin = product(normed, share_up_full)
    share_hidden = (jax.nn.silu(share_pre) * share_lin).astype(jnp.bfloat16)
    share_out = product(share_hidden, share_down_full)
    flat_routes = routes.reshape(-1)
    pair_count = row_count * top_count
    pick_table = (
        flat_routes[:, None] == jnp.arange(expert_count, dtype=jnp.int32)[None, :]
    ).astype(jnp.int32)
    rank_in_expert = jnp.sum((jnp.cumsum(pick_table, axis=0) - 1) * pick_table, axis=1)
    target = flat_routes * capacity + rank_in_expert
    slot_pair = (
        jnp.full((expert_count * capacity,), pair_count, jnp.int32)
        .at[target]
        .set(jnp.arange(pair_count, dtype=jnp.int32))
    )
    slot_token = jnp.where(slot_pair < pair_count, slot_pair // top_count, row_count)
    padded_rows = jnp.concatenate([normed, jnp.zeros((1, model_width), jnp.bfloat16)], axis=0)
    outgoing = padded_rows[slot_token].reshape(exp_count, local_experts, capacity, model_width)
    sending = own_slots(outgoing)
    working = lax.all_gather(
        lax.all_to_all(sending, "exp", split_axis=0, concat_axis=0, tiled=True),
        "tp",
        axis=2,
        tiled=True,
    )
    gate_pre = jnp.einsum(
        "sxcd,xdf->sxcf", working, expert_gate, preferred_element_type=jnp.float32
    )
    up_pre = jnp.einsum("sxcd,xdf->sxcf", working, expert_up, preferred_element_type=jnp.float32)
    inner = (jax.nn.silu(gate_pre) * up_pre).astype(jnp.bfloat16)
    result_rows = jnp.einsum(
        "sxcf,xfd->sxcd", inner, expert_down, preferred_element_type=jnp.float32
    )
    result_rows = lax.psum_scatter(
        result_rows.astype(jnp.bfloat16), "tp", scatter_dimension=2, tiled=True
    ).astype(jnp.float32)
    back_rows = lax.all_to_all(
        result_rows.astype(jnp.bfloat16), "exp", split_axis=0, concat_axis=0, tiled=True
    ).astype(result_rows.dtype)
    returned = back_rows
    returned = place_slots(returned)
    expert_rows = returned.reshape(expert_count * capacity, model_width)[target].reshape(
        row_count, top_count, model_width
    )
    mixture = jnp.einsum("tk,tkd->td", gates, expert_rows) + share_weight[:, None] * share_out
    mixture = lax.psum(mixture.astype(jnp.bfloat16), "tp").astype(jnp.float32)
    output = valid_rows[:, None] * (hidden_state + mixture)
    grad_out = cotangent.astype(jnp.float32) * valid_rows[:, None]
    share_grad = (grad_out * share_weight[:, None]).astype(jnp.bfloat16)
    grad_share_hidden = (
        product_bt(share_grad, share_down_full).astype(jnp.bfloat16).astype(jnp.float32)
    )
    grad_share_pre = (grad_share_hidden * share_lin * silu_grad(share_pre)).astype(jnp.bfloat16)
    grad_share_lin = (grad_share_hidden * jax.nn.silu(share_pre)).astype(jnp.bfloat16)
    d_shared_down = product_at(share_hidden, share_grad)
    d_shared_gate = product_at(normed, grad_share_pre)
    d_shared_up = product_at(normed, grad_share_lin)
    back_normed = product_bt(grad_share_pre, share_gate_full) + product_bt(
        grad_share_lin, share_up_full
    )
    gate_part = jnp.einsum("td,tkd->tk", grad_out, expert_rows)
    share_part = jnp.sum(grad_out * share_out, axis=1)
    pair_grads = (
        (grad_out[:, None, :] * gates[:, :, None])
        .astype(jnp.bfloat16)
        .reshape(pair_count, model_width)
    )
    padded_grads = jnp.concatenate([pair_grads, jnp.zeros((1, model_width), jnp.bfloat16)], axis=0)
    outgoing_grads = padded_grads[slot_pair].reshape(
        exp_count, local_experts, capacity, model_width
    )
    sending_grads = own_slots(outgoing_grads)
    arrived_grads, arrived_rows = (
        lax.all_to_all(sending_grads, "exp", split_axis=0, concat_axis=0, tiled=True),
        lax.all_to_all(sending, "exp", split_axis=0, concat_axis=0, tiled=True),
    )
    arrived_grads, arrived_rows = (
        lax.all_gather(arrived_grads, "tp", axis=2, tiled=True),
        lax.all_gather(arrived_rows, "tp", axis=2, tiled=True),
    )
    gate_pre = jnp.einsum(
        "sxcd,xdf->sxcf", arrived_rows, expert_gate, preferred_element_type=jnp.float32
    )
    up_pre = jnp.einsum(
        "sxcd,xdf->sxcf", arrived_rows, expert_up, preferred_element_type=jnp.float32
    )
    inner = (jax.nn.silu(gate_pre) * up_pre).astype(jnp.bfloat16)
    grad_inner = jnp.einsum(
        "sxcd,xfd->sxcf", arrived_grads, expert_down, preferred_element_type=jnp.float32
    )
    grad_inner = grad_inner.astype(jnp.bfloat16).astype(jnp.float32)
    grad_gate_pre = (grad_inner * up_pre * silu_grad(gate_pre)).astype(jnp.bfloat16)
    grad_up_pre = (grad_inner * jax.nn.silu(gate_pre)).astype(jnp.bfloat16)
    rows_back = jnp.einsum(
        "sxcf,xdf->sxcd", grad_gate_pre, expert_gate, preferred_element_type=jnp.float32
    )
    rows_back = rows_back + jnp.einsum(
        "sxcf,xdf->sxcd", grad_up_pre, expert_up, preferred_element_type=jnp.float32
    )
    rows_back = lax.psum_scatter(
        rows_back.astype(jnp.bfloat16), "tp", scatter_dimension=2, tiled=True
    ).astype(jnp.float32)
    returned_grads = lax.all_to_all(
        rows_back.astype(jnp.bfloat16), "exp", split_axis=0, concat_axis=0, tiled=True
    ).astype(rows_back.dtype)
    returned_grads = place_slots(returned_grads)
    d_expert_gate = jnp.einsum(
        "sxcd,sxcf->xdf", arrived_rows, grad_gate_pre, preferred_element_type=jnp.float32
    )
    d_expert_up = jnp.einsum(
        "sxcd,sxcf->xdf", arrived_rows, grad_up_pre, preferred_element_type=jnp.float32
    )
    d_expert_down = jnp.einsum(
        "sxcf,sxcd->xfd", inner, arrived_grads, preferred_element_type=jnp.float32
    )
    grad_rows = returned_grads.reshape(expert_count * capacity, model_width)[target].reshape(
        row_count, top_count, model_width
    )
    back_normed = back_normed + jnp.sum(grad_rows, axis=1)
    scalar_part = jnp.concatenate([gate_part, share_part[:, None]], axis=1)
    summed_normed, scalar_sum = (
        lax.psum(back_normed.astype(jnp.bfloat16), "tp").astype(jnp.float32),
        lax.psum(scalar_part.astype(jnp.bfloat16), "tp").astype(jnp.float32),
    )
    grad_gates = scalar_sum[:, :top_count]
    grad_share_weight = scalar_sum[:, top_count]
    grad_router_probs = jnp.einsum("tk,tke->te", grad_gates, chosen)
    grad_logits = (
        router_probs
        * (grad_router_probs - jnp.sum(grad_router_probs * router_probs, axis=1, keepdims=True))
    ).astype(jnp.bfloat16)
    grad_share_logit = (grad_share_weight * share_weight * (1.0 - share_weight)).astype(
        jnp.bfloat16
    )
    d_router = product_at(normed, grad_logits)
    d_share_vector = product(grad_share_logit, normed)
    grad_normed = (
        summed_normed
        + product_bt(grad_logits, router_full)
        + grad_share_logit.astype(jnp.float32)[:, None] * share_vector.astype(jnp.float32)[None, :]
    )
    norm_rows, d_gain_experts = norm_back(grad_normed, hidden_state, inverse_second, ffn_gain)
    grad_hidden = grad_out + norm_rows
    grad_hidden_low = grad_hidden.astype(jnp.bfloat16)
    d_out_weight = product_at(attended, grad_hidden_low)
    grad_attended = (
        product_bt(grad_hidden_low, out_full)
        .astype(jnp.bfloat16)
        .reshape(row_count, heads_here, head_dim)
    )
    scores = (
        jnp.einsum("qhd,khd->hqk", query_rot, all_keys, preferred_element_type=jnp.float32) * scale
    )
    scores = jnp.where(allowed[None, :, :], scores, MASKED)
    probs_again = jnp.exp(scores - log_total)
    probs_low = probs_again.astype(jnp.bfloat16)
    grad_values = jnp.einsum(
        "hqk,qhd->khd", probs_low, grad_attended, preferred_element_type=jnp.float32
    )
    grad_probs = jnp.einsum(
        "qhd,khd->hqk", grad_attended, all_values, preferred_element_type=jnp.float32
    )
    grad_scores = (
        probs_again * (grad_probs - jnp.sum(probs_again * grad_probs, axis=2, keepdims=True))
    ).astype(jnp.bfloat16)
    grad_query = (
        jnp.einsum("hqk,khd->qhd", grad_scores, all_keys, preferred_element_type=jnp.float32)
        * scale
    )
    grad_keys = (
        jnp.einsum("hqk,qhd->khd", grad_scores, query_rot, preferred_element_type=jnp.float32)
        * scale
    )
    own_key_grads = grad_keys[:row_count]
    own_value_grads = grad_values[:row_count]
    for distance in range(1, group_size):
        lower_row = distance * row_count
        later_keys, later_values = (
            shifted(
                grad_keys[lower_row : lower_row + row_count].astype(jnp.bfloat16), "exp", -distance
            ).astype(jnp.float32),
            shifted(
                grad_values[lower_row : lower_row + row_count].astype(jnp.bfloat16),
                "exp",
                -distance,
            ).astype(jnp.float32),
        )
        own_key_grads = own_key_grads + later_keys
        own_value_grads = own_value_grads + later_values
    grad_query_lin = (
        rotate_back(grad_query, cosine, sine_table)
        .reshape(row_count, heads_here * head_dim)
        .astype(jnp.bfloat16)
    )
    grad_key_lin = (
        rotate_back(own_key_grads, cosine, sine_table)
        .reshape(row_count, heads_here * head_dim)
        .astype(jnp.bfloat16)
    )
    grad_value_lin = own_value_grads.reshape(row_count, heads_here * head_dim).astype(jnp.bfloat16)
    d_query = product_at(normed_first, grad_query_lin)
    d_key = product_at(normed_first, grad_key_lin)
    d_value = product_at(normed_first, grad_value_lin)
    d_query_bias = jnp.sum(grad_query_lin.astype(jnp.float32), axis=0)
    d_key_bias = jnp.sum(grad_key_lin.astype(jnp.float32), axis=0)
    d_value_bias = jnp.sum(grad_value_lin.astype(jnp.float32), axis=0)
    back_first = (
        product_bt(grad_query_lin, query_full)
        + product_bt(grad_key_lin, key_full)
        + product_bt(grad_value_lin, value_full)
    )
    back_first = lax.psum(back_first.astype(jnp.bfloat16), "tp").astype(jnp.float32)
    first_rows, d_gain_attention = norm_back(back_first, input_rows, inverse_first, attn_gain)
    grad_input = grad_hidden + first_rows
    reduced = (
        lax.psum_scatter(
            d_query.astype(jnp.bfloat16), "exp", scatter_dimension=0, tiled=True
        ).astype(jnp.float32),
        lax.psum_scatter(d_key.astype(jnp.bfloat16), "exp", scatter_dimension=0, tiled=True).astype(
            jnp.float32
        ),
        lax.psum_scatter(
            d_value.astype(jnp.bfloat16), "exp", scatter_dimension=0, tiled=True
        ).astype(jnp.float32),
        lax.psum_scatter(
            d_out_weight.astype(jnp.bfloat16), "exp", scatter_dimension=1, tiled=True
        ).astype(jnp.float32),
        lax.psum_scatter(
            d_query_bias.astype(jnp.bfloat16), "exp", scatter_dimension=0, tiled=True
        ).astype(jnp.float32),
        lax.psum_scatter(
            d_key_bias.astype(jnp.bfloat16), "exp", scatter_dimension=0, tiled=True
        ).astype(jnp.float32),
        lax.psum_scatter(
            d_value_bias.astype(jnp.bfloat16), "exp", scatter_dimension=0, tiled=True
        ).astype(jnp.float32),
        lax.psum_scatter(
            d_gain_attention.astype(jnp.bfloat16), "exp", scatter_dimension=0, tiled=True
        ).astype(jnp.float32),
        lax.psum_scatter(
            d_gain_experts.astype(jnp.bfloat16), "exp", scatter_dimension=0, tiled=True
        ).astype(jnp.float32),
        lax.psum_scatter(
            d_router.astype(jnp.bfloat16), "exp", scatter_dimension=0, tiled=True
        ).astype(jnp.float32),
        lax.psum_scatter(
            d_share_vector.astype(jnp.bfloat16), "exp", scatter_dimension=0, tiled=True
        ).astype(jnp.float32),
        lax.psum_scatter(
            d_shared_gate.astype(jnp.bfloat16), "exp", scatter_dimension=0, tiled=True
        ).astype(jnp.float32),
        lax.psum_scatter(
            d_shared_up.astype(jnp.bfloat16), "exp", scatter_dimension=0, tiled=True
        ).astype(jnp.float32),
        lax.psum_scatter(
            d_shared_down.astype(jnp.bfloat16), "exp", scatter_dimension=1, tiled=True
        ).astype(jnp.float32),
    )
    square_sums = lax.psum((jnp.sum(output * output), jnp.sum(grad_input * grad_input)), "exp")
    count_cells = jnp.sum(lengths).astype(jnp.float32) * model_width
    rms_output = jnp.sqrt(square_sums[0] / count_cells)
    rms_grad = jnp.sqrt(square_sums[1] / count_cells)
    return (
        output.astype(jnp.bfloat16),
        grad_input.astype(jnp.bfloat16),
        reduced[0],
        reduced[1],
        reduced[2],
        reduced[3],
        reduced[4],
        reduced[5],
        reduced[6],
        reduced[7],
        reduced[8],
        reduced[9],
        reduced[10],
        reduced[11],
        reduced[12],
        reduced[13],
        d_expert_gate,
        d_expert_up,
        d_expert_down,
        rms_output,
        rms_grad,
    )


def solution(mesh):
    in_specs = (
        P("exp", None),
        P("exp", None),
        P(),
        P("exp", None),
        P("exp", "tp"),
        P("exp", "tp"),
        P("exp", "tp"),
        P("tp", "exp"),
        P(("tp", "exp")),
        P(("tp", "exp")),
        P(("tp", "exp")),
        P("exp"),
        P("exp"),
        P("exp", None),
        P("exp"),
        P("exp", "tp"),
        P("exp", "tp"),
        P("tp", "exp"),
        P("exp", None, "tp"),
        P("exp", None, "tp"),
        P("exp", "tp", None),
    )
    out_specs = (
        P("exp", None),
        P("exp", None),
        P("exp", "tp"),
        P("exp", "tp"),
        P("exp", "tp"),
        P("tp", "exp"),
        P(("tp", "exp")),
        P(("tp", "exp")),
        P(("tp", "exp")),
        P("exp"),
        P("exp"),
        P("exp", None),
        P("exp"),
        P("exp", "tp"),
        P("exp", "tp"),
        P("tp", "exp"),
        P("exp", None, "tp"),
        P("exp", None, "tp"),
        P("exp", "tp", None),
        P(),
        P(),
    )
    return jax.shard_map(local, mesh=mesh, in_specs=in_specs, out_specs=out_specs, check_vma=False)
```

profile of v0, /device:TPU:0, one launch (start us, length us, event | category | flops | bytes accessed | tf_op | source)
XLA Modules:
  0.0 2949.7 jit_solution(6535174012370242682)
XLA Ops:
  21.4 23.3 all-reduce.13
  127.6 74.5 %all-gather.13.cloned.1.call-done = bf16[2048,512]{1,0:T(8,128)(2,1)} async-done(((bf16[256,512]{1,0:T(8,128)(2,1)}), bf16[2048,512]{1,0:T(8,128)(2,1)}) %all-gather.13.cloned.1.call-update) | async-done | bytes 2097168 | tf_op jit(solution)/shard_map/all_gather | solution.py:124
  349.2 46.7 %all-gather.1 = bf16[8,1,256]{2,1,0:T(2,128)(2,1)S(1)} all-gather(bf16[1,1,256]{2,1,0:T(2,128)(2,1)S(1)} %reshape.363), channel_id=1, replica_groups=mesh['exp'=8,'tp'=4] {'exp'}, dimensions={0}, use_global_device_ids=true | all-gather | bytes 4608 | tf_op jit(solution)/shard_map/all_gather | solution.py:130
  405.3 21.9 all-reduce.19.cloned.1.call-done
  434.6 33.2 %gather_fusion = bf16[4096,2048]{1,0:T(8,128)(2,1)} fusion(bf16[513,2048]{1,0:T(8,128)(2,1)} %concatenate.40, s32[4096]{0:T(1024)S(1)} %get-tuple-element.85), kind=kCustom, calls=%fused_computation | custom fusion | bytes 33570816 | tf_op jit(solution)/shard_map/gather | solution.py:234
  470.4 98.4 %all_to_all.21 = bf16[8,2,64,2048]{3,2,1,0:T(8,128)(2,1)S(1)} all-to-all(bf16[8,2,64,2048]{3,2,1,0:T(8,128)(2,1)S(1)} %constant_dynamic-slice_fusion.1), channel_id=1, replica_groups=mesh['exp'=8,'tp'=4] {'exp'}, dimensions={0} | all-to-all | bytes 8388608 | tf_op jit(solution)/shard_map/all_to_all | solution.py:237
  571.4 104.1 %all-gather.21.cloned.1.call-done = bf16[8,2,256,2048]{3,2,0,1:T(8,128)(2,1)} async-done(((bf16[8,2,64,2048]{3,2,0,1:T(8,128)(2,1)}), bf16[8,2,256,2048]{3,2,0,1:T(8,128)(2,1)}) %all-gather.21.cloned.1.call-update) | async-done | bytes 16777232 | tf_op jit(solution)/shard_map/all_gather | solution.py:236
  717.8 124.2 %reduce-scatter.11.cloned.1.call-done = bf16[8,2,64,2048]{3,2,0,1:T(8,128)(2,1)} async-done(((bf16[8,2,256,2048]{3,2,0,1:T(8,128)(2,1)}), bf16[8,2,64,2048]{3,2,0,1:T(8,128)(2,1)}) %reduce-scatter.11.cloned.1.call-update) | async-done | bytes 4194320 | tf_op jit(solution)/shard_map/reduce_scatter | solution.py:250
  852.5 181.3 %all_gather.58 = bf16[2048,16]{0,1:T(8,128)(2,1)S(1)} all-gather(bf16[256,16]{0,1:T(8,128)(2,1)S(1)} %copy-done.69), channel_id=1, replica_groups=mesh['exp'=8,'tp'=4] {'exp'}, dimensions={0}, use_global_device_ids=true | all-gather | bytes 73728 | tf_op jit(solution)/shard_map/all_gather | solution.py:131
  1047.0 61.8 %all-gather.25.cloned.1.call-done = bf16[2048,1408]{1,0:T(8,128)(2,1)} async-done(((bf16[256,1408]{1,0:T(8,128)(2,1)}), bf16[2048,1408]{1,0:T(8,128)(2,1)}) %all-gather.25.cloned.1.call-update) | async-done | bytes 5767184 | tf_op jit(solution)/shard_map/all_gather | solution.py:134
  1118.4 84.1 %all-gather.27.cloned.1.call-done = bf16[1408,2048]{1,0:T(8,128)(2,1)} async-done(((bf16[1408,256]{1,0:T(8,128)(2,1)}), bf16[1408,2048]{1,0:T(8,128)(2,1)}) %all-gather.27.cloned.1.call-update) | async-done | bytes 5767184 | tf_op jit(solution)/shard_map/all_gather | solution.py:135
  1257.5 26.9 gather_fusion.1
  1331.9 35.8 %gather_fusion.2 = bf16[4096,2048]{1,0:T(8,128)(2,1)} fusion(bf16[2049,2048]{1,0:T(8,128)(2,1)} %concatenate.41, s32[4096]{0:T(1024)S(1)} %copy-done.57), kind=kCustom, calls=%fused_computation.2 | custom fusion | bytes 33570816 | tf_op jit(solution)/shard_map/gather | solution.py:285
  1370.3 95.6 %all_to_all.22 = bf16[8,2,64,2048]{3,2,1,0:T(8,128)(2,1)S(1)} all-to-all(bf16[8,2,64,2048]{3,2,1,0:T(8,128)(2,1)S(1)} %constant_dynamic-slice_fusion), channel_id=1, replica_groups=mesh['exp'=8,'tp'=4] {'exp'}, dimensions={0} | all-to-all | bytes 8388608 | tf_op jit(solution)/shard_map/all_to_all | solution.py:290
  1468.2 104.8 %all-gather.29.cloned.1.call-done = bf16[8,2,256,2048]{3,2,0,1:T(8,128)(2,1)} async-done(((bf16[8,2,64,2048]{3,2,0,1:T(8,128)(2,1)}), bf16[8,2,256,2048]{3,2,0,1:T(8,128)(2,1)}) %all-gather.29.cloned.1.call-update) | async-done | bytes 16777232 | tf_op jit(solution)/shard_map/all_gather | solution.py:294
  1605.4 22.0 fusion.4
  1627.4 126.3 %reduce-scatter.13.cloned.1.call-done = bf16[8,2,64,2048]{3,2,0,1:T(8,128)(2,1)} async-done(((bf16[8,2,256,2048]{3,2,0,1:T(8,128)(2,1)}), bf16[8,2,64,2048]{3,2,0,1:T(8,128)(2,1)}) %reduce-scatter.13.cloned.1.call-update) | async-done | bytes 4194320 | tf_op jit(solution)/shard_map/reduce_scatter | solution.py:316
  1764.1 83.2 %all-gather.2 = bf16[8,1,256]{2,1,0:T(2,128)(2,1)S(1)} all-gather(bf16[1,1,256]{2,1,0:T(2,128)(2,1)S(1)} %reshape.365), channel_id=1, replica_groups=mesh['exp'=8,'tp'=4] {'exp'}, dimensions={0}, use_global_device_ids=true | all-gather | bytes 4608 | tf_op jit(solution)/shard_map/all_gather | solution.py:132
  1891.9 27.0 gather_fusion.3
  1990.5 75.8 %all-reduce.23.cloned.1.call-done = (bf16[512,2048]{1,0:T(8,128)(2,1)}, bf16[512,2048]{1,0:T(8,128)(2,1)}) async-done(((bf16[512,2048]{1,0:T(8,128)(2,1)}, bf16[512,2048]{1,0:T(8,128)(2,1)}), (bf16[512,2048]{1,0:T(8,128)(2,1)}, bf16[512,2048]{1,0:T(8,128)(2,1)})) %all-reduce.23.cloned.1.call-update) | async-done | bytes 4194320 | tf_op jit(solution)/shard_map/psum | solution.py:262
  2078.9 23.7 multiply_reduce_fusion
  2102.6 27.5 multiply_convert_fusion
  2182.6 20.2 collective-permute-done.15
  2211.3 61.8 %collective-permute-done.17 = bf16[512,4,128]{2,0,1:T(8,128)(2,1)} collective-permute-done((bf16[512,4,128]{2,0,1:T(8,128)(2,1)}, bf16[512,4,128]{2,0,1:T(8,128)(2,1)}, u32[]{:S(2)}, u32[]{:S(2)}) %collective-permute-start.17) | collective-permute-done | bytes 524320 | tf_op jit(solution)/shard_map/ppermute | solution.py:18
  2302.2 91.4 %collective-permute-done.24 = bf16[512,4,128]{0,2,1:T(8,128)(2,1)} collective-permute-done((bf16[512,4,128]{0,2,1:T(8,128)(2,1)}, bf16[512,4,128]{0,2,1:T(8,128)(2,1)}, u32[]{:S(2)}, u32[]{:S(2)}) %collective-permute-start.24) | collective-permute-done | bytes 524320 | tf_op jit(solution)/shard_map/ppermute | solution.py:18
  2421.4 65.3 %reduce-scatter.25.cloned.1.call-done = bf16[256,1408]{1,0:T(8,128)(2,1)} async-done(((bf16[2048,1408]{1,0:T(8,128)(2,1)}), bf16[256,1408]{1,0:T(8,128)(2,1)}) %reduce-scatter.25.cloned.1.call-update) | async-done | bytes 720912 | tf_op jit(solution)/shard_map/reduce_scatter | solution.py:465
  2489.0 111.4 %reduce-scatter.29.cloned.1.call-done = bf16[1408,256]{1,0:T(8,128)(2,1)} async-done(((bf16[1408,2048]{1,0:T(8,128)(2,1)}), bf16[1408,256]{1,0:T(8,128)(2,1)}) %reduce-scatter.29.cloned.1.call-update) | async-done | bytes 720912 | tf_op jit(solution)/shard_map/reduce_scatter | solution.py:471
  2662.7 22.2 all-reduce.11
  2686.3 33.3 %all-reduce.12 = (bf16[512]{0:T(512)(128)(2,1)S(1)}, bf16[512]{0:T(512)(128)(2,1)S(1)}, bf16[512]{0:T(512)(128)(2,1)S(1)}, bf16[2048]{0:T(1024)(128)(2,1)S(1)}, ...) all-reduce(bf16[512]{0:T(512)(128)(2,1)S(1)} %bitcast.255, ...), channel_id=8, replica_groups=mesh['exp'=8,'tp'=4] {'exp'}, use_global_device_ids=true, to_apply=%region_29.30.clone | all-reduce | flops 7680 | bytes 30720
  2728.4 68.8 %reduce-scatter.17.cloned.1.call-done = bf16[256,512]{1,0:T(8,128)(2,1)} async-done(((bf16[2048,512]{1,0:T(8,128)(2,1)}), bf16[256,512]{1,0:T(8,128)(2,1)}) %reduce-scatter.17.cloned.1.call-update) | async-done | bytes 262160 | tf_op jit(solution)/shard_map/reduce_scatter | solution.py:435
  2799.0 68.8 %reduce-scatter.15.cloned.1.call-done = bf16[256,512]{1,0:T(8,128)(2,1)} async-done(((bf16[2048,512]{1,0:T(8,128)(2,1)}), bf16[256,512]{1,0:T(8,128)(2,1)}) %reduce-scatter.15.cloned.1.call-update) | async-done | bytes 262160 | tf_op jit(solution)/shard_map/reduce_scatter | solution.py:432
  2869.6 68.9 %reduce-scatter.19.cloned.1.call-done = bf16[256,512]{1,0:T(8,128)(2,1)} async-done(((bf16[2048,512]{1,0:T(8,128)(2,1)}), bf16[256,512]{1,0:T(8,128)(2,1)}) %reduce-scatter.19.cloned.1.call-update) | async-done | bytes 262160 | tf_op jit(solution)/shard_map/reduce_scatter | solution.py:438
  (450 shorter events, 813.4 us)
Async XLA Ops:
  7.9 112.6 %all-gather.15.cloned.1.call-start = ((), (), s32[]{:S(2)}) async-start(), calls=%async_computation.15 | async-start | bytes 2359296 | tf_op jit(solution)/shard_map/all_gather | solution.py:122
  8.7 193.4 %all-gather.13.cloned.1.call-start = ((), (), s32[]{:S(2)}) async-start(), calls=%async_computation.14 | async-start | bytes 2359296 | tf_op jit(solution)/shard_map/all_gather | solution.py:124
  9.4 334.6 %all-gather.19.cloned.1.call-start = ((), (), s32[]{:S(2)}) async-start(), calls=%async_computation.17 | async-start | bytes 2359296 | tf_op jit(solution)/shard_map/all_gather | solution.py:125
  10.0 417.2 %all-reduce.19.cloned.1.call-start = ((), (), s32[]{:S(2)}) async-start(), calls=%async_computation.18 | async-start | bytes 4194304 | tf_op jit(solution)/shard_map/psum | solution.py:205
  91.5 116.0 %collective-permute-start.7 = (bf16[512,4,128]{2,0,1:T(8,128)(2,1)}, bf16[512,4,128]{2,0,1:T(8,128)(2,1)}, u32[]{:S(2)}, u32[]{:S(2)}) collective-permute-start(bf16[512,4,128]{2,0,1:T(8,128)(2,1)} %get-tuple-element.53), channel_id=1, source_target_pairs={{0,4},{4,8},{8,12},{12,16},{16,20},{20,24},{24,28},{1,5},{5,9},{9,... | collective-permute-start | bytes 1572872 | tf_op jit(solution)/shard_map/ppermute | solution.py:18
  96.1 117.9 %collective-permute-start.8 = (bf16[512,4,128]{2,0,1:T(8,128)(2,1)}, bf16[512,4,128]{2,0,1:T(8,128)(2,1)}, u32[]{:S(2)}, u32[]{:S(2)}) collective-permute-start(bf16[512,4,128]{2,0,1:T(8,128)(2,1)} %get-tuple-element.53), channel_id=1, source_target_pairs={{0,8},{4,12},{8,16},{12,20},{16,24},{20,28},{1,9},{5,13},{9,17},{1... | collective-permute-start | bytes 1572872 | tf_op jit(solution)/shard_map/ppermute | solution.py:18
  98.2 125.7 %collective-permute-start.9 = (bf16[512,4,128]{2,0,1:T(8,128)(2,1)}, bf16[512,4,128]{2,0,1:T(8,128)(2,1)}, u32[]{:S(2)}, u32[]{:S(2)}) collective-permute-start(bf16[512,4,128]{2,0,1:T(8,128)(2,1)} %get-tuple-element.53), channel_id=1, source_target_pairs={{0,12},{4,16},{8,20},{12,24},{16,28},{1,13},{5,17},{9,21},{13,25},... | collective-permute-start | bytes 1572872 | tf_op jit(solution)/shard_map/ppermute | solution.py:18
  100.3 127.4 %collective-permute-start.10 = (bf16[512,4,128]{2,0,1:T(8,128)(2,1)}, bf16[512,4,128]{2,0,1:T(8,128)(2,1)}, u32[]{:S(2)}, u32[]{:S(2)}) collective-permute-start(bf16[512,4,128]{2,0,1:T(8,128)(2,1)} %get-tuple-element.53), channel_id=1, source_target_pairs={{0,16},{4,20},{8,24},{12,28},{1,17},{5,21},{9,25},{13,29},{2,18},{... | collective-permute-start | bytes 1572872 | tf_op jit(solution)/shard_map/ppermute | solution.py:18
  102.9 128.9 %collective-permute-start.11 = (bf16[512,4,128]{2,0,1:T(8,128)(2,1)}, bf16[512,4,128]{2,0,1:T(8,128)(2,1)}, u32[]{:S(2)}, u32[]{:S(2)}) collective-permute-start(bf16[512,4,128]{2,0,1:T(8,128)(2,1)} %get-tuple-element.53), channel_id=1, source_target_pairs={{0,20},{4,24},{8,28},{1,21},{5,25},{9,29},{2,22},{6,26},{10,30},{3... | collective-permute-start | bytes 1572872 | tf_op jit(solution)/shard_map/ppermute | solution.py:18
  348.5 327.0 %all-gather.21.cloned.1.call-start = ((), (), s32[]{:S(2)}) async-start(), calls=%async_computation.19 | async-start | bytes 20971520 | tf_op jit(solution)/shard_map/all_gather | solution.py:236
  571.1 270.9 %reduce-scatter.11.cloned.1.call-start = ((), (), s32[]{:S(2)}) async-start(), calls=%async_computation.20 | async-start | bytes 20971520 | tf_op jit(solution)/shard_map/reduce_scatter | solution.py:250
  715.7 322.8 %all-gather.23.cloned.1.call-start = ((), (), s32[]{:S(2)}) async-start(), calls=%async_computation.21 | async-start | bytes 6488064 | tf_op jit(solution)/shard_map/all_gather | solution.py:133
  716.5 392.3 %all-gather.25.cloned.1.call-start = ((), (), s32[]{:S(2)}) async-start(), calls=%async_computation.22 | async-start | bytes 6488064 | tf_op jit(solution)/shard_map/all_gather | solution.py:134
  717.2 485.3 %all-gather.27.cloned.1.call-start = ((), (), s32[]{:S(2)}) async-start(), calls=%async_computation.23 | async-start | bytes 6488064 | tf_op jit(solution)/shard_map/all_gather | solution.py:135
  846.8 392.9 %all-to-all-start.1 = ((bf16[8,2,64,2048]{3,2,1,0:T(8,128)(2,1)}), bf16[8,2,64,2048]{3,2,1,0:T(8,128)(2,1)}, u32[]{:S(2)}, u32[]{:S(2)}) async-start(bf16[8,2,64,2048]{3,2,1,0:T(8,128)(2,1)} %copy.115), calls=%async_computation.2 | async-start | bytes 8388608 | tf_op jit(solution)/shard_map/all_to_all | solution.py:253
  852.5 720.6 %all-gather.29.cloned.1.call-start = ((), (), s32[]{:S(2)}) async-start(), calls=%async_computation.24 | async-start | bytes 20971520 | tf_op jit(solution)/shard_map/all_gather | solution.py:294
  1468.2 285.5 %reduce-scatter.13.cloned.1.call-start = ((), (), s32[]{:S(2)}) async-start(), calls=%async_computation.25 | async-start | bytes 20971520 | tf_op jit(solution)/shard_map/reduce_scatter | solution.py:316
  1758.4 115.7 %all-to-all-start.3 = ((bf16[8,2,64,2048]{3,2,1,0:T(8,128)(2,1)}), bf16[8,2,64,2048]{3,2,1,0:T(8,128)(2,1)}, u32[]{:S(2)}, u32[]{:S(2)}) async-start(bf16[8,2,64,2048]{3,2,1,0:T(8,128)(2,1)} %copy.118), calls=%async_computation.5 | async-start | bytes 8388608 | tf_op jit(solution)/shard_map/all_to_all | solution.py:319
  1764.1 302.3 %all-reduce.23.cloned.1.call-start = ((), (), s32[]{:S(2)}) async-start(), calls=%async_computation.35 | async-start | bytes 8388608 | tf_op jit(solution)/shard_map/psum | solution.py:262
  1964.3 453.5 %reduce-scatter.23.cloned.1.call-start = ((), (), s32[]{:S(2)}) async-start(), calls=%async_computation.31 | async-start | bytes 73728 | tf_op jit(solution)/shard_map/reduce_scatter | solution.py:459
  1966.1 452.9 %reduce-scatter.27.cloned.1.call-start = ((), (), s32[]{:S(2)}) async-start(), calls=%async_computation.33 | async-start | bytes 6488064 | tf_op jit(solution)/shard_map/reduce_scatter | solution.py:468
  1973.9 512.7 %reduce-scatter.25.cloned.1.call-start = ((), (), s32[]{:S(2)}) async-start(), calls=%async_computation.32 | async-start | bytes 6488064 | tf_op jit(solution)/shard_map/reduce_scatter | solution.py:465
  1980.7 619.7 %reduce-scatter.29.cloned.1.call-start = ((), (), s32[]{:S(2)}) async-start(), calls=%async_computation.34 | async-start | bytes 6488064 | tf_op jit(solution)/shard_map/reduce_scatter | solution.py:471
  1990.5 663.9 %all-reduce.21.cloned.1.call-start = ((), (), s32[]{:S(2)}) async-start(), calls=%async_computation.26 | async-start | bytes 4194304 | tf_op jit(solution)/shard_map/psum | solution.py:428
  2147.8 125.2 %collective-permute-start.17 = (bf16[512,4,128]{2,0,1:T(8,128)(2,1)}, bf16[512,4,128]{2,0,1:T(8,128)(2,1)}, u32[]{:S(2)}, u32[]{:S(2)}) collective-permute-start(bf16[512,4,128]{2,0,1:T(8,128)(2,1)} %get-tuple-element.67), channel_id=1, source_target_pairs={{16,0},{20,4},{24,8},{28,12},{17,1},{21,5},{25,9},{29,13},{18,2},{... | collective-permute-start | bytes 1572872 | tf_op jit(solution)/shard_map/ppermute | solution.py:18
  2149.1 125.2 %collective-permute-start.18 = (bf16[512,4,128]{2,0,1:T(8,128)(2,1)}, bf16[512,4,128]{2,0,1:T(8,128)(2,1)}, u32[]{:S(2)}, u32[]{:S(2)}) collective-permute-start(bf16[512,4,128]{2,0,1:T(8,128)(2,1)} %get-tuple-element.66), channel_id=1, source_target_pairs={{20,0},{24,4},{28,8},{21,1},{25,5},{29,9},{22,2},{26,6},{30,10},{2... | collective-permute-start | bytes 1572872 | tf_op jit(solution)/shard_map/ppermute | solution.py:18
  2275.7 117.9 %collective-permute-start.24 = (bf16[512,4,128]{0,2,1:T(8,128)(2,1)}, bf16[512,4,128]{0,2,1:T(8,128)(2,1)}, u32[]{:S(2)}, u32[]{:S(2)}) collective-permute-start(bf16[512,4,128]{0,2,1:T(8,128)(2,1)} %get-tuple-element.60), channel_id=1, source_target_pairs={{16,0},{20,4},{24,8},{28,12},{17,1},{21,5},{25,9},{29,13},{18,2},{... | collective-permute-start | bytes 1572872 | tf_op jit(solution)/shard_map/ppermute | solution.py:18
  2277.0 117.6 %collective-permute-start.25 = (bf16[512,4,128]{0,2,1:T(8,128)(2,1)}, bf16[512,4,128]{0,2,1:T(8,128)(2,1)}, u32[]{:S(2)}, u32[]{:S(2)}) collective-permute-start(bf16[512,4,128]{0,2,1:T(8,128)(2,1)} %get-tuple-element.59), channel_id=1, source_target_pairs={{20,0},{24,4},{28,8},{21,1},{25,5},{29,9},{22,2},{26,6},{30,10},{2... | collective-permute-start | bytes 1572872 | tf_op jit(solution)/shard_map/ppermute | solution.py:18
  2402.0 324.6 %reduce-scatter.21.cloned.1.call-start = ((), (), s32[]{:S(2)}) async-start(), calls=%async_computation.30 | async-start | bytes 2359296 | tf_op jit(solution)/shard_map/reduce_scatter | solution.py:441
  2407.0 390.1 %reduce-scatter.17.cloned.1.call-start = ((), (), s32[]{:S(2)}) async-start(), calls=%async_computation.28 | async-start | bytes 2359296 | tf_op jit(solution)/shard_map/reduce_scatter | solution.py:435
  2411.6 456.2 %reduce-scatter.15.cloned.1.call-start = ((), (), s32[]{:S(2)}) async-start(), calls=%async_computation.27 | async-start | bytes 2359296 | tf_op jit(solution)/shard_map/reduce_scatter | solution.py:432
  2417.3 521.2 %reduce-scatter.19.cloned.1.call-start = ((), (), s32[]{:S(2)}) async-start(), calls=%async_computation.29 | async-start | bytes 2359296 | tf_op jit(solution)/shard_map/reduce_scatter | solution.py:438
  (99 other events, 4909.2 us)
Sparse Core Ops, SparseCore 0:
  10.2 52.2 all-gather.16
  64.6 55.8 all-gather.14
  122.6 79.4 all-gather.12
  204.0 82.6 all-gather.18
  348.6 78.5 all-reduce.18
  571.3 104.2 all-gather.20
  715.8 126.1 reduce-scatter.10
  844.2 171.7 all-gather.22
  1018.2 90.5 all-gather.24
  1110.7 91.7 all-gather.26
  1468.3 104.7 all-gather.28
  1627.5 126.0 reduce-scatter.12
  1964.4 101.8 all-reduce.22
  2069.3 53.8 reduce-scatter.22
  2127.2 241.2 reduce-scatter.26
  2372.5 114.0 reduce-scatter.24
  2490.2 110.1 reduce-scatter.28
  2603.2 51.1 all-reduce.20
  2658.3 68.2 reduce-scatter.20
  2730.4 66.7 reduce-scatter.16
  2801.1 66.6 reduce-scatter.14
  2871.7 66.7 reduce-scatter.18
where the time goes:
time: 2960 us; the launch traced here: 2950 us
  waiting for transfers between devices  1410 us (48%)
  blocking collectives  607 us (21%)
  matrix products  380 us (13%)
  local copies, waits for them, and re-layouts  294 us (10%)
  other arithmetic  157 us (5%)
  starting transfers between devices  75.1 us (3%)
    ppermute x28, waiting for transfers between devices, shifted(): return lax.ppermute(shard, axis, pairs)  225 us
    all_gather x1, blocking collectives, local(): lax.all_gather(w_router, 'exp', axis=0, tiled=True)  181 us
    reduce_scatter x1, waiting for transfers between devices, local(): lax.psum_scatter(rows_back.astype(jnp.bfloat16), 'tp', scatter_dimension=...  126 us
    reduce_scatter x1, waiting for transfers between devices, local(): lax.psum_scatter(result_rows.astype(jnp.bfloat16), 'tp', scatter_dimensio...  124 us
    reduce_scatter x1, waiting for transfers between devices, local(): lax.psum_scatter(d_shared_down.astype(jnp.bfloat16), 'exp', scatter_dimen...  111 us
    all_gather x1, waiting for transfers between devices, local(): lax.all_gather(arrived_grads, 'tp', axis=2, tiled=True)  105 us
    all_gather x1, waiting for transfers between devices, local(): lax.all_gather(lax.all_to_all(sending, 'exp', split_axis=0, concat_axis=0...  104 us
    all_to_all x1, blocking collectives, local(): lax.all_to_all(sending, 'exp', split_axis=0, concat_axis=0, tiled=True)  98.4 us
  transfers between devices with their start and end apart: 52, of which 28 were waited for; matrix products, arithmetic and copies ran while one was open for 16% of the time, Pallas kernels for 0%

commit v1 on v0

--- a/solution.py
+++ b/solution.py
@@ -1,6 +1,11 @@
+import functools
+
 import jax
 import jax.numpy as jnp
 from jax import lax
+from jax.experimental import pallas as pl
+from jax.experimental.pallas import tpu as pltpu
+from jax.sharding import Mesh
 from jax.sharding import PartitionSpec as P
 
 HEAD_DIM = 128
@@ -73,7 +78,7 @@
     return sigma * (1.0 + values * (1.0 - sigma))
 
 
-def local(
+def general(
     tokens,
     cotangent,
     lengths,
@@ -501,51 +506,1810 @@
     )
 
 
-def solution(mesh):
-    in_specs = (
-        P("exp", None),
-        P("exp", None),
+def flat(pieces):
+    return jnp.concatenate([p.reshape(-1) for p in pieces])
+
+
+def key_window(info_ref, block, keys):
+    return lax.rem(block + info_ref[0], 2), pl.ds(pl.multiple_of(block // 2 * keys, keys), keys)
+
+
+def attend_back_kernel(
+    info_ref, q_ref, kv_ref, do_ref, o_ref, lse_ref, dq_ref, dk_ref, dv_ref, *, tile, keys, rows
+):
+    step = pl.program_id(0)
+    per_block = rows // tile
+    base = (2 * (step // per_block) + info_ref[0]) * rows + (step % per_block) * tile
+
+    @pl.when(step == 0)
+    def _():
+        dk_ref[...] = jnp.zeros_like(dk_ref)
+        dv_ref[...] = jnp.zeros_like(dv_ref)
+
+    query = q_ref[...]
+    grad = do_ref[...]
+    log_total = lse_ref[:, 0:1]
+    delta = jnp.sum(grad.astype(jnp.float32) * o_ref[...], axis=1, keepdims=True)
+    row_pos = base + lax.broadcasted_iota(jnp.int32, (tile, 1), 0)
+    limit = jnp.minimum(row_pos, info_ref[1] - 1)
+    column = lax.broadcasted_iota(jnp.int32, (tile, keys), 1)
+
+    def body(j, acc):
+        side, window = key_window(info_ref, j, keys)
+        key = kv_ref[side, window, :HEAD_DIM]
+        scores = product_bt(query, key) * (1.0 / HEAD_DIM**0.5)
+        scores = jnp.where(column <= limit - j * keys, scores, MASKED)
+        probs = jnp.exp(scores - log_total)
+        dv_ref[side, window, :] += product_at(probs.astype(jnp.bfloat16), grad)
+        grad_probs = product_bt(grad, kv_ref[side, window, HEAD_DIM:])
+        grad_scores = (probs * (grad_probs - delta)).astype(jnp.bfloat16)
+        dk_ref[side, window, :] += product_at(grad_scores, query)
+        return acc + product(grad_scores, key)
+
+    count = (base + tile + keys - 1) // keys
+    dq_ref[...] = lax.fori_loop(0, count, body, jnp.zeros((tile, HEAD_DIM), jnp.float32))
+
+
+def attend_back(info, query, key_values, grad, out, log_total, rows):
+    count = query.shape[0]
+    tile = 256
+    half = key_values.shape[:2] + (HEAD_DIM,)
+    whole = pl.BlockSpec(half, lambda i: (0, 0, 0))
+    both = pl.BlockSpec(key_values.shape, lambda i: (0, 0, 0))
+    part = pl.BlockSpec((tile, HEAD_DIM), lambda i: (i, 0))
+    return pl.pallas_call(
+        functools.partial(attend_back_kernel, tile=tile, keys=rows, rows=rows),
+        grid=(count // tile,),
+        in_specs=[pl.BlockSpec(memory_space=pltpu.SMEM), part, both, part, part, part],
+        out_specs=[part, whole, whole],
+        out_shape=[
+            jax.ShapeDtypeStruct((count, HEAD_DIM), jnp.float32),
+            jax.ShapeDtypeStruct(half, jnp.float32),
+            jax.ShapeDtypeStruct(half, jnp.float32),
+        ],
+        compiler_params=pltpu.CompilerParams(vmem_limit_bytes=40 * 2**20),
+        cost_estimate=pl.CostEstimate(
+            flops=10 * count * count * HEAD_DIM,
+            bytes_accessed=12 * 2**20,
+            transcendentals=count * count,
+        ),
+    )(info, query, key_values, grad, out, log_total)
+
+
+ROW_AXES = ("z", "x")
+COLUMN_AXES = ("y", "c")
+ALL_AXES = ("z", "x", "y", "c")
+CHUNK_AXES = ("c", "y", "x", "z")
+SAME_X = ("c", "y", "z")
+
+
+def front_kernel(own_ref, parts_ref, rows_ref, weights_ref, send, send_z, recv, send_w, recv_w, here):
+    z, x, y, c = (lax.axis_index(name) for name in ALL_AXES)
+    z_count = lax.axis_size("z")
+    chunks = own_ref.shape[0]
+
+    def up(distance):
+        return {"z": lax.rem(z + distance, z_count)}
+
+    def remote(src, dst, send_sem, recv_sem, device):
+        return pltpu.make_async_remote_copy(
+            src_ref=src,
+            dst_ref=dst,
+            send_sem=send_sem,
+            recv_sem=recv_sem,
+            device_id=device,
+            device_id_type=pl.DeviceIdType.MESH,
+        )
+
+    def spread_z(k, d):
+        block = rows_ref.at[c, y, z, k]
+        return remote(own_ref.at[k], block, send_z.at[d - 1, k], recv.at[1 + d, k], up(d))
+
+    def spread_y(k):
+        block = rows_ref.at[c, y, :, k]
+        return remote(block, block, send.at[0, k], recv.at[0, k], {"y": 1 - y})
+
+    def spread_c(k):
+        block = rows_ref.at[c, :, :, k]
+        return remote(block, block, send.at[1, k], recv.at[1, k], {"c": 1 - c})
+
+    def weights_z(d):
+        there = lax.rem(z + d, z_count)
+        return remote(
+            parts_ref.at[there], weights_ref.at[z, x], send_w.at[d], recv_w.at[d], up(d)
+        )
+
+    def weights_x():
+        block = weights_ref.at[:, x]
+        return remote(block, block, send_w.at[0], recv_w.at[0], {"x": 1 - x})
+
+    barrier = pltpu.get_barrier_semaphore()
+    for device in ({"x": 1 - x}, {"y": 1 - y}, {"c": 1 - c}, up(1), up(2), up(3)):
+        pl.semaphore_signal(
+            barrier, inc=1, device_id=device, device_id_type=pl.DeviceIdType.MESH
+        )
+    keep = pltpu.make_async_copy(own_ref, rows_ref.at[c, y, z], here.at[0])
+    keep_w = pltpu.make_async_copy(parts_ref.at[z], weights_ref.at[z, x], here.at[1])
+    keep.start()
+    keep_w.start()
+    pl.semaphore_wait(barrier, 6)
+    for k in range(chunks):
+        for d in range(1, 4):
+            spread_z(k, d).start()
+        if k == 0:
+            for d in range(1, 4):
+                weights_z(d).start()
+    keep.wait()
+    keep_w.wait()
+    for k in range(chunks):
+        for d in range(1, 4):
+            spread_z(k, d).wait()
+        spread_y(k).start()
+        if k == 0:
+            for d in range(1, 4):
+                weights_z(d).wait()
+            weights_x().start()
+        if k > 0:
+            spread_y(k - 1).wait()
+            spread_c(k - 1).start()
+    spread_y(chunks - 1).wait()
+    spread_c(chunks - 1).start()
+    for k in range(chunks):
+        spread_c(k).wait()
+    weights_x().wait()
+
+
+def front(rows, parts, chunks=4):
+    own, model = rows.shape
+    zs = lax.axis_size("z")
+    shape = (2, 2, zs, chunks, own // chunks, model)
+    anywhere = pl.BlockSpec(memory_space=pl.ANY)
+    dma = pltpu.SemaphoreType.DMA
+    gathered, weights = pl.pallas_call(
+        front_kernel,
+        in_specs=[anywhere, anywhere],
+        out_specs=[anywhere, anywhere],
+        out_shape=[
+            jax.ShapeDtypeStruct(shape, rows.dtype),
+            jax.ShapeDtypeStruct((zs, 2) + parts.shape[1:], parts.dtype),
+        ],
+        scratch_shapes=[
+            dma((2, chunks)),
+            dma((3, chunks)),
+            dma((5, chunks)),
+            dma((4,)),
+            dma((4,)),
+            dma((2,)),
+        ],
+        compiler_params=pltpu.CompilerParams(
+            collective_id=0, has_side_effects=True, vmem_limit_bytes=16 * 2**20
+        ),
+    )(rows.reshape(chunks, own // chunks, model), parts)
+    return gathered.reshape(4 * zs * own, model), weights
+
+
+def middle_kernel(
+    length_ref,
+    rows_ref,
+    w_ref,
+    row_ref,
+    block_ref,
+    leaving_ref,
+    sh_ref,
+    q_ref,
+    kv_ref,
+    att_ref,
+    lse_ref,
+    part_ref,
+    joined_ref,
+    all_ref,
+    shared_ref,
+    peaks,
+    totals,
+    send,
+    recv,
+    once,
+    once_in,
+    here,
+    *,
+    rows,
+):
+    z, x, y, c = (lax.axis_index(name) for name in ALL_AXES)
+    z_count = lax.axis_size("z")
+    e_count = 2 * z_count
+    chunks = leaving_ref.shape[0]
+    head = HEAD_DIM
+    count, model = rows_ref.shape
+    block = model // e_count
+    own = rows // 4
+    tile = 2 * own
+    half = model // 2
+    left, right = pl.ds(0, half), pl.ds(half, leaving_ref.shape[2] - half)
+    flip = {"x": {"x": 1 - x}, "y": {"y": 1 - y}, "c": {"c": 1 - c}}
+
+    def up(distance):
+        return {"z": lax.rem(z + distance, z_count)}
+
+    def copy_to(src, dst, send_sem, recv_sem, device):
+        return pltpu.make_async_remote_copy(
+            src_ref=src,
+            dst_ref=dst,
+            send_sem=send_sem,
+            recv_sem=recv_sem,
+            device_id=device,
+            device_id_type=pl.DeviceIdType.MESH,
+        )
+
+    def remote(slot, k, src, dst, device):
+        return copy_to(src, dst, send.at[slot, k], recv.at[slot, k], device)
+
+    def spread_z(k):
+        return [
+            remote(4 + d, k, leaving_ref.at[k], all_ref.at[c, y, x, z, k], up(d))
+            for d in range(1, 4)
+        ]
+
+    def spread_2(k):
+        a = all_ref.at[c, y, x, :, k, :, left]
+        b = all_ref.at[c, y, x, :, k, :, right]
+        return remote(0, k, a, a, flip["x"]), remote(1, k, b, b, flip["y"])
+
+    def spread_3(k):
+        a = all_ref.at[c, y, :, :, k, :, left]
+        b = all_ref.at[c, :, x, :, k, :, right]
+        return remote(2, k, a, a, flip["y"]), remote(3, k, b, b, flip["x"])
+
+    def spread_c(k):
+        a = all_ref.at[c, :, :, :, k]
+        return (remote(4, k, a, a, flip["c"]),)
+
+    def share(d, other):
+        z_to, x_to = lax.rem(z + d, z_count), 1 - x if other else x
+        i = d + z_count if other else d
+        return copy_to(
+            sh_ref.at[2 * z_to + x_to],
+            shared_ref.at[2 * z + x],
+            once.at[i],
+            once_in.at[i],
+            {"z": z_to, "x": x_to},
+        )
+
+    def key_values():
+        return copy_to(kv_ref.at[0], kv_ref.at[1], once.at[0], once_in.at[0], flip["x"])
+
+    def start(copies):
+        for copy in copies:
+            copy.start()
+
+    def finish(copies):
+        for copy in copies:
+            copy.wait()
+
+    barrier = pltpu.get_barrier_semaphore()
+    partners = [flip["x"], flip["y"], flip["c"], up(1), up(2), up(3)]
+    partners += [{"z": lax.rem(z + d, z_count), "x": 1 - x} for d in range(1, 4)]
+    for device in partners:
+        pl.semaphore_signal(
+            barrier, inc=1, device_id=device, device_id_type=pl.DeviceIdType.MESH
+        )
+    keep = pltpu.make_async_copy(leaving_ref, all_ref.at[c, y, x, z], here.at[0])
+    keep_share = pltpu.make_async_copy(
+        sh_ref.at[2 * z + x], shared_ref.at[2 * z + x], here.at[1]
+    )
+    keep.start()
+    keep_share.start()
+    for i in range(z_count):
+        for j in range(2):
+            e = 2 * i + j
+            joined_ref[e * block : (e + 1) * block] = w_ref[i, j, :block]
+    bias = w_ref[z, 0, pl.ds(block, 16)].astype(jnp.float32) + w_ref[
+        z, 1, pl.ds(block, 16)
+    ].astype(jnp.float32)
+    bias = bias[0:1, : 3 * head]
+    lane = lax.broadcasted_iota(jnp.int32, (1, head), 1)
+    sign = jnp.where(lane < head // 2, -1.0, 1.0)
+    pl.semaphore_wait(barrier, 9)
+    for k in range(chunks):
+        start(spread_z(k))
+    shares = [share(d, other) for d in range(4) for other in (False, True) if d or other]
+
+    def project(t, carry):
+        lin = product(rows_ref[pl.ds(t * tile, tile), :], joined_ref[:, : 3 * head]) + bias
+        for h in range(2):
+            s = 2 * t + h
+            z_of, y_of, c_of = lax.rem(s, 4), lax.rem(s // 4, 2), s // 8
+            place = pl.ds(pl.multiple_of((z_of * 4 + y_of * 2 + c_of) * own, own), own)
+            block_cos, block_sin = block_ref[0, pl.ds(s, 1)], block_ref[1, pl.ds(s, 1)]
+            cosine = block_cos * row_ref[0] - block_sin * row_ref[1]
+            sine = (block_sin * row_ref[0] + block_cos * row_ref[1]) * sign
+            part = lin[h * own : (h + 1) * own]
+            query, key = part[:, :head], part[:, head : 2 * head]
+            query = query * cosine + pltpu.roll(query, head // 2, 1) * sine
+            key = key * cosine + pltpu.roll(key, head // 2, 1) * sine
+            q_ref[place, :] = query.astype(jnp.bfloat16)
+            kv_ref[0, place, :head] = key.astype(jnp.bfloat16)
+            kv_ref[0, place, head:] = part[:, 2 * head :].astype(jnp.bfloat16)
+        return carry
+
+    lax.fori_loop(0, count // tile, project, 0)
+    key_values().start()
+    start(shares)
+    keep.wait()
+    finish(spread_z(0))
+    start(spread_2(0))
+    column = lax.broadcasted_iota(jnp.int32, (tile, rows), 1)
+
+    def scan(i, side, blocks, carry):
+        query = q_ref[pl.ds(pl.multiple_of(i * tile, tile), tile), :]
+        base = (2 * (i // 2) + x) * rows + lax.rem(i, 2) * tile
+        row_pos = base + lax.broadcasted_iota(jnp.int32, (tile, 1), 0)
+        limit = jnp.minimum(row_pos, length_ref[0] - 1)
+        parity = x if side == 0 else 1 - x
+
+        def body(m, carry):
+            peak, total, acc = carry
+            window = pl.ds(pl.multiple_of(m * rows, rows), rows)
+            scores = product_bt(query, kv_ref[side, window, :head]) * (1.0 / head**0.5)
+            scores = jnp.where(column <= limit - (2 * m + parity) * rows, scores, MASKED)
+            new_peak = jnp.maximum(peak, jnp.max(scores, axis=1, keepdims=True))
+            weights = jnp.exp(scores - new_peak)
+            shrink = jnp.exp(peak - new_peak)
+            total = shrink * total + jnp.sum(weights, axis=1, keepdims=True)
+            acc = shrink * acc + product(
+                weights.astype(jnp.bfloat16), kv_ref[side, window, head:]
+            )
+            return (new_peak, total, acc)
+
+        return lax.fori_loop(0, blocks, body, carry)
+
+    def first_pass(i, carry):
+        peak, total, acc = scan(
+            i,
+            0,
+            i // 2 + 1,
+            (
+                jnp.full((tile, 1), MASKED, jnp.float32),
+                jnp.zeros((tile, 1), jnp.float32),
+                jnp.zeros((tile, head), jnp.float32),
+            ),
+        )
+        place = pl.ds(pl.multiple_of(i * tile, tile), tile)
+        peaks[place, :] = jnp.broadcast_to(peak, (tile, head))
+        totals[place, :] = jnp.broadcast_to(total, (tile, head))
+        att_ref[place, :] = acc
+        return carry
+
+    lax.fori_loop(0, count // tile, first_pass, 0)
+    finish(spread_z(1))
+    start(spread_2(1))
+    key_values().wait()
+
+    def second_pass(i, carry):
+        place = pl.ds(pl.multiple_of(i * tile, tile), tile)
+        peak, total, acc = scan(
+            i, 1, i // 2 + x, (peaks[place, 0:1], totals[place, 0:1], att_ref[place, :])
+        )
+        acc = acc / total
+        att_ref[place, :] = acc
+        lse_ref[place, :] = jnp.broadcast_to(peak + jnp.log(total), (tile, head))
+        part = product_bt(acc.astype(jnp.bfloat16), joined_ref[:, 3 * head :]).astype(
+            jnp.bfloat16
+        )
+        for h in range(2):
+            z_of, y_of, c_of = i // 2, lax.rem(i, 2), h
+            part_ref[c_of * 8 + y_of * 4 + z_of] = part[h * own : (h + 1) * own]
+        return carry
+
+    lax.fori_loop(0, count // tile, second_pass, 0)
+    finish(spread_2(0))
+    start(spread_3(0))
+    for k in range(2, chunks):
+        finish(spread_z(k))
+        start(spread_2(k))
+        finish(spread_2(k - 1))
+        start(spread_3(k - 1))
+        finish(spread_3(k - 2))
+        start(spread_c(k - 2))
+    finish(spread_2(chunks - 1))
+    start(spread_3(chunks - 1))
+    for k in (chunks - 2, chunks - 1):
+        finish(spread_3(k))
+        start(spread_c(k))
+    for k in range(chunks):
+        finish(spread_c(k))
+    finish(shares)
+    keep_share.wait()
+
+
+def middle(length, gathered, weights, row_table, block_table, leaving, shared, rows, chunks=4):
+    own, wide = leaving.shape
+    count, model = gathered.shape
+    zs = lax.axis_size("z")
+    head = HEAD_DIM
+    piece = own // chunks
+    bf16, f32 = jnp.bfloat16, jnp.float32
+    anywhere = pl.BlockSpec(memory_space=pl.ANY)
+    inside = pl.BlockSpec(memory_space=pltpu.VMEM)
+    vm, dma = pltpu.VMEM, pltpu.SemaphoreType.DMA
+    shape = jax.ShapeDtypeStruct
+    results = pl.pallas_call(
+        functools.partial(middle_kernel, rows=rows),
+        in_specs=[pl.BlockSpec(memory_space=pltpu.SMEM)] + [inside] * 4 + [anywhere] * 2,
+        out_specs=[inside] * 6 + [anywhere] * 2,
+        out_shape=[
+            shape((count, head), bf16),
+            shape((2, count, 2 * head), bf16),
+            shape((count, head), f32),
+            shape((count, head), f32),
+            shape((count // own, own, model), bf16),
+            shape((model, 4 * head), bf16),
+            shape((2, 2, 2, zs, chunks, piece, wide), bf16),
+            shape(shared.shape, bf16),
+        ],
+        scratch_shapes=[
+            vm((count, head), f32),
+            vm((count, head), f32),
+            dma((8, chunks)),
+            dma((8, chunks)),
+            dma((8,)),
+            dma((8,)),
+            dma((2,)),
+        ],
+        compiler_params=pltpu.CompilerParams(
+            collective_id=3, has_side_effects=True, vmem_limit_bytes=56 * 2**20
+        ),
+        cost_estimate=pl.CostEstimate(
+            flops=10 * count * model * head, bytes_accessed=60 * 2**20, transcendentals=count * count
+        ),
+    )(
+        length,
+        gathered,
+        weights,
+        row_table,
+        block_table,
+        leaving.reshape(chunks, piece, wide),
+        shared,
+    )
+    query, key_values, attended, log_total, partial, joined, spread, shared = results
+    return (
+        query,
+        key_values,
+        attended,
+        log_total,
+        partial.reshape(count, model),
+        joined,
+        spread.reshape(8 * zs * own, wide),
+        shared,
+    )
+
+
+def expert_rows(first, normed, grads, routes, w_ref, d_ref, s_ref, units, experts):
+    width = d_ref.shape[0]
+    rows = normed.shape[0]
+    pre = product_bt(normed, w_ref[...])
+    gate_pre = pre[:, :width]
+    up_pre = pre[:, width:]
+    lane = lax.broadcasted_iota(jnp.int32, (rows, 128), 1)
+    router_lane = lane - (128 - experts)
+    logits = jnp.where(router_lane >= 0, gate_pre[:, width - 128 :], MASKED)
+    expo = jnp.exp(logits - jnp.max(logits, axis=1, keepdims=True))
+    probs = expo / jnp.sum(expo, axis=1, keepdims=True)
+
+    def gate_of(expert):
+        picked = jnp.sum((routes == expert).astype(jnp.float32), axis=1, keepdims=True)
+        return picked * jnp.sum(
+            jnp.where(router_lane == expert, probs, 0.0), axis=1, keepdims=True
+        )
+
+    share = jax.nn.sigmoid(
+        jnp.sum(jnp.where(router_lane == 0, up_pre[:, width - 128 :], 0.0), axis=1, keepdims=True)
+    )
+    column = lax.broadcasted_iota(jnp.int32, (rows, width), 1)
+    scale = jnp.where(column < width - experts, share, 0.0)
+    for index in reversed(range(2)):
+        scale = jnp.where(column < (index + 1) * units, gate_of(first + index), scale)
+    sigma = jax.nn.sigmoid(gate_pre)
+    swish = gate_pre * sigma
+    hidden = swish * up_pre
+    scaled = (hidden * scale).astype(jnp.bfloat16)
+    mixture = product(scaled, d_ref[...]).astype(jnp.bfloat16)
+    back = product_bt(grads, d_ref[...])
+    gate_sums = product((back * hidden).astype(jnp.bfloat16), s_ref[...]).astype(jnp.bfloat16)
+    back = back * scale
+    grad_gate = (back * up_pre * (sigma * (1.0 + gate_pre * (1.0 - sigma)))).astype(jnp.bfloat16)
+    grad_up = (back * swish).astype(jnp.bfloat16)
+    pushed = product(grad_gate, w_ref[:width]) + product(grad_up, w_ref[width:])
+    return scaled, grad_gate, grad_up, mixture, pushed.astype(jnp.bfloat16), gate_sums
+
+
+def add_low(*terms):
+    total = terms[0].astype(jnp.float32)
+    for term in terms[1:]:
+        total = total + term.astype(jnp.float32)
+    return total.astype(jnp.bfloat16)
+
+
+def stream_kernel(
+    part_ref,
+    x_ref,
+    gain_ref,
+    g_ref,
+    eg_ref,
+    eu_ref,
+    ed_ref,
+    sh_ref,
+    router_ref,
+    s_ref,
+    all_ref,
+    hs_ref,
+    dgu_ref,
+    out_ref,
+    hidden_ref,
+    own_ref,
+    lrc_ref,
+    lr2_ref,
+    lr3_ref,
+    lca_ref,
+    lcb_ref,
+    l2a_ref,
+    l2b_ref,
+    l3a_ref,
+    l3b_ref,
+    lza_ref,
+    lzb_ref,
+    w_ref,
+    d_ref,
+    n_buf,
+    g_buf,
+    pa,
+    pb,
+    ca,
+    cb,
+    da,
+    db,
+    ea,
+    eb,
+    fa,
+    fb,
+    qa,
+    qb,
+    sa,
+    sb,
+    ta,
+    tb,
+    hs_buf,
+    dgu_buf,
+    ra,
+    rb,
+    rc,
+    rd,
+    re,
+    rf,
+    send,
+    send_z,
+    send_r,
+    recv,
+    here,
+    weigh,
+    *,
+    units,
+    experts,
+):
+    z, x, y, c = (lax.axis_index(name) for name in ALL_AXES)
+    z_count = lax.axis_size("z")
+    chunks = x_ref.shape[0]
+    model = x_ref.shape[2]
+    width = d_ref.shape[0]
+    cut = pa.shape[-1]
+    half = model // 2
+    left, right = pl.ds(0, half), pl.ds(half, half)
+    first = 2 * (2 * z + x)
+    flip = {"x": {"x": 1 - x}, "y": {"y": 1 - y}, "c": {"c": 1 - c}}
+
+    def up(distance):
+        return {"z": lax.rem(z + distance, z_count)}
+
+    def remote(slot, k, src, dst, device):
+        return pltpu.make_async_remote_copy(
+            src_ref=src,
+            dst_ref=dst,
+            send_sem=send.at[slot, lax.rem(k, 2)],
+            recv_sem=recv.at[slot, k],
+            device_id=device,
+            device_id_type=pl.DeviceIdType.MESH,
+        )
+
+    def spread_z(k, d):
+        return pltpu.make_async_remote_copy(
+            src_ref=own_ref.at[k],
+            dst_ref=all_ref.at[c, y, x, z, k],
+            send_sem=send_z.at[d - 1, k],
+            recv_sem=recv.at[20 + d, k],
+            device_id=up(d),
+            device_id_type=pl.DeviceIdType.MESH,
+        )
+
+    def heads_c(k):
+        return pltpu.make_async_remote_copy(
+            src_ref=part_ref.at[1 - c, :, :, k],
+            dst_ref=lrc_ref.at[k],
+            send_sem=send_r.at[k],
+            recv_sem=recv.at[24, k],
+            device_id=flip["c"],
+            device_id_type=pl.DeviceIdType.MESH,
+        )
+
+    def heads_y(k):
+        return (remote(17, k, rc.at[lax.rem(k, 2), 1 - y], lr2_ref.at[k], flip["y"]),)
+
+    def heads_z(k):
+        copies = []
+        for d in range(1, 4):
+            there = lax.rem(z + d, z_count)
+            copies.append(remote(17 + d, k, re.at[lax.rem(k, 2), there], lr3_ref.at[k, d - 1], up(d)))
+        return copies
+
+    def load_hc(k):
+        return (
+            pltpu.make_async_copy(part_ref.at[c, :, :, k], ra, here.at[15]),
+            pltpu.make_async_copy(lrc_ref.at[k], rb, here.at[16]),
+        )
+
+    def load_hy(k):
+        return (pltpu.make_async_copy(lr2_ref.at[k], rd, here.at[17]),)
+
+    def load_hz(k):
+        return (pltpu.make_async_copy(lr3_ref.at[k], rf, here.at[18]),)
+
+    def keep(k):
+        return pltpu.make_async_copy(own_ref.at[k], all_ref.at[c, y, x, z, k], here.at[19 + lax.rem(k, 2)])
+
+    def spread_2(k):
+        a = all_ref.at[c, y, x, :, k, :, left]
+        b = all_ref.at[c, y, x, :, k, :, right]
+        return remote(0, k, a, a, flip["x"]), remote(1, k, b, b, flip["y"])
+
+    def spread_3(k):
+        a = all_ref.at[c, y, :, :, k, :, left]
+        b = all_ref.at[c, :, x, :, k, :, right]
+        return remote(2, k, a, a, flip["y"]), remote(3, k, b, b, flip["x"])
+
+    def spread_c(k):
+        a = all_ref.at[c, :, :, :, k]
+        return (remote(4, k, a, a, flip["c"]),)
+
+    def sum_c(k):
+        slot = lax.rem(k, 2)
+        return (
+            remote(5, k, pa.at[slot, 1 - c], lca_ref.at[k], flip["c"]),
+            remote(6, k, pb.at[slot, 1 - c], lcb_ref.at[k], flip["c"]),
+        )
+
+    def sum_2(k):
+        return (
+            remote(7, k, qa.at[lax.rem(k, 2), 1 - y], l2a_ref.at[k], flip["y"]),
+            remote(8, k, qb.at[lax.rem(k, 2), :, 1 - x], l2b_ref.at[k], flip["x"]),
+        )
+
+    def sum_3(k):
+        return (
+            remote(9, k, sa.at[lax.rem(k, 2), 1 - x], l3a_ref.at[k], flip["x"]),
+            remote(10, k, sb.at[lax.rem(k, 2), 1 - y], l3b_ref.at[k], flip["y"]),
+        )
+
+    def sum_z(k):
+        copies = []
+        for d in range(1, 4):
+            there = lax.rem(z + d, z_count)
+            copies.append(remote(10 + d, k, ta.at[lax.rem(k, 2), there], lza_ref.at[k, d - 1], up(d)))
+            copies.append(remote(13 + d, k, tb.at[lax.rem(k, 2), there], lzb_ref.at[k, d - 1], up(d)))
+        return copies
+
+    def load_rows(k):
+        slot = lax.rem(k, 2)
+        return (
+            pltpu.make_async_copy(all_ref.at[:, :, :, :, k], n_buf.at[slot], here.at[slot]),
+            pltpu.make_async_copy(g_ref.at[:, :, :, :, k], g_buf.at[slot], here.at[13 + slot]),
+        )
+
+    def load_c(k):
+        return (
+            pltpu.make_async_copy(lca_ref.at[k], ca, here.at[2]),
+            pltpu.make_async_copy(lcb_ref.at[k], cb, here.at[3]),
+        )
+
+    def load_2(k):
+        return (
+            pltpu.make_async_copy(l2a_ref.at[k], da, here.at[4]),
+            pltpu.make_async_copy(l2b_ref.at[k], db, here.at[5]),
+        )
+
+    def load_3(k):
+        return (
+            pltpu.make_async_copy(l3a_ref.at[k], ea, here.at[6]),
+            pltpu.make_async_copy(l3b_ref.at[k], eb, here.at[7]),
+        )
+
+    def load_z(k):
+        return (
+            pltpu.make_async_copy(lza_ref.at[k], fa, here.at[8]),
+            pltpu.make_async_copy(lzb_ref.at[k], fb, here.at[9]),
+        )
+
+    def store_rows(k):
+        return (
+            pltpu.make_async_copy(hs_buf, hs_ref.at[:, :, :, :, k], here.at[10]),
+            pltpu.make_async_copy(dgu_buf, dgu_ref.at[:, :, :, :, k], here.at[11]),
+        )
+
+    def start(copies):
+        for copy in copies:
+            copy.start()
+
+    def finish(copies):
+        for copy in copies:
+            copy.wait()
+
+    def at(k, body):
+        pl.when((k >= 0) & (k < chunks))(lambda: body(k))
+
+    barrier = pltpu.get_barrier_semaphore()
+    for device in (flip["x"], flip["y"], flip["c"], up(1), up(2), up(3)):
+        pl.semaphore_signal(
+            barrier, inc=1, device_id=device, device_id_type=pl.DeviceIdType.MESH
+        )
+    pl.semaphore_wait(barrier, 6)
+
+    def first_sends(k, carry):
+        heads_c(k).start()
+        return carry
+
+    lax.fori_loop(0, chunks, first_sends, 0)
+    routed, share = eg_ref.shape[0], sh_ref.shape[1] // 3
+    low = pl.ds(routed, share)
+    high = pl.ds(width + routed, share)
+
+    def weight_copies():
+        pairs = [
+            (eg_ref, w_ref.at[pl.ds(0, routed)]),
+            (eu_ref, w_ref.at[pl.ds(width, routed)]),
+            (ed_ref, d_ref.at[pl.ds(0, routed)]),
+            (router_ref.at[0], w_ref.at[pl.ds(width - experts, experts)]),
+            (router_ref.at[1], w_ref.at[pl.ds(2 * width - experts, experts)]),
+        ]
+        cells = model // sh_ref.shape[0]
+        for e in range(sh_ref.shape[0]):
+            columns = pl.ds(e * cells, cells)
+            pairs.append((sh_ref.at[e, pl.ds(0, share)], w_ref.at[low, columns]))
+            pairs.append((sh_ref.at[e, pl.ds(share, share)], w_ref.at[high, columns]))
+            pairs.append((sh_ref.at[e, pl.ds(2 * share, share)], d_ref.at[low, columns]))
+        return [
+            pltpu.make_async_copy(src, dst, weigh.at[i]) for i, (src, dst) in enumerate(pairs)
+        ]
+
+    start(weight_copies())
+    d_ref[pl.ds(width - experts, experts), :] = jnp.zeros((experts, model), jnp.bfloat16)
+
+    def arrive_hc(k):
+        heads_c(k).wait()
+        start(load_hc(k))
+
+    def arrive_hy(k):
+        finish(heads_y(k))
+        start(load_hy(k))
+
+    def arrive_hz(k):
+        finish(heads_z(k))
+        start(load_hz(k))
+
+    def close_hc(k):
+        finish(load_hc(k))
+        slot = lax.rem(k, 2)
+
+        def each(i, carry):
+            for j in range(2):
+                rc[slot, j, i] = add_low(ra[j, i], rb[j, i])
+            return carry
+
+        lax.fori_loop(0, z_count, each, 0)
+        start(heads_y(k))
+
+    def close_hy(k):
+        finish(load_hy(k))
+        slot = lax.rem(k, 2)
+        for i in range(4):
+            re[slot, i] = add_low(rc[slot, y, i], rd[i])
+        start(heads_z(k))
+
+    def close_hz(k):
+        finish(load_hz(k))
+        total = re[lax.rem(k, 2), z].astype(jnp.float32)
+        for d in range(3):
+            total = total + rf[d].astype(jnp.float32)
+        hidden = x_ref[k].astype(jnp.float32) + total
+        inverse = lax.rsqrt(jnp.mean(hidden * hidden, axis=1, keepdims=True) + EPSILON)
+        hidden_ref[k] = hidden
+        own_ref[k] = (hidden * inverse * gain_ref[...]).astype(jnp.bfloat16)
+        keep(k).start()
+        for d in range(1, 4):
+            spread_z(k, d).start()
+
+    def gather_2(k):
+        keep(k).wait()
+        for d in range(1, 4):
+            spread_z(k, d).wait()
+        start(spread_2(k))
+
+    def gather_3(k):
+        finish(spread_2(k))
+        start(spread_3(k))
+
+    def gather_c(k):
+        finish(spread_3(k))
+        start(spread_c(k))
+
+    def gathered(k):
+        finish(spread_c(k))
+        start(load_rows(k))
+
+    def work(k, part):
+        slot = lax.rem(k, 2)
+        rows = 256
+        normed = n_buf[slot, part].reshape(rows, model)
+        grads = g_buf[slot, part].reshape(rows, model + 128)
+        routes = grads[:, model : model + 128].astype(jnp.int32)
+        grads = grads[:, :model]
+        scaled, grad_gate, grad_up, mixture, pushed, gate_sums = expert_rows(
+            first, normed, grads, routes, w_ref, d_ref, s_ref, units, experts
+        )
+        shape = (2, 2, z_count, 16)
+        hs_buf[part] = scaled.reshape(shape + (width,))
+        dgu_buf[part, :, :, :, :, :width] = grad_gate.reshape(shape + (width,))
+        dgu_buf[part, :, :, :, :, width:] = grad_up.reshape(shape + (width,))
+        pa[slot, part] = mixture[:, :cut].reshape(shape + (cut,))
+        rest = model - cut
+        pb[slot, part, :, :, :, :, :rest] = mixture[:, cut:].reshape(shape + (rest,))
+        pb[slot, part, :, :, :, :, rest : rest + model] = pushed.reshape(shape + (model,))
+        pb[slot, part, :, :, :, :, rest + model :] = gate_sums.reshape(shape + (128,))
+
+    def work_first(k):
+        finish(load_rows(k))
+        at(k - 1, lambda j: finish(store_rows(j)))
+        work(k, 0)
+
+    def work_second(k):
+        work(k, 1)
+        start(store_rows(k))
+
+    def arrive_c(k):
+        finish(sum_c(k))
+        start(load_c(k))
+
+    def arrive_2(k):
+        finish(sum_2(k))
+        start(load_2(k))
+
+    def arrive_3(k):
+        finish(sum_3(k))
+        start(load_3(k))
+
+    def arrive_z(k):
+        finish(sum_z(k))
+        start(load_z(k))
+
+    def close_z(k):
+        finish(load_z(k))
+        slot = lax.rem(k, 2)
+        own_a = ta[slot, z].astype(jnp.float32)
+        own_b = tb[slot, z].astype(jnp.float32)
+        for d in range(3):
+            own_a = own_a + fa[d].astype(jnp.float32)
+            own_b = own_b + fb[d].astype(jnp.float32)
+        out_ref[k, :, :cut] = own_a
+        out_ref[k, :, cut:] = own_b
+
+    def close_3(k):
+        finish(load_3(k))
+        slot = lax.rem(k, 2)
+
+        def each(i, carry):
+            ta[slot, i] = add_low(sa[slot, x, i], ea[i])
+            tb[slot, i] = add_low(sb[slot, y, i], eb[i])
+            return carry
+
+        lax.fori_loop(0, z_count, each, 0)
+        start(sum_z(k))
+
+    def close_2(k):
+        finish(load_2(k))
+        slot = lax.rem(k, 2)
+
+        def each(i, carry):
+            for j in range(2):
+                sa[slot, j, i] = add_low(qa[slot, y, j, i], da[j, i])
+                sb[slot, j, i] = add_low(qb[slot, j, x, i], db[j, i])
+            return carry
+
+        lax.fori_loop(0, z_count, each, 0)
+        start(sum_3(k))
+
+    def close_c(k):
+        finish(load_c(k))
+        slot = lax.rem(k, 2)
+
+        def each(i, carry):
+            for j in range(2):
+                for m in range(2):
+                    qa[slot, j, m, i] = add_low(pa[slot, c, j, m, i], ca[j, m, i])
+                    qb[slot, j, m, i] = add_low(pb[slot, c, j, m, i], cb[j, m, i])
+            return carry
+
+        lax.fori_loop(0, z_count, each, 0)
+        start(sum_2(k))
+
+    def tick(i, carry):
+        at(i - 11, gathered)
+        at(i - 10, gather_c)
+        at(i - 8, gather_3)
+        at(i - 6, gather_2)
+        pl.when(i == 12)(lambda: finish(weight_copies()))
+        at(i - 12, work_first)
+        at(i - 19, arrive_z)
+        at(i - 17, arrive_3)
+        at(i - 15, arrive_2)
+        at(i - 13, arrive_c)
+        at(i - 4, arrive_hz)
+        at(i - 2, arrive_hy)
+        at(i, arrive_hc)
+        at(i - 12, work_second)
+        at(i - 4, close_hz)
+        at(i - 2, close_hy)
+        at(i, close_hc)
+        at(i - 19, close_z)
+        at(i - 17, close_3)
+        at(i - 15, close_2)
+        at(i - 13, close_c)
+        at(i - 12, lambda k: start(sum_c(k)))
+        return carry
+
+    lax.fori_loop(0, chunks + 19, tick, 0)
+    finish(store_rows(chunks - 1))
+
+
+def stream(
+    partial, tokens, gain, grads, gates, ups, downs, shared, router, segments, units, experts, chunks
+):
+    own, model = tokens.shape
+    width = segments.shape[0]
+    piece = own // chunks
+    zs = lax.axis_size("z")
+    lead = (2, 2, 2, zs)
+    partial = partial.reshape((2, 2, zs, chunks, piece, model))
+    grads = grads.reshape(lead + (chunks, piece, model + 128))
+    tokens = tokens.reshape(chunks, piece, model)
+    cut = model // 2
+    extra = 2 * model + 128 - cut
+    bf16 = jnp.bfloat16
+    shapes = [
+        (lead + (chunks, piece, model), bf16),
+        (lead + (chunks, piece, width), bf16),
+        (lead + (chunks, piece, 2 * width), bf16),
+        ((chunks, piece, 2 * model + 128), jnp.float32),
+        ((chunks, piece, model), jnp.float32),
+        ((chunks, piece, model), bf16),
+        ((chunks, 2, zs, piece, model), bf16),
+        ((chunks, zs, piece, model), bf16),
+        ((chunks, 3, piece, model), bf16),
+        ((chunks, 2, 2, zs, piece, cut), bf16),
+        ((chunks, 2, 2, zs, piece, extra), bf16),
+        ((chunks, 2, zs, piece, cut), bf16),
+        ((chunks, 2, zs, piece, extra), bf16),
+        ((chunks, zs, piece, cut), bf16),
+        ((chunks, zs, piece, extra), bf16),
+        ((chunks, 3, piece, cut), bf16),
+        ((chunks, 3, piece, extra), bf16),
+    ]
+    anywhere = pl.BlockSpec(memory_space=pl.ANY)
+    inside = pl.BlockSpec(memory_space=pltpu.VMEM)
+    vm = pltpu.VMEM
+    dma = pltpu.SemaphoreType.DMA
+    scratch = [
+        vm((2 * width, model), bf16),
+        vm((width, model), bf16),
+        vm((2,) + lead + (piece, model), bf16),
+        vm((2,) + lead + (piece, model + 128), bf16),
+        vm((2,) + lead + (piece, cut), bf16),
+        vm((2,) + lead + (piece, extra), bf16),
+        vm((2, 2, zs, piece, cut), bf16),
+        vm((2, 2, zs, piece, extra), bf16),
+        vm((2, zs, piece, cut), bf16),
+        vm((2, zs, piece, extra), bf16),
+        vm((zs, piece, cut), bf16),
+        vm((zs, piece, extra), bf16),
+        vm((3, piece, cut), bf16),
+        vm((3, piece, extra), bf16),
+        vm((2, 2, 2, zs, piece, cut), bf16),
+        vm((2, 2, 2, zs, piece, extra), bf16),
+        vm((2, 2, zs, piece, cut), bf16),
+        vm((2, 2, zs, piece, extra), bf16),
+        vm((2, zs, piece, cut), bf16),
+        vm((2, zs, piece, extra), bf16),
+        vm(lead + (piece, width), bf16),
+        vm(lead + (piece, 2 * width), bf16),
+        vm((2, zs, piece, model), bf16),
+        vm((2, zs, piece, model), bf16),
+        vm((2, 2, zs, piece, model), bf16),
+        vm((zs, piece, model), bf16),
+        vm((2, zs, piece, model), bf16),
+        vm((3, piece, model), bf16),
+        dma((21, 2)),
+        dma((3, chunks)),
+        dma((chunks,)),
+        dma((25, chunks)),
+        dma((21,)),
+        dma((5 + 3 * shared.shape[0],)),
+    ]
+    rows = own * 8 * zs
+    results = pl.pallas_call(
+        functools.partial(stream_kernel, units=units, experts=experts),
+        in_specs=[anywhere, inside, inside] + [anywhere] * 6 + [inside],
+        out_specs=[anywhere] * 3 + [inside] * 3 + [anywhere] * 11,
+        out_shape=[jax.ShapeDtypeStruct(s, t) for s, t in shapes],
+        scratch_shapes=scratch,
+        compiler_params=pltpu.CompilerParams(
+            collective_id=1, has_side_effects=True, vmem_limit_bytes=61 * 2**20
+        ),
+        cost_estimate=pl.CostEstimate(
+            flops=12 * rows * model * width,
+            bytes_accessed=rows * (14 * model + 6 * width),
+            transcendentals=rows * width,
+        ),
+    )(partial, tokens, gain, grads, gates, ups, downs, shared, router, segments)
+    gathered, scaled, slopes, sums, hidden, normed = results[:6]
+    return (
+        gathered.reshape(rows, model),
+        scaled.reshape(rows, width),
+        slopes.reshape(rows, 2 * width),
+        sums.reshape(own, 2 * model + 128),
+        hidden.reshape(own, model),
+        normed.reshape(own, model),
+    )
+
+
+def finish_kernel(
+    part_ref,
+    grads_ref,
+    x_ref,
+    wp_ref,
+    bp_ref,
+    w_ref,
+    e_ref,
+    rows_ref,
+    heads_ref,
+    bias_ref,
+    gain_ref,
+    square_ref,
+    extra_ref,
+    lc,
+    ly,
+    lz,
+    rc,
+    re,
+    gt,
+    wl,
+    bl,
+    ws,
+    gs,
+    gl,
+    ss,
+    sl,
+    ls,
+    ll,
+    lx,
+    lu,
+    lv,
+    send,
+    send_k,
+    recv,
+    once,
+    once_in,
+    here,
+):
+    z, x, y, c = (lax.axis_index(name) for name in ALL_AXES)
+    z_count = lax.axis_size("z")
+    chunks, _, model = x_ref.shape
+    head = HEAD_DIM
+    flip = {"x": {"x": 1 - x}, "y": {"y": 1 - y}, "c": {"c": 1 - c}}
+
+    def up(distance):
+        return {"z": lax.rem(z + distance, z_count)}
+
+    def copy_to(src, dst, send_sem, recv_sem, device):
+        return pltpu.make_async_remote_copy(
+            src_ref=src,
+            dst_ref=dst,
+            send_sem=send_sem,
+            recv_sem=recv_sem,
+            device_id=device,
+            device_id_type=pl.DeviceIdType.MESH,
+        )
+
+    def heads_c(k):
+        return copy_to(
+            part_ref.at[1 - c, :, :, k], lc.at[k], send_k.at[k], recv.at[0, k], flip["c"]
+        )
+
+    def heads_y(k):
+        return copy_to(rc.at[lax.rem(k, 2), 1 - y], ly.at[k], send.at[0, lax.rem(k, 2)], recv.at[1, k], flip["y"])
+
+    def heads_z(k, d):
+        there = lax.rem(z + d, z_count)
+        return copy_to(
+            re.at[lax.rem(k, 2), there], lz.at[k, d - 1], send.at[d, lax.rem(k, 2)], recv.at[1 + d, k], up(d)
+        )
+
+    def keep(k):
+        return pltpu.make_async_copy(gt.at[k], rows_ref.at[y, c, k], here.at[lax.rem(k, 2)])
+
+    def rows_y(k):
+        return copy_to(gt.at[k], rows_ref.at[y, c, k], send.at[4, lax.rem(k, 2)], recv.at[5, k], flip["y"])
+
+    def rows_c(k):
+        block = rows_ref.at[:, c, k]
+        return copy_to(block, block, send.at[5, lax.rem(k, 2)], recv.at[6, k], flip["c"])
+
+    def single(i, src, dst, device):
+        return copy_to(src, dst, once.at[i], once_in.at[i], device)
+
+    def weights_x():
+        return (
+            single(0, wp_ref.at[1 - x], wl, flip["x"]),
+            single(1, bp_ref.at[1 - x], bl, flip["x"]),
+        )
+
+    def weights_z(d):
+        return single(1 + d, ws.at[lax.rem(z + d, z_count)], heads_ref.at[z], up(d))
+
+    def at(k, body):
+        pl.when((k >= 0) & (k < chunks))(lambda: body(k))
+
+    barrier = pltpu.get_barrier_semaphore()
+    for device in (flip["x"], flip["y"], flip["c"], up(1), up(2), up(3)):
+        pl.semaphore_signal(
+            barrier, inc=1, device_id=device, device_id_type=pl.DeviceIdType.MESH
+        )
+    square_ref[...] = jnp.zeros_like(square_ref)
+    pl.semaphore_wait(barrier, 6)
+
+    def first_sends(k, carry):
+        heads_c(k).start()
+        return carry
+
+    lax.fori_loop(0, chunks, first_sends, 0)
+    for copy in weights_x():
+        copy.start()
+
+    def close_c(k):
+        heads_c(k).wait()
+        slot = lax.rem(k, 2)
+
+        def each(i, carry):
+            for j in range(2):
+                rc[slot, j, i] = add_low(part_ref[c, j, i, k], lc[k, j, i])
+            return carry
+
+        lax.fori_loop(0, z_count, each, 0)
+        heads_y(k).start()
+
+    def close_y(k):
+        heads_y(k).wait()
+        slot = lax.rem(k, 2)
+        for i in range(4):
+            re[slot, i] = add_low(rc[slot, y, i], ly[k, i])
+        for d in range(1, 4):
+            heads_z(k, d).start()
+
+    def close_z(k):
+        for d in range(1, 4):
+            heads_z(k, d).wait()
+        pushed = re[lax.rem(k, 2), z].astype(jnp.float32)
+        for d in range(3):
+            pushed = pushed + lz[k, d].astype(jnp.float32)
+        values = x_ref[k].astype(jnp.float32)
+        inverse = lax.rsqrt(jnp.mean(values * values, axis=1, keepdims=True) + EPSILON)
+        scaled = values * inverse
+        total = grads_ref[k] + inverse * (
+            pushed - scaled * jnp.mean(pushed * scaled, axis=1, keepdims=True)
+        )
+        gt[k] = total.astype(jnp.bfloat16)
+        squares = total * total
+        squares = squares[:8] + squares[8:]
+        lanes = squares[:, :128]
+        for j in range(1, model // 128):
+            lanes = lanes + squares[:, j * 128 : (j + 1) * 128]
+        square_ref[...] += lanes
+        keep(k).start()
+        rows_y(k).start()
+
+    def close_rows(k):
+        keep(k).wait()
+        rows_y(k).wait()
+        rows_c(k).start()
+
+    def close_all(k):
+        rows_c(k).wait()
+
+    def weights_sum():
+        for copy in weights_x():
+            copy.wait()
+        bias_ref[...] = bp_ref[x].astype(jnp.float32) + bl[...].astype(jnp.float32)
+
+        def each(i, carry):
+            ws[i] = add_low(wp_ref[x, i], wl[i])
+            return carry
+
+        lax.fori_loop(0, z_count, each, 0)
+        heads_ref[z] = ws[z]
+        for d in range(1, 4):
+            weights_z(d).start()
+
+    def extra_c():
+        return single(13, e_ref, ll.at[0], flip["c"])
+
+    def extra_y():
+        return single(14, ls, ll.at[1], flip["y"])
+
+    def extra_x():
+        return single(15, lx.at[1 - x], lu, flip["x"])
+
+    def extra_z(d):
+        return single(15 + d, lx.at[x, lax.rem(z + d, z_count)], lv.at[d - 1], up(d))
+
+    def extra_sum_c():
+        extra_c().wait()
+        ls[...] = e_ref[...] + ll[0]
+        extra_y().start()
+
+    def extra_sum_y():
+        extra_y().wait()
+        lx[...] = ls[...] + ll[1]
+        extra_x().start()
+
+    def extra_sum_x():
+        extra_x().wait()
+        lx[x] = lx[x] + lu[...]
+        for d in range(1, 4):
+            extra_z(d).start()
+
+    extra_c().start()
+
+    def tick(i, carry):
+        at(i - 7, close_all)
+        at(i - 6, close_rows)
+        at(i - 4, close_z)
+        at(i - 2, close_y)
+        at(i, close_c)
+        pl.when(i == 2)(weights_sum)
+        pl.when(i == 2)(extra_sum_c)
+        pl.when(i == 4)(extra_sum_y)
+        pl.when(i == 6)(extra_sum_x)
+        return carry
+
+    lax.fori_loop(0, chunks + 7, tick, 0)
+    for d in range(1, 4):
+        extra_z(d).wait()
+    extra_ref[...] = lx[x, z] + lv[0] + lv[1] + lv[2]
+    ss[0] = square_ref[...]
+    squares_c = single(5, ss.at[0], sl.at[0], flip["c"])
+    squares_c.start()
+    for d in range(1, 4):
+        weights_z(d).wait()
+    total = jnp.zeros(gain_ref.shape, jnp.float32)
+    for i in range(4):
+        for j in range(3):
+            columns = slice(j * head, (j + 1) * head)
+            total = total + w_ref[i, :, columns].astype(jnp.float32) * heads_ref[
+                i, :, columns
+            ].astype(jnp.float32)
+    gs[0] = total
+    gain_y = single(6, gs.at[0], gl.at[0], flip["y"])
+    gain_y.start()
+    squares_c.wait()
+    ss[1] = ss[0] + sl[0]
+    squares_y = single(7, ss.at[1], sl.at[1], flip["y"])
+    squares_y.start()
+    gain_y.wait()
+    gs[1] = gs[0] + gl[0]
+    gain_c = single(8, gs.at[1], gl.at[1], flip["c"])
+    gain_c.start()
+    squares_y.wait()
+    ss[2] = ss[1] + sl[1]
+    squares_x = single(9, ss.at[2], sl.at[2], flip["x"])
+    squares_x.start()
+    squares_x.wait()
+    ss[3] = ss[2] + sl[2]
+    squares_z = [single(9 + d, ss.at[3], sl.at[2 + d], up(d)) for d in range(1, 4)]
+    for copy in squares_z:
+        copy.start()
+    gain_c.wait()
+    gain_ref[...] = gs[1] + gl[1]
+    for copy in squares_z:
+        copy.wait()
+    square_ref[...] = ss[3] + sl[3] + sl[4] + sl[5]
+
+
+def finish(partial, grads, tokens, weight_parts, bias_parts, weights, extras, chunks):
+    own, model = tokens.shape
+    piece = own // chunks
+    zs = lax.axis_size("z")
+    bf16, f32 = jnp.bfloat16, jnp.float32
+    block, wide = weight_parts.shape[2:]
+    anywhere = pl.BlockSpec(memory_space=pl.ANY)
+    inside = pl.BlockSpec(memory_space=pltpu.VMEM)
+    vm = pltpu.VMEM
+    dma = pltpu.SemaphoreType.DMA
+    rows, heads, bias, gain, square, extra = pl.pallas_call(
+        finish_kernel,
+        in_specs=[inside] * 7,
+        out_specs=[anywhere] + [inside] * 5,
+        out_shape=[
+            jax.ShapeDtypeStruct((2, 2, chunks, piece, model), bf16),
+            jax.ShapeDtypeStruct((zs, block, wide), bf16),
+            jax.ShapeDtypeStruct(bias_parts.shape[1:], f32),
+            jax.ShapeDtypeStruct((block, 128), f32),
+            jax.ShapeDtypeStruct((8, 128), f32),
+            jax.ShapeDtypeStruct(extras.shape[2:], f32),
+        ],
+        scratch_shapes=[
+            vm((chunks, 2, zs, piece, model), bf16),
+            vm((chunks, zs, piece, model), bf16),
+            vm((chunks, 3, piece, model), bf16),
+            vm((2, 2, zs, piece, model), bf16),
+            vm((2, zs, piece, model), bf16),
+            vm((chunks, piece, model), bf16),
+            vm((zs, block, wide), bf16),
+            vm(bias_parts.shape[1:], bf16),
+            vm((zs, block, wide), bf16),
+            vm((2, block, 128), f32),
+            vm((2, block, 128), f32),
+            vm((4, 8, 128), f32),
+            vm((6, 8, 128), f32),
+            vm(extras.shape, f32),
+            vm((2,) + extras.shape, f32),
+            vm(extras.shape, f32),
+            vm(extras.shape[1:], f32),
+            vm((3,) + extras.shape[2:], f32),
+            dma((6, 2)),
+            dma((chunks,)),
+            dma((7, chunks)),
+            dma((19,)),
+            dma((19,)),
+            dma((2,)),
+        ],
+        compiler_params=pltpu.CompilerParams(
+            collective_id=2, has_side_effects=True, vmem_limit_bytes=48 * 2**20
+        ),
+        cost_estimate=pl.CostEstimate(
+            flops=100 * own * model, bytes_accessed=40 * 2**20, transcendentals=0
+        ),
+    )(
+        partial.reshape(2, 2, zs, chunks, piece, model),
+        grads.reshape(chunks, piece, model),
+        tokens.reshape(chunks, piece, model),
+        weight_parts,
+        bias_parts,
+        weights,
+        extras,
+    )
+    return rows.reshape(4 * own, model), heads, bias, gain, square, extra
+
+
+def weight_grads_kernel(
+    n_ref, g_ref, slopes_ref, scaled_ref, gate_ref, up_ref, down_ref, sh_ref, *, units, share
+):
+    width = scaled_ref.shape[1]
+    low = 2 * units
+    first = product_at(n_ref[...], slopes_ref[...]).T
+    second = product_at(g_ref[...], scaled_ref[...]).T
+    for ref, rows in ((gate_ref, first[:width]), (up_ref, first[width:]), (down_ref, second)):
+        for i in range(2):
+            ref[i] = rows[i * units : (i + 1) * units]
+    for i, rows in enumerate((first[:width], first[width:], second)):
+        sh_ref[0, i * share : (i + 1) * share] = rows[low : low + share].astype(jnp.bfloat16)
+
+
+def weight_grads(normed, grads, slopes, scaled, units, share, blocks):
+    count, model = normed.shape
+    width = scaled.shape[1]
+    block = model // blocks
+    one = pl.Buffered(1)
+    f32, bf16 = jnp.float32, jnp.bfloat16
+    rows = pl.BlockSpec((2, units, block), lambda i: (0, 0, i))
+    return pl.pallas_call(
+        functools.partial(weight_grads_kernel, units=units, share=share),
+        grid=(blocks,),
+        in_specs=[
+            pl.BlockSpec((count, block), lambda i: (0, i)),
+            pl.BlockSpec((count, block), lambda i: (0, i)),
+            pl.BlockSpec(slopes.shape, lambda i: (0, 0), pipeline_mode=one),
+            pl.BlockSpec(scaled.shape, lambda i: (0, 0), pipeline_mode=one),
+        ],
+        out_specs=[rows, rows, rows, pl.BlockSpec((1, 3 * share, block), lambda i: (i, 0, 0))],
+        out_shape=[jax.ShapeDtypeStruct((2, units, model), f32)] * 3
+        + [jax.ShapeDtypeStruct((blocks, 3 * share, block), bf16)],
+        compiler_params=pltpu.CompilerParams(vmem_limit_bytes=56 * 2**20),
+        cost_estimate=pl.CostEstimate(
+            flops=6 * count * model * width,
+            bytes_accessed=count * (4 * model + 6 * width) + 12 * model * width,
+            transcendentals=0,
+        ),
+    )(normed, grads, slopes, scaled)
+
+
+def packed(
+    tokens,
+    cotangent,
+    lengths,
+    routes,
+    w_query,
+    w_key,
+    w_value,
+    w_out,
+    b_query,
+    b_key,
+    b_value,
+    gain_attention,
+    gain_experts,
+    w_router,
+    w_shared_gate,
+    shared_gate,
+    shared_up,
+    shared_down,
+    expert_gate,
+    expert_up,
+    expert_down,
+    chunks=8,
+):
+    f32, bf16 = jnp.float32, jnp.bfloat16
+    heads_z = lax.axis_size("z")
+    exp_count = heads_z * lax.axis_size("x")
+    tp_count = lax.axis_size("y") * lax.axis_size("c")
+    z_index, x_index = lax.axis_index("z"), lax.axis_index("x")
+    exp_index = z_index * lax.axis_size("x") + x_index
+    tp_index = lax.axis_index("y") * lax.axis_size("c") + lax.axis_index("c")
+    rows, model = tokens.shape
+    total_rows = rows * exp_count
+    own = rows // tp_count
+    block = model // exp_count
+    local_experts, _, units = expert_gate.shape
+    experts = local_experts * exp_count
+    shared_units = shared_gate.shape[1] // exp_count
+    head = HEAD_DIM
+    length = lengths[0]
+
+    def my_rows(array):
+        return lax.dynamic_slice_in_dim(array, tp_index * own, own, 0)
+
+    own_tokens = my_rows(tokens).astype(f32)
+    normed_first = (own_tokens * norm_scale(own_tokens)).astype(bf16)
+    gain_rows = gain_attention.astype(f32)
+    attn_gain_own = gain_rows[:, None]
+    query_part, key_part, value_part = (
+        (w.astype(f32) * attn_gain_own).astype(bf16).reshape(block, heads_z, head)
+        for w in (w_query, w_key, w_value)
+    )
+    out_part = w_out.reshape(heads_z, head, block).transpose(2, 0, 1)
+    attn_parts = jnp.concatenate([query_part, key_part, value_part, out_part], axis=2)
+    half_dim = head // 2
+    side = x_index * half_dim
+    bias_row = jnp.zeros((3, head), bf16)
+    bias_row = lax.dynamic_update_slice(
+        bias_row, jnp.stack([b_query, b_key, b_value]), (jnp.zeros_like(side), side)
+    )
+    small = flat([gain_experts, w_router.T, w_shared_gate])
+    small = jnp.pad(small, (0, 15 * 4 * head - small.shape[0])).reshape(15, 4 * head)
+    small = jnp.concatenate([jnp.pad(bias_row.reshape(1, 3 * head), ((0, 0), (0, head))), small])
+    attn_parts = jnp.concatenate(
+        [
+            attn_parts.transpose(1, 0, 2),
+            jnp.broadcast_to(small[None], (heads_z, 16, 4 * head)),
+        ],
+        axis=1,
+    )
+    first_half, arrived_weights = front(normed_first, attn_parts)
+    small = arrived_weights[:, :, block + 1 :].reshape(exp_count, 15 * 4 * head)
+
+    own_first = exp_index * rows + tp_index * own
+    own_positions = own_first + jnp.arange(own, dtype=jnp.int32)
+    valid = (own_positions < length).astype(f32)[:, None]
+    grad_out_low = (my_rows(cotangent).astype(f32) * valid).astype(bf16)
+    own_routes = my_rows(routes)
+    leaving = jnp.concatenate(
+        [grad_out_low, jnp.pad(own_routes.astype(bf16), ((0, 0), (0, 124)), constant_values=-1.0)],
+        axis=1,
+    )
+    shared_parts = jnp.concatenate(
+        [
+            w.reshape(exp_count, shared_units, block)
+            for w in (shared_gate.T, shared_up.T, shared_down)
+        ],
+        axis=1,
+    )
+    place = 0
+    ffn_gain = small[:, place : place + block].reshape(model).astype(f32)
+    place += block
+    router_rows = (
+        small[:, place : place + block * experts]
+        .reshape(exp_count, experts, block)
+        .transpose(1, 0, 2)
+        .reshape(experts, model)
+    )
+    place += block * experts
+    share_vector = small[:, place : place + block].reshape(model)
+
+    frequency = ROPE_BASE ** (-(jnp.arange(half_dim, dtype=f32) * 2.0) / head)
+    row_angle = jnp.arange(own, dtype=f32)[:, None] * frequency[None, :]
+    places = (
+        jnp.arange(2)[:, None, None] * own
+        + jnp.arange(2)[None, :, None] * 2 * own
+        + (jnp.arange(heads_z)[None, None, :] * 2 + x_index) * rows
+    )
+    block_angle = places.reshape(-1).astype(f32)[:, None] * frequency[None, :]
+    row_cos, row_sin = jnp.cos(row_angle)[None], jnp.sin(row_angle)[None]
+    block_cos, block_sin = jnp.cos(block_angle)[:, None], jnp.sin(block_angle)[:, None]
+    cosine = (block_cos * row_cos - block_sin * row_sin).reshape(heads_z * rows, half_dim)
+    sine = (block_sin * row_cos + block_cos * row_sin).reshape(heads_z * rows, half_dim)
+
+    def rope_back(values):
+        one, two = values[:, :half_dim], values[:, half_dim:]
+        return jnp.concatenate([one * cosine + two * sine, two * cosine - one * sine], axis=1)
+
+    def by_position(array):
+        return (
+            array.reshape((2, 2, heads_z, own) + array.shape[1:])
+            .transpose(2, 1, 0, 3, 4)
+            .reshape(array.shape)
+        )
+
+    def by_owner(array):
+        return (
+            array.reshape((heads_z, 2, 2, own) + array.shape[1:])
+            .transpose(2, 1, 0, 3, 4)
+            .reshape(array.shape)
+        )
+
+    flip = [(0, 1), (1, 0)]
+    def twice(cos, sin):
+        return jnp.stack([jnp.tile(cos, (1, 2)), jnp.tile(sin, (1, 2))])
+
+    query_rot, key_values, attended, log_total, attn_part, attn_weights, grad_all, shared_parts = (
+        middle(
+            lengths,
+            first_half,
+            arrived_weights,
+            twice(row_cos[0], row_sin[0]),
+            twice(block_cos[:, 0], block_sin[:, 0]),
+            leaving,
+            shared_parts,
+            rows,
+        )
+    )
+    info = jnp.stack([x_index, length]).astype(jnp.int32)
+    attended_low = by_owner(attended.astype(bf16))
+    out_weight = attn_weights[:, 3 * head :]
+
+    width = local_experts * units + shared_units + experts
+    router_pair = jnp.stack(
+        [router_rows, jnp.pad(share_vector[None, :], ((0, experts - 1), (0, 0)))]
+    )
+    unit = jnp.arange(width, dtype=jnp.int32)
+    segment = jnp.where(
+        unit < local_experts * units, exp_index * local_experts + unit // units, experts
+    )
+    segments = (
+        (segment[:, None] == jnp.arange(128, dtype=jnp.int32)[None, :])
+        & (unit < width - experts)[:, None]
+    ).astype(bf16)
+    normed_all, scaled_all, slope_all, mixed_sum, hidden_state, normed = stream(
+        attn_part,
+        my_rows(tokens),
+        ffn_gain[None, :],
+        grad_all,
+        expert_gate.transpose(0, 2, 1).reshape(local_experts * units, model),
+        expert_up.transpose(0, 2, 1).reshape(local_experts * units, model),
+        expert_down.reshape(local_experts * units, model),
+        shared_parts,
+        router_pair,
+        segments,
+        units,
+        experts,
+        chunks,
+    )
+    inverse_second = norm_scale(hidden_state)
+    d_expert_gate, d_expert_up, d_expert_down, d_shared = weight_grads(
+        normed_all, grad_all, slope_all, scaled_all, units, shared_units, exp_count
+    )
+
+    output = valid * (hidden_state + mixed_sum[:, :model])
+    mixed = lax.all_gather(output.astype(bf16), COLUMN_AXES, axis=0, tiled=True)
+
+    router_probs = jax.nn.softmax(product_bt(normed, router_rows), axis=1)
+    share_weight = jax.nn.sigmoid(product(normed, share_vector))
+    chosen = jnp.sum(
+        (own_routes[:, :, None] == jnp.arange(experts, dtype=jnp.int32)[None, None, :]).astype(f32),
+        axis=1,
+    )
+    grad_router_probs = chosen * mixed_sum[:, 2 * model : 2 * model + experts]
+    grad_share_weight = mixed_sum[:, 2 * model + experts]
+    grad_logits = (
+        router_probs
+        * (grad_router_probs - jnp.sum(grad_router_probs * router_probs, axis=1, keepdims=True))
+    ).astype(bf16)
+    grad_share_logit = (grad_share_weight * share_weight * (1.0 - share_weight)).astype(bf16)
+    grad_normed = (
+        mixed_sum[:, model : 2 * model]
+        + product(grad_logits, router_rows)
+        + grad_share_logit.astype(f32)[:, None] * share_vector.astype(f32)[None, :]
+    )
+    norm_rows, d_gain_experts = norm_back(grad_normed, hidden_state, inverse_second, ffn_gain)
+    grad_hidden = grad_out_low.astype(f32) + norm_rows
+    hidden_half = lax.all_gather(grad_hidden.astype(bf16), SAME_X, axis=0, tiled=True)
+    router_grads = product_at(
+        jnp.concatenate([grad_logits, grad_share_logit[:, None]], axis=1), normed
+    )
+    extras = jnp.concatenate(
+        [
+            router_grads,
+            d_gain_experts[None, :],
+            jnp.broadcast_to(jnp.sum(output * output), (1, model)),
+            jnp.zeros((5, model), f32),
+        ]
+    )
+    extras = extras.reshape(-1, heads_z, 2, block).transpose(2, 1, 0, 3)
+    hidden_half, d_shared = lax.optimization_barrier((hidden_half, d_shared))
+    arrived = lax.all_to_all(d_shared, ROW_AXES, 0, 0, tiled=True).astype(f32)
+    d_shared_gate, d_shared_up, d_shared_down = (
+        arrived[:, k * shared_units : (k + 1) * shared_units].reshape(
+            exp_count * shared_units, block
+        )
+        for k in range(3)
+    )
+    d_shared_gate, d_shared_up = d_shared_gate.T, d_shared_up.T
+    grad_attended = product(hidden_half, out_weight).astype(bf16)
+    d_out_weight = product_at(hidden_half, attended_low)
+    scale = 1.0 / head**0.5
+    grad_query, grad_key, grad_value = attend_back(
+        info, query_rot, key_values, by_position(grad_attended), attended, log_total, rows
+    )
+    grad_kv = jnp.concatenate([grad_key, grad_value], axis=2).astype(bf16)
+    away = lax.ppermute(grad_kv[1], "x", flip)
+    grad_kv = by_owner(
+        jnp.concatenate([grad_key[0], grad_value[0]], axis=1) + away.astype(f32)
+    )
+    grad_qkv = jnp.concatenate(
+        [
+            rope_back(by_owner(grad_query)) * scale,
+            rope_back(grad_kv[:, :head]) * scale,
+            grad_kv[:, head:],
+        ],
+        axis=1,
+    ).astype(bf16)
+    d_attn = jnp.concatenate([product_at(first_half, grad_qkv), d_out_weight], axis=1).astype(bf16)
+    d_biases = jnp.sum(grad_qkv.astype(f32), axis=0).astype(bf16).reshape(3, 2, head // 2)
+    d_biases = jnp.pad(
+        d_biases.transpose(1, 0, 2).reshape(2, 1, 3 * head // 2),
+        ((0, 0), (0, 15), (0, 4 * head - 3 * head // 2)),
+    )
+    raw = jnp.concatenate(
+        [w.reshape(block, heads_z, head) for w in (w_query, w_key, w_value)], axis=2
+    ).transpose(1, 0, 2)
+    grad_tokens, d_attn, d_bias_row, d_gain_attention, squares, extras = finish(
+        product_bt(grad_qkv, attn_weights[:, : 3 * head]).astype(bf16),
+        grad_hidden,
+        my_rows(tokens),
+        d_attn.reshape(heads_z, 2, block, 4 * head).transpose(1, 0, 2, 3),
+        d_biases,
+        raw,
+        extras,
+        chunks,
+    )
+    d_attn = d_attn.astype(f32)
+    d_bias_row = d_bias_row[0]
+    d_gain_attention = jnp.sum(d_gain_attention, axis=1)
+    d_query, d_key, d_value = (
+        d_attn[:, :, k * head : (k + 1) * head].transpose(1, 0, 2).reshape(block, heads_z * head)
+        * attn_gain_own
+        for k in range(3)
+    )
+    d_out = d_attn[:, :, 3 * head :].transpose(0, 2, 1).reshape(heads_z * head, block)
+    half_head = head // 2
+
+    d_router, d_share_vector = extras[:experts].T, extras[experts]
+    d_gain_experts = extras[experts + 1]
+    cells = length.astype(f32) * model
+    rms_output = jnp.sqrt(extras[experts + 2, 0] / cells)
+    rms_grad = jnp.sqrt(jnp.sum(squares) / cells)
+    return (
+        mixed,
+        grad_tokens,
+        d_query,
+        d_key,
+        d_value,
+        d_out,
+        d_bias_row[:half_head],
+        d_bias_row[half_head : 2 * half_head],
+        d_bias_row[2 * half_head : 3 * half_head],
+        d_gain_attention,
+        d_gain_experts,
+        d_router,
+        d_share_vector,
+        d_shared_gate,
+        d_shared_up,
+        d_shared_down,
+        d_expert_gate.transpose(0, 2, 1),
+        d_expert_up.transpose(0, 2, 1),
+        d_expert_down,
+        rms_output,
+        rms_grad,
+    )
+
+
+def specs(row, column):
+    both = column + row
+    ins = (
+        P(row, None),
+        P(row, None),
         P(),
-        P("exp", None),
-        P("exp", "tp"),
-        P("exp", "tp"),
-        P("exp", "tp"),
-        P("tp", "exp"),
-        P(("tp", "exp")),
-        P(("tp", "exp")),
-        P(("tp", "exp")),
-        P("exp"),
-        P("exp"),
-        P("exp", None),
-        P("exp"),
-        P("exp", "tp"),
-        P("exp", "tp"),
-        P("tp", "exp"),
-        P("exp", None, "tp"),
-        P("exp", None, "tp"),
-        P("exp", "tp", None),
-    )
-    out_specs = (
-        P("exp", None),
-        P("exp", None),
-        P("exp", "tp"),
-        P("exp", "tp"),
-        P("exp", "tp"),
-        P("tp", "exp"),
-        P(("tp", "exp")),
-        P(("tp", "exp")),
-        P(("tp", "exp")),
-        P("exp"),
-        P("exp"),
-        P("exp", None),
-        P("exp"),
-        P("exp", "tp"),
-        P("exp", "tp"),
-        P("tp", "exp"),
-        P("exp", None, "tp"),
-        P("exp", None, "tp"),
-        P("exp", "tp", None),
+        P(row, None),
+        P(row, column),
+        P(row, column),
+        P(row, column),
+        P(column, row),
+        P(both),
+        P(both),
+        P(both),
+        P(row),
+        P(row),
+        P(row, None),
+        P(row),
+        P(row, column),
+        P(row, column),
+        P(column, row),
+        P(row, None, column),
+        P(row, None, column),
+        P(row, column, None),
+    )
+    outs = (
+        P(row, None),
+        P(row, None),
+        P(row, column),
+        P(row, column),
+        P(row, column),
+        P(column, row),
+        P(both),
+        P(both),
+        P(both),
+        P(row),
+        P(row),
+        P(row, None),
+        P(row),
+        P(row, column),
+        P(row, column),
+        P(column, row),
+        P(row, None, column),
+        P(row, None, column),
+        P(row, column, None),
         P(),
         P(),
     )
-    return jax.shard_map(local, mesh=mesh, in_specs=in_specs, out_specs=out_specs, check_vma=False)
+    return ins, outs
+
+
+def solution(mesh):
+    if (mesh.shape["exp"], mesh.shape["tp"]) == (8, 4):
+        body, row, column = packed, ROW_AXES, COLUMN_AXES
+        mesh = Mesh(mesh.devices.reshape(4, 2, 2, 2), ALL_AXES)
+    else:
+        body, row, column = general, ("exp",), ("tp",)
+    ins, outs = specs(row, column)
+    return jax.shard_map(body, mesh=mesh, in_specs=ins, out_specs=outs, check_vma=False)

time: 2960 us -> 1010 us (0.34)
  waiting for transfers between devices: 1410 us -> 30.7 us
  Pallas kernels: 0 us -> 791 us
  blocking collectives: 607 us -> 0 us
  matrix products: 380 us -> 33 us
  local copies, waits for them, and re-layouts: 294 us -> 80.9 us
  other arithmetic: 157 us -> 30.1 us
  starting transfers between devices: 75.1 us -> 12 us
    pallas_call x0 -> x6, Pallas kernels: none -> 791 us  [the longest x1 348 us: stream(): pl.pallas_call(functools.partial(stream_kernel, units=units, experts=expe...]
    reduce_scatter x10 -> x0, waiting for transfers between devices: 637 us -> none  [the longest x1 126 us: local(): lax.psum_scatter(rows_back.astype(jnp.bfloat16), 'tp', scatter_dimension=...]
    all_gather x9 -> x2, waiting for transfers between devices: 445 us -> 20 us  [the longest x1 20 us: packed(): lax.all_gather(grad_hidden.astype(bf16), SAME_X, axis=0, tiled=True)]
    all_gather x4 -> x0, blocking collectives: 328 us -> none  [the longest x1 181 us: local(): lax.all_gather(w_router, 'exp', axis=0, tiled=True)]
    dot_general x17 -> x0, matrix products: 254 us -> none  [the longest x1 23.7 us: local(): jnp.einsum('qhd,khd->hqk', grad_attended, all_values, preferred_element_t...]
    ppermute x28 -> x1, waiting for transfers between devices: 225 us -> 10.6 us  [packed(): away = lax.ppermute(grad_kv[1], 'x', flip)]
    all_to_all x2 -> x0, blocking collectives: 194 us -> none  [the longest x1 98.4 us: local(): lax.all_to_all(sending, 'exp', split_axis=0, concat_axis=0, tiled=True)]
    gather x4 -> x0, local copies, waits for them, and re-layouts: 123 us -> none  [the longest x1 35.8 us: local(): padded_grads[slot_pair]]
  transfers between devices with their start and end apart: 52 -> 4, of which waited for: 28 -> 2; matrix products, arithmetic and copies ran while one was open for 16% -> 8% of each run, Pallas kernels for 0% -> 17%
where the time goes in v1:
time: 1010 us; the launch traced here: 998 us
  Pallas kernels  791 us (78%)
  local copies, waits for them, and re-layouts  80.9 us (8%)
  matrix products  33 us (3%)
  waiting for transfers between devices  30.7 us (3%)
  other arithmetic  30.1 us (3%)
  between operations  19.9 us (2%)
  starting transfers between devices  12 us (1%)
    pallas_call x1, Pallas kernels, stream(): pl.pallas_call(functools.partial(stream_kernel, units=units, experts=expe...  348 us
    pallas_call x1, Pallas kernels, middle(): pl.pallas_call(functools.partial(middle_kernel, rows=rows), in_specs=[pl....  147 us
    pallas_call x1, Pallas kernels, finish(): pl.pallas_call(finish_kernel, in_specs=[inside] * 7, out_specs=[anywhere]...  112 us
    pallas_call x1, Pallas kernels, front(): pl.pallas_call(front_kernel, in_specs=[anywhere, anywhere], out_specs=[an...  98.8 us
    pallas_call x1, Pallas kernels, weight_grads(): pl.pallas_call(functools.partial(weight_grads_kernel, units=units, share=...  59.8 us
    dot_general x3, local copies, waits for them, and re-layouts, product_at(): lax.dot_general(left, right, (((0,), (0,)), ((), ())), preferred_element_...  25.7 us
    pallas_call x1, Pallas kernels, attend_back(): pl.pallas_call(functools.partial(attend_back_kernel, tile=tile, keys=rows...  25.7 us
  transfers between devices with their start and end apart: 4, of which 2 were waited for; matrix products, arithmetic and copies ran while one was open for 8% of the time, Pallas kernels for 17%

profile of v1, /device:TPU:0, one launch (start us, length us, event | category | flops | bytes accessed | tf_op | source)
XLA Modules:
  0.0 997.7 jit_solution(4422060032115036349)
XLA Ops:
  11.9 98.8 %shard_map.364 = (bf16[2,2,4,4,32,2048]{5,4,3,2,1,0:T(8,128)(2,1)S(1)}, bf16[4,2,272,512]{3,2,1,0:T(8,128)(2,1)S(1)}) custom-call(bf16[4,32,2048]{2,1,0:T(8,128)(2,1)S(1)} %bitcast.228, bf16[4,272,512]{2,1,0:T(8,128)(2,1)S(1)} %pad_maximum_fusion.2.parts_ref), custom_call_target="tpu_custom_call" | custom-call | tf_op jit(solution)/shard_map/pallas_call | solution.py:668
  110.7 3.2 copy-done.2
  121.6 2.2 copy.112
  126.6 1.6 fusion.28
  131.7 1.7 fusion.33.s_ref
  134.9 147.1 %shard_map.365 = (bf16[2048,128]{1,0:T(8,128)(2,1)}, bf16[2,2048,256]{2,1,0:T(8,128)(2,1)}, f32[2048,128]{1,0:T(8,128)}, f32[2048,128]{1,0:T(8,128)}, bf16[16,12...) custom-call(s32[1]{0:T(128)} %copy.179.length_ref, ...), custom_call_target="tpu_custom_call" | custom-call | flops 5368709120 | bytes 62914560 | tf_op jit(solution)/shard_map/pallas_call | solution.py:935
  282.0 348.2 %shard_map.366 = (bf16[2,2,2,4,8,16,2048]{6,5,4,3,2,1,0:T(8,128)(2,1)}, bf16[2,2,2,4,8,16,896]{6,5,4,3,2,1,0:T(8,128)(2,1)}, bf16[2,2,2,4,8,16,1792]{6,5,4,3,2,1...) custom-call(bf16[2,2,4,8,16,2048]{5,4,3,2,1,0:T(8,128)(2,1)} %bitcas, ...), custom_call_target="tpu_custom_call" | custom-call | flops 90194313216 | bytes 139460608 | tf_op jit(solution)/shard_map/pallas_call | solution.py:1553
  636.0 3.9 multiply_reduce_fusion.1
  640.1 2.5 fusion.55
  646.3 12.4 %copy.151 = bf16[2048,2048]{1,0:T(8,128)(2,1)} copy(bf16[2048,2048]{0,1:T(8,128)(2,1)} %bitcast.224) | data formatting | bytes 16777216 | tf_op jit(solution)/shard_map/dot_general | solution.py:60
  662.6 1.6 multiply_subtract_fusion
  664.2 59.8 %shard_map.367 = (f32[2,352,2048]{2,1,0:T(8,128)}, f32[2,352,2048]{2,1,0:T(8,128)}, f32[2,352,2048]{2,1,0:T(8,128)}, bf16[8,528,256]{2,1,0:T(8,128)(2,1)}) custom-call(bf16[4096,2048]{1,0:T(8,128)(2,1)} %bitcast.300, bf16[4096,2176]{1,0:T(8,128)(2,1)} %bitcast.299, bf16[4096,1792]{1,0:T(8,128)(2,1)} %bitcast.301, bf16[4096,896]{1,0:T(8,128)(2,1)} %bitcast.303), custom_call_target="tpu_custom_call" | custom-call | flops 45097156608 | bytes 77594624 | tf_op jit(solution)/shard_map/pallas_call | solution.py:1928
  724.0 20.0 %all-gather.5.cloned.1.call-done = bf16[2048,2048]{1,0:T(8,128)(2,1)} async-done(((bf16[128,2048]{1,0:T(8,128)(2,1)}), bf16[2048,2048]{1,0:T(8,128)(2,1)}) %all-gather.5.cloned.1.call-update) | async-done | bytes 8388624 | tf_op jit(solution)/shard_map/all_gather | solution.py:2156
  744.1 5.9 convolution_convert_fusion.1
  750.1 25.7 %shard_map.368 = (f32[2048,128]{1,0:T(8,128)S(1)}, f32[2,2048,128]{2,1,0:T(8,128)S(1)}, f32[2,2048,128]{2,1,0:T(8,128)S(1)}) custom-call(s32[2]{0:T(128)S(1)} %pad_add_fusion.info_ref, bf16[2048,128]{1,0:T(8,128)(2,1)S(1)} %copy-done.11, bf16[2,2048,256]{2,1,0:T(8,128)(2,1)S(1)} %copy-done.9, bf16[2048,128]{1,0:T(8,128)(2,1)S(1)} %bitcast.231, ...), custom_call_target="tpu_custom_call" | custom-call | flops 5368709120 | bytes 12582912 | tf_op jit(solution)/shard_map/pallas_call | solution.py:560
  778.2 7.4 collective-permute-start
  786.7 12.3 %copy.152 = bf16[2048,2048]{1,0:T(8,128)(2,1)} copy(bf16[2048,2048]{0,1:T(8,128)(2,1)} %bitcast.236) | data formatting | bytes 16777216 | tf_op jit(solution)/shard_map/dot_general | solution.py:60
  799.0 4.5 all-to-all-start
  804.6 5.8 fusion.10
  810.5 10.6 %collective-permute-done = bf16[2048,256]{1,0:T(8,128)(2,1)} collective-permute-done((bf16[2048,256]{1,0:T(8,128)(2,1)}, bf16[2048,256]{1,0:T(8,128)(2,1)}, u32[]{:S(2)}, u32[]{:S(2)}) %collective-permute-start) | collective-permute-done | bytes 1048608 | tf_op jit(solution)/shard_map/ppermute | solution.py:2185
  826.3 7.9 fusion.5
  834.3 1.5 maximum_bitcast_fusion.wp_ref
  836.6 6.9 convolution_convert_fusion
  843.5 111.6 %shard_map.369 = (bf16[2,2,8,16,2048]{4,3,2,1,0:T(8,128)(2,1)S(1)}, bf16[4,256,512]{2,1,0:T(8,128)(2,1)S(1)}, f32[16,512]{1,0:T(8,128)S(1)}, f32[256,128]{1,0:T(...) custom-call(bf16[2,2,4,8,16,2048]{5,4,3,2,1,0:T(8,128)(2,1)} %bitcast.237, f32[8,16,2048]{2,1,0:T(8,128)S(1)} %bitcast.227, ...), custom_call_target="tpu_custom_call" | custom-call | flops 26214400 | bytes 41943040 | tf_op jit(solution)/shard_map/pallas_call | solution.py:1851
  957.9 2.0 copy.137
  960.9 2.3 bitcast_multiply_fusion.9
  963.2 2.1 copy.142
  965.3 2.0 copy.143
  974.3 3.7 fusion.56
  978.0 2.9 copy.140
  980.9 2.9 copy.141
  983.8 3.2 copy.180
  (253 shorter events, 53.2 us)
Async XLA Ops:
  7.2 108.2 %copy-start = (s32[512,4]{0,1:T(4,128)S(1)}, s32[512,4]{0,1:T(4,128)}, u32[]{:S(2)}) copy-start(s32[512,4]{0,1:T(4,128)} %param.24) | copy-start | bytes 24580
  7.3 3.0 copy-start.35
  7.3 3.2 copy-start.60
  7.3 716.7 %all-gather.3.cloned.1.call-start = ((), (), s32[]{:S(2)}) async-start(), calls=%async_computation.1 | async-start | bytes 2621440 | tf_op jit(solution)/shard_map/all_gather | solution.py:2134
  110.7 3.2 copy-start.2
  113.9 9.9 copy-start.8
  117.2 3.0 copy-start.29
  117.4 10.9 %copy-start.37 = (f32[16,64]{1,0:T(8,128)}, f32[16,64]{1,0:T(8,128)S(1)}, u32[]{:S(2)}) copy-start(f32[16,64]{1,0:T(8,128)S(1)} %get-tuple-element.163) | copy-start | bytes 12292
  123.8 9.6 copy-start.18
  123.8 9.6 copy-start.27
  282.0 351.8 %copy-start.45 = (f32[1,2,8,128]{3,2,1,0:T(8,128)S(1)}, f32[1,2,8,128]{3,2,1,0:T(8,128)}, u32[]{:S(2)}) copy-start(f32[1,2,8,128]{3,2,1,0:T(8,128)} %get-tuple-element.150) | copy-start | bytes 24580
  282.0 351.8 %copy-start.46 = (bf16[1,2,8,128]{3,2,1,0:T(8,128)(2,1)S(1)}, bf16[1,2,8,128]{3,2,1,0:T(8,128)(2,1)}, u32[]{:S(2)}) copy-start(bf16[1,2,8,128]{3,2,1,0:T(8,128)(2,1)} %get-tuple-element.151) | copy-start | bytes 12292
  630.2 5.0 copy-start.44
  630.2 5.0 copy-start.14
  630.2 5.0 copy-start.40
  630.2 5.8 copy-start.13
  630.2 5.8 copy-start.51
  635.2 4.8 copy-start.41
  640.0 104.1 %all-gather.5.cloned.1.call-start = ((), (), s32[]{:S(2)}) async-start(), calls=%async_computation.2 | async-start | bytes 8912896 | tf_op jit(solution)/shard_map/all_gather | solution.py:2156
  646.3 12.4 %copy-start.6 = (f32[2048,128]{1,0:T(8,128)S(1)}, f32[2048,128]{1,0:T(8,128)}, u32[]{:S(2)}) copy-start(f32[2048,128]{1,0:T(8,128)} %get-tuple-element.68.o_ref) | copy-start | bytes 3145732
  744.1 6.0 copy-start.7
  744.1 6.0 copy-start.9
  744.1 6.0 copy-start.10
  744.1 6.0 copy-start.11
  778.2 42.8 %collective-permute-start = (bf16[2048,256]{1,0:T(8,128)(2,1)}, bf16[2048,256]{1,0:T(8,128)(2,1)}, u32[]{:S(2)}, u32[]{:S(2)}) collective-permute-start(bf16[2048,256]{1,0:T(8,128)(2,1)} %fusion.20), channel_id=1, source_target_pairs={{0,4},{4,0},{1,5},{5,1},{2,6},{6,2},{3,7},{7,3},{8,12},{12,8},{9,1... | collective-permute-start | bytes 3145736 | tf_op jit(solution)/shard_map/ppermute | solution.py:2185
  799.0 175.3 %all-to-all-start = ((bf16[8,528,256]{2,1,0:T(8,128)(2,1)}), bf16[8,528,256]{2,1,0:T(8,128)(2,1)}, u32[]{:S(2)}, u32[]{:S(2)}) async-start(bf16[8,528,256]{2,1,0:T(8,128)(2,1)} %get-tuple-element.78), calls=%async_computation | async-start | bytes 4325376 | tf_op jit(solution)/shard_map/all_to_all | solution.py:2170
  804.6 16.4 %copy-start.17 = (f32[2048,128]{1,0:T(8,128)S(1)}, f32[2048,128]{1,0:T(8,128)}, u32[]{:S(2)}) copy-start(f32[2048,128]{1,0:T(8,128)} %slice_bitcast_fusion) | copy-start | bytes 3145732
  836.6 6.9 copy-start.4
  836.6 6.9 copy-start.5
  956.6 4.3 copy-start.49
  963.2 5.1 copy-start.26
  983.8 4.5 copy-start.1
  (34 other events, 69.0 us)
Sparse Core Ops, SparseCore 0:
  640.1 26.1 all-gather.2
  669.1 74.8 all-gather.4

commit v2 on v1

--- a/solution.py
+++ b/solution.py
@@ -2,6 +2,7 @@
 
 import jax
 import jax.numpy as jnp
+import numpy as np
 from jax import lax
 from jax.experimental import pallas as pl
 from jax.experimental.pallas import tpu as pltpu
@@ -723,8 +724,6 @@
     block = model // e_count
     own = rows // 4
     tile = 2 * own
-    half = model // 2
-    left, right = pl.ds(0, half), pl.ds(half, leaving_ref.shape[2] - half)
     flip = {"x": {"x": 1 - x}, "y": {"y": 1 - y}, "c": {"c": 1 - c}}
 
     def up(distance):
@@ -750,18 +749,19 @@
         ]
 
     def spread_2(k):
-        a = all_ref.at[c, y, x, :, k, :, left]
-        b = all_ref.at[c, y, x, :, k, :, right]
-        return remote(0, k, a, a, flip["x"]), remote(1, k, b, b, flip["y"])
+        a = all_ref.at[c, y, x, :, k]
+        return (remote(0, k, a, a, flip["x"]),)
 
     def spread_3(k):
-        a = all_ref.at[c, y, :, :, k, :, left]
-        b = all_ref.at[c, :, x, :, k, :, right]
-        return remote(2, k, a, a, flip["y"]), remote(3, k, b, b, flip["x"])
+        a = all_ref.at[c, y, :, :, k]
+        return (remote(1, k, a, a, flip["y"]),)
 
     def spread_c(k):
-        a = all_ref.at[c, :, :, :, k]
-        return (remote(4, k, a, a, flip["c"]),)
+        copies = []
+        for j in range(2):
+            a = all_ref.at[c, j, :, :, k]
+            copies.append(remote(2 + j, k, a, a, flip["c"]))
+        return copies
 
     def share(d, other):
         z_to, x_to = lax.rem(z + d, z_count), 1 - x if other else x
@@ -819,7 +819,7 @@
             s = 2 * t + h
             z_of, y_of, c_of = lax.rem(s, 4), lax.rem(s // 4, 2), s // 8
             place = pl.ds(pl.multiple_of((z_of * 4 + y_of * 2 + c_of) * own, own), own)
-            block_cos, block_sin = block_ref[0, pl.ds(s, 1)], block_ref[1, pl.ds(s, 1)]
+            block_cos, block_sin = block_ref[x, 0, pl.ds(s, 1)], block_ref[x, 1, pl.ds(s, 1)]
             cosine = block_cos * row_ref[0] - block_sin * row_ref[1]
             sine = (block_sin * row_ref[0] + block_cos * row_ref[1]) * sign
             part = lin[h * own : (h + 1) * own]
@@ -882,6 +882,8 @@
     lax.fori_loop(0, count // tile, first_pass, 0)
     finish(spread_z(1))
     start(spread_2(1))
+    finish(spread_2(0))
+    start(spread_3(0))
     key_values().wait()
 
     def second_pass(i, carry):
@@ -898,21 +900,29 @@
         for h in range(2):
             z_of, y_of, c_of = i // 2, lax.rem(i, 2), h
             part_ref[c_of * 8 + y_of * 4 + z_of] = part[h * own : (h + 1) * own]
+
+        @pl.when(i == 2)
+        def _():
+            finish(spread_z(2))
+            start(spread_2(2))
+            finish(spread_2(1))
+            start(spread_3(1))
+
+        @pl.when(i == 5)
+        def _():
+            finish(spread_z(3))
+            start(spread_2(3))
+            finish(spread_2(2))
+            start(spread_3(2))
+            finish(spread_3(0))
+            start(spread_c(0))
+
         return carry
 
     lax.fori_loop(0, count // tile, second_pass, 0)
-    finish(spread_2(0))
-    start(spread_3(0))
-    for k in range(2, chunks):
-        finish(spread_z(k))
-        start(spread_2(k))
-        finish(spread_2(k - 1))
-        start(spread_3(k - 1))
-        finish(spread_3(k - 2))
-        start(spread_c(k - 2))
-    finish(spread_2(chunks - 1))
-    start(spread_3(chunks - 1))
-    for k in (chunks - 2, chunks - 1):
+    finish(spread_2(3))
+    start(spread_3(3))
+    for k in range(1, chunks):
         finish(spread_3(k))
         start(spread_c(k))
     for k in range(chunks):
@@ -1088,6 +1098,8 @@
     send,
     send_z,
     send_r,
+    send_c,
+    recv_c,
     recv,
     here,
     weigh,
@@ -1174,16 +1186,33 @@
         b = all_ref.at[c, :, x, :, k, :, right]
         return remote(2, k, a, a, flip["y"]), remote(3, k, b, b, flip["x"])
 
+    def across(slot, k, src, dst):
+        return pltpu.make_async_remote_copy(
+            src_ref=src,
+            dst_ref=dst,
+            send_sem=send_c.at[slot, lax.rem(k, 2)],
+            recv_sem=recv_c.at[slot, k],
+            device_id=flip["c"],
+            device_id_type=pl.DeviceIdType.MESH,
+        )
+
     def spread_c(k):
-        a = all_ref.at[c, :, :, :, k]
-        return (remote(4, k, a, a, flip["c"]),)
+        copies = []
+        for j in range(2):
+            for m in range(2):
+                a = all_ref.at[c, j, m, :, k]
+                copies.append(across(2 * j + m, k, a, a))
+        return copies
 
     def sum_c(k):
         slot = lax.rem(k, 2)
-        return (
-            remote(5, k, pa.at[slot, 1 - c], lca_ref.at[k], flip["c"]),
-            remote(6, k, pb.at[slot, 1 - c], lcb_ref.at[k], flip["c"]),
-        )
+        copies = []
+        for j in range(2):
+            for m in range(2):
+                i = 4 + 2 * j + m
+                copies.append(across(i, k, pa.at[slot, 1 - c, j, m], lca_ref.at[k, j, m]))
+                copies.append(across(4 + i, k, pb.at[slot, 1 - c, j, m], lcb_ref.at[k, j, m]))
+        return copies
 
     def sum_2(k):
         return (
@@ -1545,6 +1574,8 @@
         dma((21, 2)),
         dma((3, chunks)),
         dma((chunks,)),
+        dma((12, 2)),
+        dma((12, chunks)),
         dma((25, chunks)),
         dma((21,)),
         dma((5 + 3 * shared.shape[0],)),
@@ -1584,8 +1615,12 @@
     bp_ref,
     w_ref,
     e_ref,
+    scale_ref,
     rows_ref,
-    heads_ref,
+    dq_ref,
+    dk_ref,
+    dv_ref,
+    do_ref,
     bias_ref,
     gain_ref,
     square_ref,
@@ -1599,6 +1634,7 @@
     wl,
     bl,
     ws,
+    heads_ref,
     gs,
     gl,
     ss,
@@ -1781,6 +1817,33 @@
         for d in range(1, 4):
             extra_z(d).start()
 
+    def gain_y():
+        return single(6, gs.at[0], gl.at[0], flip["y"])
+
+    def gain_c():
+        return single(8, gs.at[1], gl.at[1], flip["c"])
+
+    def weights_done():
+        for d in range(1, 4):
+            weights_z(d).wait()
+        total = jnp.zeros(gain_ref.shape, jnp.float32)
+        scale = scale_ref[...]
+        for i in range(4):
+            place = slice(i * head, (i + 1) * head)
+            for j, ref in enumerate((dq_ref, dk_ref, dv_ref)):
+                columns = slice(j * head, (j + 1) * head)
+                values = heads_ref[i, :, columns].astype(jnp.float32)
+                total = total + w_ref[i, :, columns].astype(jnp.float32) * values
+                ref[:, place] = values * scale
+            do_ref[place, :] = heads_ref[i, :, 3 * head :].astype(jnp.float32).T
+        gs[0] = total
+        gain_y().start()
+
+    def gain_sum():
+        gain_y().wait()
+        gs[1] = gs[0] + gl[0]
+        gain_c().start()
+
     extra_c().start()
 
     def tick(i, carry):
@@ -1793,6 +1856,8 @@
         pl.when(i == 2)(extra_sum_c)
         pl.when(i == 4)(extra_sum_y)
         pl.when(i == 6)(extra_sum_x)
+        pl.when(i == 7)(weights_done)
+        pl.when(i == 9)(gain_sum)
         return carry
 
     lax.fori_loop(0, chunks + 7, tick, 0)
@@ -1802,26 +1867,10 @@
     ss[0] = square_ref[...]
     squares_c = single(5, ss.at[0], sl.at[0], flip["c"])
     squares_c.start()
-    for d in range(1, 4):
-        weights_z(d).wait()
-    total = jnp.zeros(gain_ref.shape, jnp.float32)
-    for i in range(4):
-        for j in range(3):
-            columns = slice(j * head, (j + 1) * head)
-            total = total + w_ref[i, :, columns].astype(jnp.float32) * heads_ref[
-                i, :, columns
-            ].astype(jnp.float32)
-    gs[0] = total
-    gain_y = single(6, gs.at[0], gl.at[0], flip["y"])
-    gain_y.start()
     squares_c.wait()
     ss[1] = ss[0] + sl[0]
     squares_y = single(7, ss.at[1], sl.at[1], flip["y"])
     squares_y.start()
-    gain_y.wait()
-    gs[1] = gs[0] + gl[0]
-    gain_c = single(8, gs.at[1], gl.at[1], flip["c"])
-    gain_c.start()
     squares_y.wait()
     ss[2] = ss[1] + sl[1]
     squares_x = single(9, ss.at[2], sl.at[2], flip["x"])
@@ -1831,14 +1880,14 @@
     squares_z = [single(9 + d, ss.at[3], sl.at[2 + d], up(d)) for d in range(1, 4)]
     for copy in squares_z:
         copy.start()
-    gain_c.wait()
+    gain_c().wait()
     gain_ref[...] = gs[1] + gl[1]
     for copy in squares_z:
         copy.wait()
     square_ref[...] = ss[3] + sl[3] + sl[4] + sl[5]
 
 
-def finish(partial, grads, tokens, weight_parts, bias_parts, weights, extras, chunks):
+def finish(partial, grads, tokens, weight_parts, bias_parts, weights, extras, scale, chunks):
     own, model = tokens.shape
     piece = own // chunks
     zs = lax.axis_size("z")
@@ -1848,13 +1897,16 @@
     inside = pl.BlockSpec(memory_space=pltpu.VMEM)
     vm = pltpu.VMEM
     dma = pltpu.SemaphoreType.DMA
-    rows, heads, bias, gain, square, extra = pl.pallas_call(
+    rows, d_query, d_key, d_value, d_out, bias, gain, square, extra = pl.pallas_call(
         finish_kernel,
-        in_specs=[inside] * 7,
-        out_specs=[anywhere] + [inside] * 5,
+        in_specs=[inside] * 8,
+        out_specs=[anywhere] + [inside] * 8,
         out_shape=[
             jax.ShapeDtypeStruct((2, 2, chunks, piece, model), bf16),
-            jax.ShapeDtypeStruct((zs, block, wide), bf16),
+            jax.ShapeDtypeStruct((block, wide), f32),
+            jax.ShapeDtypeStruct((block, wide), f32),
+            jax.ShapeDtypeStruct((block, wide), f32),
+            jax.ShapeDtypeStruct((wide, block), f32),
             jax.ShapeDtypeStruct(bias_parts.shape[1:], f32),
             jax.ShapeDtypeStruct((block, 128), f32),
             jax.ShapeDtypeStruct((8, 128), f32),
@@ -1869,6 +1921,7 @@
             vm((chunks, piece, model), bf16),
             vm((zs, block, wide), bf16),
             vm(bias_parts.shape[1:], bf16),
+            vm((zs, block, wide), bf16),
             vm((zs, block, wide), bf16),
             vm((2, block, 128), f32),
             vm((2, block, 128), f32),
@@ -1900,8 +1953,9 @@
         bias_parts,
         weights,
         extras,
-    )
-    return rows.reshape(4 * own, model), heads, bias, gain, square, extra
+        scale,
+    )
+    return rows.reshape(4 * own, model), d_query, d_key, d_value, d_out, bias, gain, square, extra
 
 
 def weight_grads_kernel(
@@ -2047,16 +2101,20 @@
     place += block * experts
     share_vector = small[:, place : place + block].reshape(model)
 
-    frequency = ROPE_BASE ** (-(jnp.arange(half_dim, dtype=f32) * 2.0) / head)
-    row_angle = jnp.arange(own, dtype=f32)[:, None] * frequency[None, :]
-    places = (
-        jnp.arange(2)[:, None, None] * own
-        + jnp.arange(2)[None, :, None] * 2 * own
-        + (jnp.arange(heads_z)[None, None, :] * 2 + x_index) * rows
-    )
-    block_angle = places.reshape(-1).astype(f32)[:, None] * frequency[None, :]
-    row_cos, row_sin = jnp.cos(row_angle)[None], jnp.sin(row_angle)[None]
-    block_cos, block_sin = jnp.cos(block_angle)[:, None], jnp.sin(block_angle)[:, None]
+    frequency = np.tile(ROPE_BASE ** (-np.arange(half_dim) * 2.0 / head), 2)
+    row_angle = np.arange(own)[:, None] * frequency
+    starts = (
+        np.arange(2)[:, None, None, None] * rows
+        + np.arange(2)[None, :, None, None] * own
+        + np.arange(2)[None, None, :, None] * 2 * own
+        + np.arange(heads_z)[None, None, None, :] * 2 * rows
+    )
+    block_angle = starts.reshape(2, -1, 1) * frequency
+    row_table = np.stack([np.cos(row_angle), np.sin(row_angle)]).astype(np.float32)
+    block_table = np.stack([np.cos(block_angle), np.sin(block_angle)], axis=1).astype(np.float32)
+    row_cos, row_sin = jnp.asarray(row_table[:, None, :, :half_dim])
+    block_both = lax.dynamic_index_in_dim(jnp.asarray(block_table), x_index, 0, keepdims=False)
+    block_cos, block_sin = block_both[:, :, None, :half_dim]
     cosine = (block_cos * row_cos - block_sin * row_sin).reshape(heads_z * rows, half_dim)
     sine = (block_sin * row_cos + block_cos * row_sin).reshape(heads_z * rows, half_dim)
 
@@ -2079,16 +2137,13 @@
         )
 
     flip = [(0, 1), (1, 0)]
-    def twice(cos, sin):
-        return jnp.stack([jnp.tile(cos, (1, 2)), jnp.tile(sin, (1, 2))])
-
     query_rot, key_values, attended, log_total, attn_part, attn_weights, grad_all, shared_parts = (
         middle(
             lengths,
             first_half,
             arrived_weights,
-            twice(row_cos[0], row_sin[0]),
-            twice(block_cos[:, 0], block_sin[:, 0]),
+            jnp.asarray(row_table),
+            jnp.asarray(block_table),
             leaving,
             shared_parts,
             rows,
@@ -2176,7 +2231,7 @@
     )
     d_shared_gate, d_shared_up = d_shared_gate.T, d_shared_up.T
     grad_attended = product(hidden_half, out_weight).astype(bf16)
-    d_out_weight = product_at(hidden_half, attended_low)
+    d_out_weight = product_at(attended_low, hidden_half)
     scale = 1.0 / head**0.5
     grad_query, grad_key, grad_value = attend_back(
         info, query_rot, key_values, by_position(grad_attended), attended, log_total, rows
@@ -2194,7 +2249,7 @@
         ],
         axis=1,
     ).astype(bf16)
-    d_attn = jnp.concatenate([product_at(first_half, grad_qkv), d_out_weight], axis=1).astype(bf16)
+    d_attn = jnp.concatenate([product_at(grad_qkv, first_half), d_out_weight]).astype(bf16)
     d_biases = jnp.sum(grad_qkv.astype(f32), axis=0).astype(bf16).reshape(3, 2, head // 2)
     d_biases = jnp.pad(
         d_biases.transpose(1, 0, 2).reshape(2, 1, 3 * head // 2),
@@ -2203,25 +2258,19 @@
     raw = jnp.concatenate(
         [w.reshape(block, heads_z, head) for w in (w_query, w_key, w_value)], axis=2
     ).transpose(1, 0, 2)
-    grad_tokens, d_attn, d_bias_row, d_gain_attention, squares, extras = finish(
+    grad_tokens, d_query, d_key, d_value, d_out, d_bias_row, d_gain_attention, squares, extras = finish(
         product_bt(grad_qkv, attn_weights[:, : 3 * head]).astype(bf16),
         grad_hidden,
         my_rows(tokens),
-        d_attn.reshape(heads_z, 2, block, 4 * head).transpose(1, 0, 2, 3),
+        d_attn.reshape(4 * head, heads_z, 2, block).transpose(2, 1, 3, 0),
         d_biases,
         raw,
         extras,
+        attn_gain_own,
         chunks,
     )
-    d_attn = d_attn.astype(f32)
     d_bias_row = d_bias_row[0]
     d_gain_attention = jnp.sum(d_gain_attention, axis=1)
-    d_query, d_key, d_value = (
-        d_attn[:, :, k * head : (k + 1) * head].transpose(1, 0, 2).reshape(block, heads_z * head)
-        * attn_gain_own
-        for k in range(3)
-    )
-    d_out = d_attn[:, :, 3 * head :].transpose(0, 2, 1).reshape(heads_z * head, block)
     half_head = head // 2
 
     d_router, d_share_vector = extras[:experts].T, extras[experts]

time: 1010 us -> 1010 us (level)
  Pallas kernels: 791 us -> 819 us
  waiting for transfers between devices: 30.7 us -> 17 us
    pallas_call x1, Pallas kernels: 147 us -> 177 us  [middle(): pl.pallas_call(functools.partial(middle_kernel, rows=rows), in_specs=[pl....]
    ppermute x1, waiting for transfers between devices: 10.6 us -> 0.01 us  [packed(): away = lax.ppermute(grad_kv[1], 'x', flip)]
  transfers between devices with their start and end apart: 4 -> 4, of which waited for: 2 -> 1; matrix products, arithmetic and copies ran while one was open for 8% -> 8% of each run, Pallas kernels for 17% -> 17%
where the time goes in v2:
time: 1010 us; the launch traced here: 1000 us
  Pallas kernels  819 us (81%)
  local copies, waits for them, and re-layouts  77.4 us (8%)
  matrix products  33.5 us (3%)
  other arithmetic  26.7 us (3%)
  between operations  19.7 us (2%)
  waiting for transfers between devices  17 us (2%)
  starting transfers between devices  11.8 us (1%)
    pallas_call x1, Pallas kernels, stream(): pl.pallas_call(functools.partial(stream_kernel, units=units, experts=expe...  343 us
    pallas_call x1, Pallas kernels, middle(): pl.pallas_call(functools.partial(middle_kernel, rows=rows), in_specs=[pl....  177 us
    pallas_call x1, Pallas kernels, finish(): pl.pallas_call(finish_kernel, in_specs=[inside] * 8, out_specs=[anywhere]...  114 us
    pallas_call x1, Pallas kernels, front(): pl.pallas_call(front_kernel, in_specs=[anywhere, anywhere], out_specs=[an...  98.8 us
    pallas_call x1, Pallas kernels, weight_grads(): pl.pallas_call(functools.partial(weight_grads_kernel, units=units, share=...  59.8 us
    dot_general x3, local copies, waits for them, and re-layouts, product_at(): lax.dot_general(left, right, (((0,), (0,)), ((), ())), preferred_element_...  26 us
    pallas_call x1, Pallas kernels, attend_back(): pl.pallas_call(functools.partial(attend_back_kernel, tile=tile, keys=rows...  25.7 us
  transfers between devices with their start and end apart: 4, of which 1 were waited for; matrix products, arithmetic and copies ran while one was open for 8% of the time, Pallas kernels for 17%

profile of v2, /device:TPU:0, one launch (start us, length us, event | category | flops | bytes accessed | tf_op | source)
XLA Modules:
  0.0 1004.8 jit_solution(2862244926415444988)
XLA Ops:
  11.8 98.8 %shard_map.391 = (bf16[2,2,4,4,32,2048]{5,4,3,2,1,0:T(8,128)(2,1)S(1)}, bf16[4,2,272,512]{3,2,1,0:T(8,128)(2,1)S(1)}) custom-call(bf16[4,32,2048]{2,1,0:T(8,128)(2,1)S(1)} %bitcast.226, bf16[4,272,512]{2,1,0:T(8,128)(2,1)S(1)} %pad_maximum_fusion.2.parts_ref), custom_call_target="tpu_custom_call" | custom-call | tf_op jit(solution)/shard_map/pallas_call | solution.py:669
  110.6 3.2 copy-done.2
  118.1 2.2 copy.105
  122.9 1.6 fusion.24
  126.1 1.7 fusion.33.s_ref
  129.2 176.8 %shard_map.392 = (bf16[2048,128]{1,0:T(8,128)(2,1)}, bf16[2,2048,256]{2,1,0:T(8,128)(2,1)}, f32[2048,128]{1,0:T(8,128)}, f32[2048,128]{1,0:T(8,128)}, bf16[16,12...) custom-call(s32[1]{0:T(128)} %copy.180.length_ref, ...), custom_call_target="tpu_custom_call" | custom-call | flops 5368709120 | bytes 62914560 | tf_op jit(solution)/shard_map/pallas_call | solution.py:945
  306.1 343.3 %shard_map.393 = (bf16[2,2,2,4,8,16,2048]{6,5,4,3,2,1,0:T(8,128)(2,1)}, bf16[2,2,2,4,8,16,896]{6,5,4,3,2,1,0:T(8,128)(2,1)}, bf16[2,2,2,4,8,16,1792]{6,5,4,3,2,1...) custom-call(bf16[2,2,4,8,16,2048]{5,4,3,2,1,0:T(8,128)(2,1)} %bitcas, ...), custom_call_target="tpu_custom_call" | custom-call | flops 90194313216 | bytes 139460608 | tf_op jit(solution)/shard_map/pallas_call | solution.py:1584
  654.7 3.9 multiply_reduce_fusion.1
  658.8 2.5 fusion.53
  663.3 12.5 %copy.138 = bf16[2048,2048]{1,0:T(8,128)(2,1)} copy(bf16[2048,2048]{0,1:T(8,128)(2,1)} %bitcast.222) | data formatting | bytes 16777216 | tf_op jit(solution)/shard_map/dot_general | solution.py:61
  677.1 2.3 reshape.359
  683.0 59.8 %shard_map.394 = (f32[2,352,2048]{2,1,0:T(8,128)}, f32[2,352,2048]{2,1,0:T(8,128)}, f32[2,352,2048]{2,1,0:T(8,128)}, bf16[8,528,256]{2,1,0:T(8,128)(2,1)}) custom-call(bf16[4096,2048]{1,0:T(8,128)(2,1)} %bitcast.295, bf16[4096,2176]{1,0:T(8,128)(2,1)} %bitcast.294, bf16[4096,1792]{1,0:T(8,128)(2,1)} %bitcast.296, bf16[4096,896]{1,0:T(8,128)(2,1)} %bitcast.298), custom_call_target="tpu_custom_call" | custom-call | flops 45097156608 | bytes 77594624 | tf_op jit(solution)/shard_map/pallas_call | solution.py:1982
  742.7 17.0 %all-gather.5.cloned.1.call-done = bf16[2048,2048]{1,0:T(8,128)(2,1)} async-done(((bf16[128,2048]{1,0:T(8,128)(2,1)}), bf16[2048,2048]{1,0:T(8,128)(2,1)}) %all-gather.5.cloned.1.call-update) | async-done | bytes 8388624 | tf_op jit(solution)/shard_map/all_gather | solution.py:2211
  759.7 5.9 convolution_convert_fusion.1
  765.7 25.7 %shard_map.395 = (f32[2048,128]{1,0:T(8,128)S(1)}, f32[2,2048,128]{2,1,0:T(8,128)S(1)}, f32[2,2048,128]{2,1,0:T(8,128)S(1)}) custom-call(s32[2]{0:T(128)S(1)} %pad_add_fusion.info_ref, bf16[2048,128]{1,0:T(8,128)(2,1)S(1)} %copy-done.13, bf16[2,2048,256]{2,1,0:T(8,128)(2,1)S(1)} %copy-done.11, bf16[2048,128]{1,0:T(8,128)(2,1)S(1)} %bitcast.228, ...), custom_call_target="tpu_custom_call" | custom-call | flops 5368709120 | bytes 12582912 | tf_op jit(solution)/shard_map/pallas_call | solution.py:561
  794.0 7.4 collective-permute-start
  801.4 2.6 copy.109
  804.0 2.6 reshape.338
  806.6 12.5 %copy.139 = bf16[2048,2048]{1,0:T(8,128)(2,1)} copy(bf16[2048,2048]{0,1:T(8,128)(2,1)} %bitcast.230) | data formatting | bytes 16777216 | tf_op jit(solution)/shard_map/dot_general | solution.py:61
  819.1 4.4 all-to-all-start
  824.5 6.6 fusion.10
  832.6 2.0 copy.112
  834.6 2.1 reshape.340
  836.8 2.3 fusion.25
  839.8 8.2 fusion.5
  850.5 6.9 convolution_convert_fusion
  857.4 114.2 %shard_map.396 = (bf16[2,2,8,16,2048]{4,3,2,1,0:T(8,128)(2,1)}, f32[256,512]{1,0:T(8,128)S(1)}, f32[256,512]{1,0:T(8,128)S(1)}, f32[256,512]{1,0:T(8,128)S(1)}, ...) custom-call(bf16[2,2,4,8,16,2048]{5,4,3,2,1,0:T(8,128)(2,1)} %bitcas, ...), custom_call_target="tpu_custom_call" | custom-call | flops 26214400 | bytes 41943040 | tf_op jit(solution)/shard_map/pallas_call | solution.py:1900
  974.8 1.6 reduce_sum.111
  978.2 3.7 fusion.54
  981.9 2.9 copy.130
  984.8 2.9 copy.131
  987.7 3.3 copy.181
  (218 shorter events, 41.6 us)
Async XLA Ops:
  7.2 108.1 %copy-start = (s32[512,4]{0,1:T(4,128)S(1)}, s32[512,4]{0,1:T(4,128)}, u32[]{:S(2)}) copy-start(s32[512,4]{0,1:T(4,128)} %param.27) | copy-start | bytes 24580
  7.3 735.4 %all-gather.3.cloned.1.call-start = ((), (), s32[]{:S(2)}) async-start(), calls=%async_computation.1 | async-start | bytes 2621440 | tf_op jit(solution)/shard_map/all_gather | solution.py:2189
  113.9 10.7 %copy-start.10 = (bf16[4,2,272,512]{3,2,1,0:T(8,128)(2,1)}, bf16[4,2,272,512]{3,2,1,0:T(8,128)(2,1)S(1)}, u32[]{:S(2)}) copy-start(bf16[4,2,272,512]{3,2,1,0:T(8,128)(2,1)S(1)} %get-tuple-element.56.w_ref) | copy-start | bytes 6684676
  115.3 7.0 copy-start.39
  122.3 5.5 copy-start.17
  122.3 5.5 copy-start.28
  306.1 346.9 %copy-start.38 = (f32[1,2,8,128]{3,2,1,0:T(8,128)S(1)}, f32[1,2,8,128]{3,2,1,0:T(8,128)}, u32[]{:S(2)}) copy-start(f32[1,2,8,128]{3,2,1,0:T(8,128)} %get-tuple-element.110) | copy-start | bytes 24580
  306.1 346.9 %copy-start.40 = (bf16[1,2,8,128]{3,2,1,0:T(8,128)(2,1)S(1)}, bf16[1,2,8,128]{3,2,1,0:T(8,128)(2,1)}, u32[]{:S(2)}) copy-start(bf16[1,2,8,128]{3,2,1,0:T(8,128)(2,1)} %get-tuple-element.111) | copy-start | bytes 12292
  649.4 5.0 copy-start.37
  649.4 5.0 copy-start.15
  649.4 5.3 copy-start.14
  649.5 5.3 copy-start.46
  658.7 101.0 %all-gather.5.cloned.1.call-start = ((), (), s32[]{:S(2)}) async-start(), calls=%async_computation.2 | async-start | bytes 8912896 | tf_op jit(solution)/shard_map/all_gather | solution.py:2211
  658.7 4.4 copy-start.41
  663.3 12.5 %copy-start.6 = (f32[2048,128]{1,0:T(8,128)S(1)}, f32[2048,128]{1,0:T(8,128)}, u32[]{:S(2)}) copy-start(f32[2048,128]{1,0:T(8,128)} %get-tuple-element.71.o_ref) | copy-start | bytes 3145732
  675.8 3.6 copy-start.23
  675.8 3.8 copy-start.21
  675.8 4.0 copy-start.19
  675.9 4.1 copy-start.44
  677.1 4.1 copy-start.25
  759.7 6.0 copy-start.7
  759.7 6.0 copy-start.11
  759.7 6.0 copy-start.12
  759.7 6.0 copy-start.13
  794.0 37.1 %collective-permute-start = (bf16[2048,256]{1,0:T(8,128)(2,1)}, bf16[2048,256]{1,0:T(8,128)(2,1)}, u32[]{:S(2)}, u32[]{:S(2)}) collective-permute-start(bf16[2048,256]{1,0:T(8,128)(2,1)} %fusion.20), channel_id=1, source_target_pairs={{0,4},{4,0},{1,5},{5,1},{2,6},{6,2},{3,7},{7,3},{8,12},{12,8},{9,1... | collective-permute-start | bytes 3145736 | tf_op jit(solution)/shard_map/ppermute | solution.py:2240
  819.1 159.1 %all-to-all-start = ((bf16[8,528,256]{2,1,0:T(8,128)(2,1)}), bf16[8,528,256]{2,1,0:T(8,128)(2,1)}, u32[]{:S(2)}, u32[]{:S(2)}) async-start(bf16[8,528,256]{2,1,0:T(8,128)(2,1)} %get-tuple-element.84), calls=%async_computation | async-start | bytes 4325376 | tf_op jit(solution)/shard_map/all_to_all | solution.py:2225
  824.5 6.6 copy-start.16
  839.8 8.2 copy-start.30
  850.5 6.9 copy-start.4
  850.5 6.9 copy-start.5
  987.7 3.3 copy-start.24
  991.0 4.5 copy-start.1
  (26 other events, 52.3 us)
Sparse Core Ops, SparseCore 0:
  658.8 23.1 all-gather.2
  684.8 74.8 all-gather.4

commit v3 on v2

--- a/solution.py
+++ b/solution.py
@@ -584,10 +584,28 @@
 SAME_X = ("c", "y", "z")
 
 
-def front_kernel(own_ref, parts_ref, rows_ref, weights_ref, send, send_z, recv, send_w, recv_w, here):
+def front_kernel(
+    own_ref,
+    parts_ref,
+    leaving_ref,
+    rows_ref,
+    weights_ref,
+    all_ref,
+    send,
+    send_z,
+    recv,
+    send_w,
+    recv_w,
+    send_g,
+    recv_g,
+    here,
+):
     z, x, y, c = (lax.axis_index(name) for name in ALL_AXES)
     z_count = lax.axis_size("z")
     chunks = own_ref.shape[0]
+    half = own_ref.shape[2] // 2
+    left, right = pl.ds(0, half), pl.ds(half, leaving_ref.shape[2] - half)
+    flip = {"x": {"x": 1 - x}, "y": {"y": 1 - y}, "c": {"c": 1 - c}}
 
     def up(distance):
         return {"z": lax.rem(z + distance, z_count)}
@@ -608,11 +626,11 @@
 
     def spread_y(k):
         block = rows_ref.at[c, y, :, k]
-        return remote(block, block, send.at[0, k], recv.at[0, k], {"y": 1 - y})
+        return remote(block, block, send.at[0, k], recv.at[0, k], flip["y"])
 
     def spread_c(k):
         block = rows_ref.at[c, :, :, k]
-        return remote(block, block, send.at[1, k], recv.at[1, k], {"c": 1 - c})
+        return remote(block, block, send.at[1, k], recv.at[1, k], flip["c"])
 
     def weights_z(d):
         there = lax.rem(z + d, z_count)
@@ -622,57 +640,113 @@
 
     def weights_x():
         block = weights_ref.at[:, x]
-        return remote(block, block, send_w.at[0], recv_w.at[0], {"x": 1 - x})
+        return remote(block, block, send_w.at[0], recv_w.at[0], flip["x"])
+
+    def grads(slot, k, src, dst, device):
+        return remote(src, dst, send_g.at[slot, k], recv_g.at[slot, k], device)
+
+    def grads_z(k):
+        return [
+            grads(4 + d, k, leaving_ref.at[k], all_ref.at[c, y, x, z, k], up(d))
+            for d in range(1, 4)
+        ]
+
+    def grads_2(k):
+        a = all_ref.at[c, y, x, :, k, :, left]
+        b = all_ref.at[c, y, x, :, k, :, right]
+        return grads(0, k, a, a, flip["x"]), grads(1, k, b, b, flip["y"])
+
+    def grads_3(k):
+        a = all_ref.at[c, y, :, :, k, :, left]
+        b = all_ref.at[c, :, x, :, k, :, right]
+        return grads(2, k, a, a, flip["y"]), grads(3, k, b, b, flip["x"])
+
+    def grads_c(k):
+        a = all_ref.at[c, :, :, :, k]
+        return (grads(4, k, a, a, flip["c"]),)
+
+    def start(copies):
+        for copy in copies:
+            copy.start()
+
+    def finish(copies):
+        for copy in copies:
+            copy.wait()
 
     barrier = pltpu.get_barrier_semaphore()
-    for device in ({"x": 1 - x}, {"y": 1 - y}, {"c": 1 - c}, up(1), up(2), up(3)):
+    for device in (flip["x"], flip["y"], flip["c"], up(1), up(2), up(3)):
         pl.semaphore_signal(
             barrier, inc=1, device_id=device, device_id_type=pl.DeviceIdType.MESH
         )
-    keep = pltpu.make_async_copy(own_ref, rows_ref.at[c, y, z], here.at[0])
-    keep_w = pltpu.make_async_copy(parts_ref.at[z], weights_ref.at[z, x], here.at[1])
-    keep.start()
-    keep_w.start()
+    keep = [
+        pltpu.make_async_copy(own_ref, rows_ref.at[c, y, z], here.at[0]),
+        pltpu.make_async_copy(parts_ref.at[z], weights_ref.at[z, x], here.at[1]),
+        pltpu.make_async_copy(leaving_ref, all_ref.at[c, y, x, z], here.at[2]),
+    ]
+    start(keep)
     pl.semaphore_wait(barrier, 6)
+    def first_z(k):
+        return [spread_z(k, d) for d in range(1, 4)]
+
+    def all_weights_z():
+        return [weights_z(d) for d in range(1, 4)]
+
+    waiting = [first_z(k) for k in range(2, chunks)] + [grads_z(k) for k in range(chunks)]
+    start(first_z(0))
+    start(first_z(1))
+    finish(keep)
     for k in range(chunks):
-        for d in range(1, 4):
-            spread_z(k, d).start()
+        finish(first_z(k))
         if k == 0:
-            for d in range(1, 4):
-                weights_z(d).start()
-    keep.wait()
-    keep_w.wait()
-    for k in range(chunks):
-        for d in range(1, 4):
-            spread_z(k, d).wait()
+            start(all_weights_z())
+        start(waiting.pop(0))
         spread_y(k).start()
-        if k == 0:
-            for d in range(1, 4):
-                weights_z(d).wait()
+        if k == 2:
+            finish(all_weights_z())
             weights_x().start()
         if k > 0:
             spread_y(k - 1).wait()
             spread_c(k - 1).start()
-    spread_y(chunks - 1).wait()
-    spread_c(chunks - 1).start()
+    for k in range(chunks):
+        finish(grads_z(k))
+        if waiting:
+            start(waiting.pop(0))
+        start(grads_2(k))
+        if k == 0:
+            spread_y(chunks - 1).wait()
+            spread_c(chunks - 1).start()
+        if k > 0:
+            finish(grads_2(k - 1))
+            start(grads_3(k - 1))
+        if k > 1:
+            finish(grads_3(k - 2))
+            start(grads_c(k - 2))
+    finish(grads_2(chunks - 1))
+    start(grads_3(chunks - 1))
+    for k in (chunks - 2, chunks - 1):
+        finish(grads_3(k))
+        start(grads_c(k))
     for k in range(chunks):
         spread_c(k).wait()
+        finish(grads_c(k))
     weights_x().wait()
 
 
-def front(rows, parts, chunks=4):
+def front(rows, parts, leaving, chunks=4):
     own, model = rows.shape
+    wide = leaving.shape[1]
+    piece = own // chunks
     zs = lax.axis_size("z")
-    shape = (2, 2, zs, chunks, own // chunks, model)
     anywhere = pl.BlockSpec(memory_space=pl.ANY)
     dma = pltpu.SemaphoreType.DMA
-    gathered, weights = pl.pallas_call(
+    gathered, weights, spread = pl.pallas_call(
         front_kernel,
-        in_specs=[anywhere, anywhere],
-        out_specs=[anywhere, anywhere],
+        in_specs=[anywhere] * 3,
+        out_specs=[anywhere] * 3,
         out_shape=[
-            jax.ShapeDtypeStruct(shape, rows.dtype),
+            jax.ShapeDtypeStruct((2, 2, zs, chunks, piece, model), rows.dtype),
             jax.ShapeDtypeStruct((zs, 2) + parts.shape[1:], parts.dtype),
+            jax.ShapeDtypeStruct((2, 2, 2, zs, chunks, piece, wide), rows.dtype),
         ],
         scratch_shapes=[
             dma((2, chunks)),
@@ -680,13 +754,19 @@
             dma((5, chunks)),
             dma((4,)),
             dma((4,)),
-            dma((2,)),
+            dma((8, chunks)),
+            dma((8, chunks)),
+            dma((3,)),
         ],
         compiler_params=pltpu.CompilerParams(
             collective_id=0, has_side_effects=True, vmem_limit_bytes=16 * 2**20
         ),
-    )(rows.reshape(chunks, own // chunks, model), parts)
-    return gathered.reshape(4 * zs * own, model), weights
+    )(rows.reshape(chunks, piece, model), parts, leaving.reshape(chunks, piece, wide))
+    return (
+        gathered.reshape(4 * zs * own, model),
+        weights,
+        spread.reshape(8 * zs * own, wide),
+    )
 
 
 def middle_kernel(
@@ -695,7 +775,6 @@
     w_ref,
     row_ref,
     block_ref,
-    leaving_ref,
     sh_ref,
     q_ref,
     kv_ref,
@@ -703,12 +782,9 @@
     lse_ref,
     part_ref,
     joined_ref,
-    all_ref,
     shared_ref,
     peaks,
     totals,
-    send,
-    recv,
     once,
     once_in,
     here,
@@ -718,7 +794,6 @@
     z, x, y, c = (lax.axis_index(name) for name in ALL_AXES)
     z_count = lax.axis_size("z")
     e_count = 2 * z_count
-    chunks = leaving_ref.shape[0]
     head = HEAD_DIM
     count, model = rows_ref.shape
     block = model // e_count
@@ -738,30 +813,6 @@
             device_id=device,
             device_id_type=pl.DeviceIdType.MESH,
         )
-
-    def remote(slot, k, src, dst, device):
-        return copy_to(src, dst, send.at[slot, k], recv.at[slot, k], device)
-
-    def spread_z(k):
-        return [
-            remote(4 + d, k, leaving_ref.at[k], all_ref.at[c, y, x, z, k], up(d))
-            for d in range(1, 4)
-        ]
-
-    def spread_2(k):
-        a = all_ref.at[c, y, x, :, k]
-        return (remote(0, k, a, a, flip["x"]),)
-
-    def spread_3(k):
-        a = all_ref.at[c, y, :, :, k]
-        return (remote(1, k, a, a, flip["y"]),)
-
-    def spread_c(k):
-        copies = []
-        for j in range(2):
-            a = all_ref.at[c, j, :, :, k]
-            copies.append(remote(2 + j, k, a, a, flip["c"]))
-        return copies
 
     def share(d, other):
         z_to, x_to = lax.rem(z + d, z_count), 1 - x if other else x
@@ -792,11 +843,9 @@
         pl.semaphore_signal(
             barrier, inc=1, device_id=device, device_id_type=pl.DeviceIdType.MESH
         )
-    keep = pltpu.make_async_copy(leaving_ref, all_ref.at[c, y, x, z], here.at[0])
     keep_share = pltpu.make_async_copy(
-        sh_ref.at[2 * z + x], shared_ref.at[2 * z + x], here.at[1]
-    )
-    keep.start()
+        sh_ref.at[2 * z + x], shared_ref.at[2 * z + x], here.at[0]
+    )
     keep_share.start()
     for i in range(z_count):
         for j in range(2):
@@ -809,8 +858,6 @@
     lane = lax.broadcasted_iota(jnp.int32, (1, head), 1)
     sign = jnp.where(lane < head // 2, -1.0, 1.0)
     pl.semaphore_wait(barrier, 9)
-    for k in range(chunks):
-        start(spread_z(k))
     shares = [share(d, other) for d in range(4) for other in (False, True) if d or other]
 
     def project(t, carry):
@@ -834,9 +881,6 @@
     lax.fori_loop(0, count // tile, project, 0)
     key_values().start()
     start(shares)
-    keep.wait()
-    finish(spread_z(0))
-    start(spread_2(0))
     column = lax.broadcasted_iota(jnp.int32, (tile, rows), 1)
 
     def scan(i, side, blocks, carry):
@@ -880,10 +924,6 @@
         return carry
 
     lax.fori_loop(0, count // tile, first_pass, 0)
-    finish(spread_z(1))
-    start(spread_2(1))
-    finish(spread_2(0))
-    start(spread_3(0))
     key_values().wait()
 
     def second_pass(i, carry):
@@ -900,43 +940,17 @@
         for h in range(2):
             z_of, y_of, c_of = i // 2, lax.rem(i, 2), h
             part_ref[c_of * 8 + y_of * 4 + z_of] = part[h * own : (h + 1) * own]
-
-        @pl.when(i == 2)
-        def _():
-            finish(spread_z(2))
-            start(spread_2(2))
-            finish(spread_2(1))
-            start(spread_3(1))
-
-        @pl.when(i == 5)
-        def _():
-            finish(spread_z(3))
-            start(spread_2(3))
-            finish(spread_2(2))
-            start(spread_3(2))
-            finish(spread_3(0))
-            start(spread_c(0))
-
         return carry
 
     lax.fori_loop(0, count // tile, second_pass, 0)
-    finish(spread_2(3))
-    start(spread_3(3))
-    for k in range(1, chunks):
-        finish(spread_3(k))
-        start(spread_c(k))
-    for k in range(chunks):
-        finish(spread_c(k))
     finish(shares)
     keep_share.wait()
 
 
-def middle(length, gathered, weights, row_table, block_table, leaving, shared, rows, chunks=4):
-    own, wide = leaving.shape
+def middle(length, gathered, weights, row_table, block_table, shared, rows):
+    own = rows // 4
     count, model = gathered.shape
-    zs = lax.axis_size("z")
     head = HEAD_DIM
-    piece = own // chunks
     bf16, f32 = jnp.bfloat16, jnp.float32
     anywhere = pl.BlockSpec(memory_space=pl.ANY)
     inside = pl.BlockSpec(memory_space=pltpu.VMEM)
@@ -944,8 +958,8 @@
     shape = jax.ShapeDtypeStruct
     results = pl.pallas_call(
         functools.partial(middle_kernel, rows=rows),
-        in_specs=[pl.BlockSpec(memory_space=pltpu.SMEM)] + [inside] * 4 + [anywhere] * 2,
-        out_specs=[inside] * 6 + [anywhere] * 2,
+        in_specs=[pl.BlockSpec(memory_space=pltpu.SMEM)] + [inside] * 4 + [anywhere],
+        out_specs=[inside] * 6 + [anywhere],
         out_shape=[
             shape((count, head), bf16),
             shape((2, count, 2 * head), bf16),
@@ -953,17 +967,14 @@
             shape((count, head), f32),
             shape((count // own, own, model), bf16),
             shape((model, 4 * head), bf16),
-            shape((2, 2, 2, zs, chunks, piece, wide), bf16),
             shape(shared.shape, bf16),
         ],
         scratch_shapes=[
             vm((count, head), f32),
             vm((count, head), f32),
-            dma((8, chunks)),
-            dma((8, chunks)),
             dma((8,)),
             dma((8,)),
-            dma((2,)),
+            dma((1,)),
         ],
         compiler_params=pltpu.CompilerParams(
             collective_id=3, has_side_effects=True, vmem_limit_bytes=56 * 2**20
@@ -977,10 +988,9 @@
         weights,
         row_table,
         block_table,
-        leaving.reshape(chunks, piece, wide),
         shared,
     )
-    query, key_values, attended, log_total, partial, joined, spread, shared = results
+    query, key_values, attended, log_total, partial, joined, shared = results
     return (
         query,
         key_values,
@@ -988,7 +998,6 @@
         log_total,
         partial.reshape(count, model),
         joined,
-        spread.reshape(8 * zs * own, wide),
         shared,
     )
 
@@ -1397,7 +1406,8 @@
         dgu_buf[part, :, :, :, :, width:] = grad_up.reshape(shape + (width,))
         pa[slot, part] = mixture[:, :cut].reshape(shape + (cut,))
         rest = model - cut
-        pb[slot, part, :, :, :, :, :rest] = mixture[:, cut:].reshape(shape + (rest,))
+        if rest:
+            pb[slot, part, :, :, :, :, :rest] = mixture[:, cut:].reshape(shape + (rest,))
         pb[slot, part, :, :, :, :, rest : rest + model] = pushed.reshape(shape + (model,))
         pb[slot, part, :, :, :, :, rest + model :] = gate_sums.reshape(shape + (128,))
 
@@ -1516,7 +1526,7 @@
     partial = partial.reshape((2, 2, zs, chunks, piece, model))
     grads = grads.reshape(lead + (chunks, piece, model + 128))
     tokens = tokens.reshape(chunks, piece, model)
-    cut = model // 2
+    cut = model
     extra = 2 * model + 128 - cut
     bf16 = jnp.bfloat16
     shapes = [
@@ -2000,6 +2010,34 @@
     )(normed, grads, slopes, scaled)
 
 
+def head_grads_kernel(first_ref, hidden_ref, qkv_ref, att_ref, out_ref):
+    wide = qkv_ref.shape[1]
+    out_ref[0, 0, :, :wide] = product_at(first_ref[...], qkv_ref[...]).astype(jnp.bfloat16)
+    out_ref[0, 0, :, wide:] = product_at(hidden_ref[...], att_ref[...]).astype(jnp.bfloat16)
+
+
+def head_grads(first, hidden, grad_qkv, attended, block):
+    count, model = first.shape
+    wide = grad_qkv.shape[1] + attended.shape[1]
+    blocks = model // block
+    return pl.pallas_call(
+        head_grads_kernel,
+        grid=(blocks,),
+        in_specs=[
+            pl.BlockSpec((count, block), lambda i: (0, i)),
+            pl.BlockSpec((count, block), lambda i: (0, i)),
+            pl.BlockSpec(grad_qkv.shape, lambda i: (0, 0)),
+            pl.BlockSpec(attended.shape, lambda i: (0, 0)),
+        ],
+        out_specs=pl.BlockSpec((1, 1, block, wide), lambda i: (i % 2, i // 2, 0, 0)),
+        out_shape=jax.ShapeDtypeStruct((2, blocks // 2, block, wide), jnp.bfloat16),
+        compiler_params=pltpu.CompilerParams(vmem_limit_bytes=32 * 2**20),
+        cost_estimate=pl.CostEstimate(
+            flops=2 * count * model * wide, bytes_accessed=5 * count * model, transcendentals=0
+        ),
+    )(first, hidden, grad_qkv, attended)
+
+
 def packed(
     tokens,
     cotangent,
@@ -2070,9 +2108,6 @@
         ],
         axis=1,
     )
-    first_half, arrived_weights = front(normed_first, attn_parts)
-    small = arrived_weights[:, :, block + 1 :].reshape(exp_count, 15 * 4 * head)
-
     own_first = exp_index * rows + tp_index * own
     own_positions = own_first + jnp.arange(own, dtype=jnp.int32)
     valid = (own_positions < length).astype(f32)[:, None]
@@ -2082,6 +2117,8 @@
         [grad_out_low, jnp.pad(own_routes.astype(bf16), ((0, 0), (0, 124)), constant_values=-1.0)],
         axis=1,
     )
+    first_half, arrived_weights, grad_all = front(normed_first, attn_parts, leaving)
+    small = arrived_weights[:, :, block + 1 :].reshape(exp_count, 15 * 4 * head)
     shared_parts = jnp.concatenate(
         [
             w.reshape(exp_count, shared_units, block)
@@ -2137,14 +2174,13 @@
         )
 
     flip = [(0, 1), (1, 0)]
-    query_rot, key_values, attended, log_total, attn_part, attn_weights, grad_all, shared_parts = (
+    query_rot, key_values, attended, log_total, attn_part, attn_weights, shared_parts = (
         middle(
             lengths,
             first_half,
             arrived_weights,
             jnp.asarray(row_table),
             jnp.asarray(block_table),
-            leaving,
             shared_parts,
             rows,
         )
@@ -2231,7 +2267,6 @@
     )
     d_shared_gate, d_shared_up = d_shared_gate.T, d_shared_up.T
     grad_attended = product(hidden_half, out_weight).astype(bf16)
-    d_out_weight = product_at(attended_low, hidden_half)
     scale = 1.0 / head**0.5
     grad_query, grad_key, grad_value = attend_back(
         info, query_rot, key_values, by_position(grad_attended), attended, log_total, rows
@@ -2249,7 +2284,7 @@
         ],
         axis=1,
     ).astype(bf16)
-    d_attn = jnp.concatenate([product_at(grad_qkv, first_half), d_out_weight]).astype(bf16)
+    d_attn = head_grads(first_half, hidden_half, grad_qkv, attended_low, block)
     d_biases = jnp.sum(grad_qkv.astype(f32), axis=0).astype(bf16).reshape(3, 2, head // 2)
     d_biases = jnp.pad(
         d_biases.transpose(1, 0, 2).reshape(2, 1, 3 * head // 2),
@@ -2262,7 +2297,7 @@
         product_bt(grad_qkv, attn_weights[:, : 3 * head]).astype(bf16),
         grad_hidden,
         my_rows(tokens),
-        d_attn.reshape(4 * head, heads_z, 2, block).transpose(2, 1, 3, 0),
+        d_attn,
         d_biases,
         raw,
         extras,

time: 1010 us -> 963 us (0.953)
  Pallas kernels: 819 us -> 789 us
  local copies, waits for them, and re-layouts: 77.4 us -> 58.4 us
  waiting for transfers between devices: 17 us -> 34.3 us
  matrix products: 33.5 us -> 18.6 us
    pallas_call x1, Pallas kernels: 177 us -> 87.7 us  [middle(): pl.pallas_call(functools.partial(middle_kernel, rows=rows), in_specs=[pl....]
    pallas_call x1 -> x2, Pallas kernels: 98.8 us -> 181 us  [the longest x1 170 us: front(): pl.pallas_call(front_kernel, in_specs=[anywhere] * 3, out_specs=[anywhere...]
    ppermute x1, waiting for transfers between devices: 0.01 us -> 26.1 us  [packed(): away = lax.ppermute(grad_kv[1], 'x', flip)]
    dot_general x3 -> x1, local copies, waits for them, and re-layouts: 26 us -> 0.3 us  [product_at(): lax.dot_general(left, right, (((0,), (0,)), ((), ())), preferred_element_...]
    pallas_call x1, Pallas kernels: 343 us -> 320 us  [stream(): pl.pallas_call(functools.partial(stream_kernel, units=units, experts=expe...]
    dot_general x3 -> x1, matrix products: 15.2 us -> 0.37 us  [product_at(): lax.dot_general(left, right, (((0,), (0,)), ((), ())), preferred_element_...]
    unnamed x127 -> x132, local copies, waits for them, and re-layouts: 15.8 us -> 30.6 us
  transfers between devices with their start and end apart: 4 -> 4, of which waited for: 1 -> 2; matrix products, arithmetic and copies ran while one was open for 8% -> 4% of each run, Pallas kernels for 17% -> 22%
where the time goes in v3:
time: 963 us; the launch traced here: 956 us
  Pallas kernels  789 us (82%)
  local copies, waits for them, and re-layouts  58.4 us (6%)
  waiting for transfers between devices  34.3 us (4%)
  other arithmetic  23.7 us (2%)
  between operations  20 us (2%)
  matrix products  18.6 us (2%)
  starting transfers between devices  12.1 us (1%)
    pallas_call x1, Pallas kernels, stream(): pl.pallas_call(functools.partial(stream_kernel, units=units, experts=expe...  320 us
    pallas_call x1, Pallas kernels, front(): pl.pallas_call(front_kernel, in_specs=[anywhere] * 3, out_specs=[anywhere...  170 us
    pallas_call x1, Pallas kernels, finish(): pl.pallas_call(finish_kernel, in_specs=[inside] * 8, out_specs=[anywhere]...  114 us
    pallas_call x1, Pallas kernels, middle(): pl.pallas_call(functools.partial(middle_kernel, rows=rows), in_specs=[pl....  87.7 us
    pallas_call x1, Pallas kernels, weight_grads(): pl.pallas_call(functools.partial(weight_grads_kernel, units=units, share=...  60.4 us
    unnamed x132, local copies, waits for them, and re-layouts  30.6 us
    ppermute x1, waiting for transfers between devices, packed(): away = lax.ppermute(grad_kv[1], 'x', flip)  26.1 us
    pallas_call x1, Pallas kernels, attend_back(): pl.pallas_call(functools.partial(attend_back_kernel, tile=tile, keys=rows...  25.7 us
  transfers between devices with their start and end apart: 4, of which 2 were waited for; matrix products, arithmetic and copies ran while one was open for 4% of the time, Pallas kernels for 22%

profile of v3, /device:TPU:0, one launch (start us, length us, event | category | flops | bytes accessed | tf_op | source)
XLA Modules:
  0.0 955.6 jit_solution(4695166791030449336)
XLA Ops:
  8.1 1.4 fusion.7
  12.0 170.0 %shard_map.391 = (bf16[2,2,4,4,32,2048]{5,4,3,2,1,0:T(8,128)(2,1)S(1)}, bf16[4,2,272,512]{3,2,1,0:T(8,128)(2,1)S(1)}, bf16[2,2,2,4,4,32,2176]{6,5,4,3,2,1,0:T(8,128)(2,1)S(1)}) custom-call(bf16[4,32,2048]{2,1,0:T(8,128)(2,1)S(1)} %bitcast.209, bf16[4,272,512]{2,1,0:T(8,128)(2,1)S(1)} %pad_maximum_fusion.2.parts_ref, bf16[4,32,2176]{2,1,0:T(8,128)(2,1)S(1)} %bitcast.207), custom_call_target="tpu_custom_call" | custom-call | tf_op jit(solution)/shard_map/pallas_call | solution.py:742
  182.0 3.2 copy-done.3
  185.2 6.1 copy-done.15
  195.5 2.2 copy.161
  199.7 1.5 pad_maximum_fusion.4.router_ref
  201.3 1.7 fusion.22.s_ref
  203.0 2.8 pad_maximum_fusion.sh_ref
  205.8 87.7 %shard_map.392 = (bf16[2048,128]{1,0:T(8,128)(2,1)}, bf16[2,2048,256]{2,1,0:T(8,128)(2,1)}, f32[2048,128]{1,0:T(8,128)}, f32[2048,128]{1,0:T(8,128)}, bf16[16,12...) custom-call(s32[1]{0:T(128)} %copy.208.length_ref, bf16[2048,2048]{1,0:T(8,128)(2,1)} %bitcast.202, ...), custom_call_target="tpu_custom_call" | custom-call | flops 5368709120 | bytes 62914560 | tf_op jit(solution)/shard_map/pallas_call | solution.py:959
  293.5 320.1 %shard_map.393 = (bf16[2,2,2,4,8,16,2048]{6,5,4,3,2,1,0:T(8,128)(2,1)}, bf16[2,2,2,4,8,16,896]{6,5,4,3,2,1,0:T(8,128)(2,1)}, bf16[2,2,2,4,8,16,1792]{6,5,4,3,2,1...) custom-call(bf16[2,2,4,8,16,2048]{5,4,3,2,1,0:T(8,128)(2,1)} %bitcas, ...), custom_call_target="tpu_custom_call" | custom-call | flops 90194313216 | bytes 139460608 | tf_op jit(solution)/shard_map/pallas_call | solution.py:1594
  613.7 1.4 fusion.45
  620.3 3.7 multiply_reduce_fusion.1
  626.0 60.4 %shard_map.394 = (f32[2,352,2048]{2,1,0:T(8,128)}, f32[2,352,2048]{2,1,0:T(8,128)}, f32[2,352,2048]{2,1,0:T(8,128)}, bf16[8,528,256]{2,1,0:T(8,128)(2,1)}) custom-call(bf16[4096,2048]{1,0:T(8,128)(2,1)} %bitcast.276, bf16[4096,2176]{1,0:T(8,128)(2,1)} %bitcast.213, bf16[4096,1792]{1,0:T(8,128)(2,1)} %bitcast.277, bf16[4096,896]{1,0:T(8,128)(2,1)} %bitcast.279), custom_call_target="tpu_custom_call" | custom-call | flops 45097156608 | bytes 77594624 | tf_op jit(solution)/shard_map/pallas_call | solution.py:1992
  690.7 1.6 multiply_subtract_fusion
  692.3 7.5 all-gather.5.cloned.1.call-done.hidden_ref
  699.8 5.9 convolution_convert_fusion.1
  705.8 25.7 %shard_map.395 = (f32[2048,128]{1,0:T(8,128)S(1)}, f32[2,2048,128]{2,1,0:T(8,128)S(1)}, f32[2,2048,128]{2,1,0:T(8,128)S(1)}) custom-call(s32[2]{0:T(128)S(1)} %pad_add_fusion.info_ref, bf16[2048,128]{1,0:T(8,128)(2,1)S(1)} %copy-done.18, bf16[2,2048,256]{2,1,0:T(8,128)(2,1)S(1)} %copy-done.16, bf16[2048,128]{1,0:T(8,128)(2,1)S(1)} %bitcast.211, ...), custom_call_target="tpu_custom_call" | custom-call | flops 5368709120 | bytes 12582912 | tf_op jit(solution)/shard_map/pallas_call | solution.py:561
  734.3 7.4 collective-permute-start
  743.7 2.3 copy.167
  746.1 4.6 all-to-all-start
  752.1 26.1 %collective-permute-done = bf16[2048,256]{1,0:T(8,128)(2,1)} collective-permute-done((bf16[2048,256]{1,0:T(8,128)(2,1)}, bf16[2048,256]{1,0:T(8,128)(2,1)}, u32[]{:S(2)}, u32[]{:S(2)}) %collective-permute-start) | collective-permute-done | bytes 1048608 | tf_op jit(solution)/shard_map/ppermute | solution.py:2275
  778.2 1.4 maximum_add_fusion
  783.9 3.4 copy-done.4
  787.2 3.4 copy-done.5
  790.6 11.0 %shard_map.396.wp_ref = bf16[2,4,256,512]{3,2,1,0:T(8,128)(2,1)S(1)} custom-call(bf16[2048,2048]{1,0:T(8,128)(2,1)S(1)} %bitcast.203, bf16[2048,2048]{1,0:T(8,128)(2,1)S(1)} %copy-done.5, bf16[2048,384]{1,0:T(8,128)(2,1)S(1)} %get-tuple-element.93.qkv_ref, bf16[2048,128]{1,0:T(8,128)(2,1)S(1)} %bitcast.208), custom_call_target="tpu_custom_call" | custom-call | flops 4294967296 | bytes 20971520 | tf_op jit(solution)/shard_map/pallas_call | solution.py:2023
  801.6 7.0 convolution_convert_fusion
  808.6 113.6 %shard_map.397 = (bf16[2,2,8,16,2048]{4,3,2,1,0:T(8,128)(2,1)}, f32[256,512]{1,0:T(8,128)S(1)}, f32[256,512]{1,0:T(8,128)S(1)}, f32[256,512]{1,0:T(8,128)S(1)}, ...) custom-call(bf16[2,2,4,8,16,2048]{5,4,3,2,1,0:T(8,128)(2,1)} %bitcas, ...), custom_call_target="tpu_custom_call" | custom-call | flops 26214400 | bytes 41943040 | tf_op jit(solution)/shard_map/pallas_call | solution.py:1910
  925.4 1.6 reduce_sum.111
  928.7 3.7 fusion.43
  932.5 2.9 copy.183
  935.4 2.9 copy.184
  938.3 3.3 copy.209
  (216 shorter events, 38.1 us)
Async XLA Ops:
  7.3 692.4 %all-gather.5.cloned.1.call-start = ((), (), s32[]{:S(2)}) async-start(), calls=%async_computation.2 | async-start | bytes 8912896 | tf_op jit(solution)/shard_map/all_gather | solution.py:2247
  185.2 6.1 copy-start.15
  191.4 9.9 %copy-start.14 = (bf16[4,2,272,512]{3,2,1,0:T(8,128)(2,1)}, bf16[4,2,272,512]{3,2,1,0:T(8,128)(2,1)S(1)}, u32[]{:S(2)}) copy-start(bf16[4,2,272,512]{3,2,1,0:T(8,128)(2,1)S(1)} %get-tuple-element.56.w_ref) | copy-start | bytes 6684676
  293.5 320.2 %copy-start.39 = (bf16[2,8,8,256]{3,1,2,0:T(8,128)(2,1)S(1)}, bf16[2,8,8,256]{3,1,2,0:T(8,128)(2,1)}, u32[]{:S(2)}) copy-start(bf16[2,8,8,256]{3,1,2,0:T(8,128)(2,1)} %copy.193) | copy-start | bytes 196612
  613.6 6.4 copy-start.42
  613.6 6.4 copy-start.43
  613.7 6.4 copy-start.20
  613.7 6.7 copy-start.23
  613.7 6.7 copy-start.49
  620.3 3.7 copy-start.24
  625.2 118.5 %all-gather.3.cloned.1.call-start = ((), (), s32[]{:S(2)}) async-start(), calls=%async_computation.1 | async-start | bytes 2621440 | tf_op jit(solution)/shard_map/all_gather | solution.py:2225
  626.0 61.6 %copy-start.30 = (bf16[256,512]{0,1:T(8,128)(2,1)S(1)}, bf16[256,512]{0,1:T(8,128)(2,1)}, u32[]{:S(2)}) copy-start(bf16[256,512]{0,1:T(8,128)(2,1)} %copy-done.29) | copy-start | bytes 786436
  626.0 62.5 %copy-start.28 = (bf16[256,512]{0,1:T(8,128)(2,1)S(1)}, bf16[256,512]{0,1:T(8,128)(2,1)}, u32[]{:S(2)}) copy-start(bf16[256,512]{0,1:T(8,128)(2,1)} %copy-done.27) | copy-start | bytes 786436
  686.4 3.8 copy-start.44
  686.4 4.3 copy-start.40
  686.4 4.3 copy-start.41
  699.8 6.0 copy-start.11
  699.8 6.0 copy-start.16
  699.8 6.0 copy-start.17
  699.8 6.0 copy-start.18
  733.2 8.5 copy-start.32
  733.2 8.5 copy-start.33
  733.2 8.5 copy-start.34
  734.3 9.3 copy-start.47
  734.3 43.9 %collective-permute-start = (bf16[2048,256]{1,0:T(8,128)(2,1)}, bf16[2048,256]{1,0:T(8,128)(2,1)}, u32[]{:S(2)}, u32[]{:S(2)}) collective-permute-start(bf16[2048,256]{1,0:T(8,128)(2,1)} %fusion.9), channel_id=1, source_target_pairs={{0,4},{4,0},{1,5},{5,1},{2,6},{6,2},{3,7},{7,3},{8,12},{12,8},{9,1... | collective-permute-start | bytes 3145736 | tf_op jit(solution)/shard_map/ppermute | solution.py:2275
  746.1 182.7 %all-to-all-start = ((bf16[8,528,256]{2,1,0:T(8,128)(2,1)}), bf16[8,528,256]{2,1,0:T(8,128)(2,1)}, u32[]{:S(2)}, u32[]{:S(2)}) async-start(bf16[8,528,256]{2,1,0:T(8,128)(2,1)} %get-tuple-element.84), calls=%async_computation | async-start | bytes 4325376 | tf_op jit(solution)/shard_map/all_to_all | solution.py:2261
  783.9 3.4 copy-start.4
  790.6 11.0 %copy-start.56 = (bf16[2048,512]{1,0:T(8,128)(2,1)S(1)}, bf16[2048,512]{1,0:T(8,128)(2,1)}, u32[]{:S(2)}) copy-start(bf16[2048,512]{1,0:T(8,128)(2,1)} %get-tuple-element.70) | copy-start | bytes 6291460
  801.6 7.0 copy-start.2
  801.6 7.0 copy-start.8
  801.6 7.0 copy-start.9
  941.6 4.5 copy-start.1
  (29 other events, 61.4 us)
Sparse Core Ops, SparseCore 0:
  625.3 74.3 all-gather.4
  701.9 20.8 all-gather.2

commit v4 on v3

--- a/solution.py
+++ b/solution.py
@@ -691,36 +691,34 @@
     def all_weights_z():
         return [weights_z(d) for d in range(1, 4)]
 
-    waiting = [first_z(k) for k in range(2, chunks)] + [grads_z(k) for k in range(chunks)]
     start(first_z(0))
-    start(first_z(1))
+    start(grads_z(0))
     finish(keep)
     for k in range(chunks):
         finish(first_z(k))
-        if k == 0:
-            start(all_weights_z())
-        start(waiting.pop(0))
+        if k + 1 < chunks:
+            start(first_z(k + 1))
         spread_y(k).start()
-        if k == 2:
+        if k == 1:
             finish(all_weights_z())
             weights_x().start()
         if k > 0:
             spread_y(k - 1).wait()
             spread_c(k - 1).start()
-    for k in range(chunks):
         finish(grads_z(k))
-        if waiting:
-            start(waiting.pop(0))
+        if k == 0:
+            start(all_weights_z())
+        if k + 1 < chunks:
+            start(grads_z(k + 1))
         start(grads_2(k))
-        if k == 0:
-            spread_y(chunks - 1).wait()
-            spread_c(chunks - 1).start()
         if k > 0:
             finish(grads_2(k - 1))
             start(grads_3(k - 1))
         if k > 1:
             finish(grads_3(k - 2))
             start(grads_c(k - 2))
+    spread_y(chunks - 1).wait()
+    spread_c(chunks - 1).start()
     finish(grads_2(chunks - 1))
     start(grads_3(chunks - 1))
     for k in (chunks - 2, chunks - 1):

time: 963 us -> 954 us (level)
  Pallas kernels: 789 us -> 779 us
    pallas_call x1, Pallas kernels: 87.7 us -> 76.5 us  [middle(): pl.pallas_call(functools.partial(middle_kernel, rows=rows), in_specs=[pl....]
where the time goes in v4:
time: 954 us; the launch traced here: 947 us
  Pallas kernels  779 us (82%)
  local copies, waits for them, and re-layouts  58.4 us (6%)
  waiting for transfers between devices  35.3 us (4%)
  other arithmetic  23.7 us (2%)
  between operations  20 us (2%)
  matrix products  18.6 us (2%)
  starting transfers between devices  12.1 us (1%)
    pallas_call x1, Pallas kernels, stream(): pl.pallas_call(functools.partial(stream_kernel, units=units, experts=expe...  320 us
    pallas_call x1, Pallas kernels, front(): pl.pallas_call(front_kernel, in_specs=[anywhere] * 3, out_specs=[anywhere...  172 us
    pallas_call x1, Pallas kernels, finish(): pl.pallas_call(finish_kernel, in_specs=[inside] * 8, out_specs=[anywhere]...  114 us
    pallas_call x1, Pallas kernels, middle(): pl.pallas_call(functools.partial(middle_kernel, rows=rows), in_specs=[pl....  76.5 us
    pallas_call x1, Pallas kernels, weight_grads(): pl.pallas_call(functools.partial(weight_grads_kernel, units=units, share=...  60.2 us
    unnamed x132, local copies, waits for them, and re-layouts  30.6 us
    ppermute x1, waiting for transfers between devices, packed(): away = lax.ppermute(grad_kv[1], 'x', flip)  26.1 us
    pallas_call x1, Pallas kernels, attend_back(): pl.pallas_call(functools.partial(attend_back_kernel, tile=tile, keys=rows...  25.7 us
  transfers between devices with their start and end apart: 4, of which 2 were waited for; matrix products, arithmetic and copies ran while one was open for 4% of the time, Pallas kernels for 22%

profile of v4, /device:TPU:0, one launch (start us, length us, event | category | flops | bytes accessed | tf_op | source)
XLA Modules:
  0.0 947.1 jit_solution(14621243179283614359)
XLA Ops:
  8.1 1.4 fusion.7
  12.0 171.8 %shard_map.391 = (bf16[2,2,4,4,32,2048]{5,4,3,2,1,0:T(8,128)(2,1)S(1)}, bf16[4,2,272,512]{3,2,1,0:T(8,128)(2,1)S(1)}, bf16[2,2,2,4,4,32,2176]{6,5,4,3,2,1,0:T(8,128)(2,1)S(1)}) custom-call(bf16[4,32,2048]{2,1,0:T(8,128)(2,1)S(1)} %bitcast.209, bf16[4,272,512]{2,1,0:T(8,128)(2,1)S(1)} %pad_maximum_fusion.2.parts_ref, bf16[4,32,2176]{2,1,0:T(8,128)(2,1)S(1)} %bitcast.207), custom_call_target="tpu_custom_call" | custom-call | tf_op jit(solution)/shard_map/pallas_call | solution.py:740
  183.8 3.2 copy-done.3
  187.0 6.1 copy-done.15
  197.4 2.2 copy.161
  201.6 1.5 pad_maximum_fusion.4.router_ref
  203.1 1.7 fusion.22.s_ref
  204.8 2.8 pad_maximum_fusion.sh_ref
  207.6 76.5 %shard_map.392 = (bf16[2048,128]{1,0:T(8,128)(2,1)}, bf16[2,2048,256]{2,1,0:T(8,128)(2,1)}, f32[2048,128]{1,0:T(8,128)}, f32[2048,128]{1,0:T(8,128)}, bf16[16,12...) custom-call(s32[1]{0:T(128)} %copy.208.length_ref, bf16[2048,2048]{1,0:T(8,128)(2,1)} %bitcast.202, ...), custom_call_target="tpu_custom_call" | custom-call | flops 5368709120 | bytes 62914560 | tf_op jit(solution)/shard_map/pallas_call | solution.py:957
  284.1 320.1 %shard_map.393 = (bf16[2,2,2,4,8,16,2048]{6,5,4,3,2,1,0:T(8,128)(2,1)}, bf16[2,2,2,4,8,16,896]{6,5,4,3,2,1,0:T(8,128)(2,1)}, bf16[2,2,2,4,8,16,1792]{6,5,4,3,2,1...) custom-call(bf16[2,2,4,8,16,2048]{5,4,3,2,1,0:T(8,128)(2,1)} %bitcas, ...), custom_call_target="tpu_custom_call" | custom-call | flops 90194313216 | bytes 139460608 | tf_op jit(solution)/shard_map/pallas_call | solution.py:1592
  604.2 1.4 fusion.45
  610.9 3.7 multiply_reduce_fusion.1
  616.5 60.2 %shard_map.394 = (f32[2,352,2048]{2,1,0:T(8,128)}, f32[2,352,2048]{2,1,0:T(8,128)}, f32[2,352,2048]{2,1,0:T(8,128)}, bf16[8,528,256]{2,1,0:T(8,128)(2,1)}) custom-call(bf16[4096,2048]{1,0:T(8,128)(2,1)} %bitcast.276, bf16[4096,2176]{1,0:T(8,128)(2,1)} %bitcast.213, bf16[4096,1792]{1,0:T(8,128)(2,1)} %bitcast.277, bf16[4096,896]{1,0:T(8,128)(2,1)} %bitcast.279), custom_call_target="tpu_custom_call" | custom-call | flops 45097156608 | bytes 77594624 | tf_op jit(solution)/shard_map/pallas_call | solution.py:1990
  681.1 1.6 multiply_subtract_fusion
  682.7 8.5 all-gather.5.cloned.1.call-done.hidden_ref
  691.2 5.9 convolution_convert_fusion.1
  697.2 25.7 %shard_map.395 = (f32[2048,128]{1,0:T(8,128)S(1)}, f32[2,2048,128]{2,1,0:T(8,128)S(1)}, f32[2,2048,128]{2,1,0:T(8,128)S(1)}) custom-call(s32[2]{0:T(128)S(1)} %pad_add_fusion.info_ref, bf16[2048,128]{1,0:T(8,128)(2,1)S(1)} %copy-done.18, bf16[2,2048,256]{2,1,0:T(8,128)(2,1)S(1)} %copy-done.16, bf16[2048,128]{1,0:T(8,128)(2,1)S(1)} %bitcast.211, ...), custom_call_target="tpu_custom_call" | custom-call | flops 5368709120 | bytes 12582912 | tf_op jit(solution)/shard_map/pallas_call | solution.py:561
  725.7 7.4 collective-permute-start
  735.2 2.3 copy.167
  737.5 4.6 all-to-all-start
  743.5 26.1 %collective-permute-done = bf16[2048,256]{1,0:T(8,128)(2,1)} collective-permute-done((bf16[2048,256]{1,0:T(8,128)(2,1)}, bf16[2048,256]{1,0:T(8,128)(2,1)}, u32[]{:S(2)}, u32[]{:S(2)}) %collective-permute-start) | collective-permute-done | bytes 1048608 | tf_op jit(solution)/shard_map/ppermute | solution.py:2273
  769.6 1.4 maximum_add_fusion
  775.3 3.4 copy-done.4
  778.7 3.4 copy-done.5
  782.1 11.0 %shard_map.396.wp_ref = bf16[2,4,256,512]{3,2,1,0:T(8,128)(2,1)S(1)} custom-call(bf16[2048,2048]{1,0:T(8,128)(2,1)S(1)} %bitcast.203, bf16[2048,2048]{1,0:T(8,128)(2,1)S(1)} %copy-done.5, bf16[2048,384]{1,0:T(8,128)(2,1)S(1)} %get-tuple-element.93.qkv_ref, bf16[2048,128]{1,0:T(8,128)(2,1)S(1)} %bitcast.208), custom_call_target="tpu_custom_call" | custom-call | flops 4294967296 | bytes 20971520 | tf_op jit(solution)/shard_map/pallas_call | solution.py:2021
  793.1 7.0 convolution_convert_fusion
  800.0 113.7 %shard_map.397 = (bf16[2,2,8,16,2048]{4,3,2,1,0:T(8,128)(2,1)}, f32[256,512]{1,0:T(8,128)S(1)}, f32[256,512]{1,0:T(8,128)S(1)}, f32[256,512]{1,0:T(8,128)S(1)}, ...) custom-call(bf16[2,2,4,8,16,2048]{5,4,3,2,1,0:T(8,128)(2,1)} %bitcas, ...), custom_call_target="tpu_custom_call" | custom-call | flops 26214400 | bytes 41943040 | tf_op jit(solution)/shard_map/pallas_call | solution.py:1908
  916.9 1.6 reduce_sum.111
  920.3 3.7 fusion.43
  924.0 2.9 copy.183
  926.9 2.9 copy.184
  929.8 3.3 copy.209
  (216 shorter events, 38.1 us)
Async XLA Ops:
  7.3 683.9 %all-gather.5.cloned.1.call-start = ((), (), s32[]{:S(2)}) async-start(), calls=%async_computation.2 | async-start | bytes 8912896 | tf_op jit(solution)/shard_map/all_gather | solution.py:2245
  187.0 6.1 copy-start.15
  193.2 9.9 %copy-start.14 = (bf16[4,2,272,512]{3,2,1,0:T(8,128)(2,1)}, bf16[4,2,272,512]{3,2,1,0:T(8,128)(2,1)S(1)}, u32[]{:S(2)}) copy-start(bf16[4,2,272,512]{3,2,1,0:T(8,128)(2,1)S(1)} %get-tuple-element.56.w_ref) | copy-start | bytes 6684676
  284.1 320.2 %copy-start.39 = (bf16[2,8,8,256]{3,1,2,0:T(8,128)(2,1)S(1)}, bf16[2,8,8,256]{3,1,2,0:T(8,128)(2,1)}, u32[]{:S(2)}) copy-start(bf16[2,8,8,256]{3,1,2,0:T(8,128)(2,1)} %copy.193) | copy-start | bytes 196612
  604.2 6.4 copy-start.42
  604.2 6.4 copy-start.43
  604.2 6.4 copy-start.20
  604.2 6.7 copy-start.23
  604.2 6.7 copy-start.49
  610.8 3.7 copy-start.24
  615.7 119.4 %all-gather.3.cloned.1.call-start = ((), (), s32[]{:S(2)}) async-start(), calls=%async_computation.1 | async-start | bytes 2621440 | tf_op jit(solution)/shard_map/all_gather | solution.py:2223
  616.5 61.5 %copy-start.30 = (bf16[256,512]{0,1:T(8,128)(2,1)S(1)}, bf16[256,512]{0,1:T(8,128)(2,1)}, u32[]{:S(2)}) copy-start(bf16[256,512]{0,1:T(8,128)(2,1)} %copy-done.29) | copy-start | bytes 786436
  616.5 62.3 %copy-start.28 = (bf16[256,512]{0,1:T(8,128)(2,1)S(1)}, bf16[256,512]{0,1:T(8,128)(2,1)}, u32[]{:S(2)}) copy-start(bf16[256,512]{0,1:T(8,128)(2,1)} %copy-done.27) | copy-start | bytes 786436
  676.7 3.8 copy-start.44
  676.7 4.3 copy-start.40
  676.7 4.3 copy-start.41
  691.2 6.0 copy-start.11
  691.2 6.0 copy-start.16
  691.2 6.0 copy-start.17
  691.2 6.0 copy-start.18
  724.6 8.5 copy-start.32
  724.6 8.5 copy-start.33
  724.6 8.5 copy-start.34
  725.7 9.3 copy-start.47
  725.7 43.9 %collective-permute-start = (bf16[2048,256]{1,0:T(8,128)(2,1)}, bf16[2048,256]{1,0:T(8,128)(2,1)}, u32[]{:S(2)}, u32[]{:S(2)}) collective-permute-start(bf16[2048,256]{1,0:T(8,128)(2,1)} %fusion.9), channel_id=1, source_target_pairs={{0,4},{4,0},{1,5},{5,1},{2,6},{6,2},{3,7},{7,3},{8,12},{12,8},{9,1... | collective-permute-start | bytes 3145736 | tf_op jit(solution)/shard_map/ppermute | solution.py:2273
  737.5 182.8 %all-to-all-start = ((bf16[8,528,256]{2,1,0:T(8,128)(2,1)}), bf16[8,528,256]{2,1,0:T(8,128)(2,1)}, u32[]{:S(2)}, u32[]{:S(2)}) async-start(bf16[8,528,256]{2,1,0:T(8,128)(2,1)} %get-tuple-element.84), calls=%async_computation | async-start | bytes 4325376 | tf_op jit(solution)/shard_map/all_to_all | solution.py:2259
  775.3 3.4 copy-start.4
  782.1 11.0 %copy-start.56 = (bf16[2048,512]{1,0:T(8,128)(2,1)S(1)}, bf16[2048,512]{1,0:T(8,128)(2,1)}, u32[]{:S(2)}) copy-start(bf16[2048,512]{1,0:T(8,128)(2,1)} %get-tuple-element.70) | copy-start | bytes 6291460
  793.0 7.0 copy-start.2
  793.0 7.0 copy-start.8
  793.1 7.0 copy-start.9
  933.1 4.5 copy-start.1
  (29 other events, 61.4 us)
Sparse Core Ops, SparseCore 0:
  615.8 75.2 all-gather.4
  693.3 20.8 all-gather.2
